TPU v7x, 32 devices: a whole 2x2x4 slice. The times are simulated.
32 devices in a mesh: fsdp: 2 (over x), cp: 16 (over z, y, core).
Axes of the slice: x: 2, y: 2, z: 4, core: 2. Of those that a mesh axis runs over, the one named last changes fastest.
Arguments:
- tokens: bfloat16 [4, 1024, 2048], P('fsdp', 'cp'), may hold values from -6 to 6
- cotangent: bfloat16 [4, 1024, 2048], P('fsdp', 'cp'), may hold values from -6 to 6
- attn_gain: bfloat16 [2048], P(('fsdp', 'cp')), may hold values from 0.5 to 1.5
- q_weight: bfloat16 [2048, 2048], P(('fsdp', 'cp')), may hold values from -0.125 to 0.125
- k_weight: bfloat16 [2048, 512], P(('fsdp', 'cp')), may hold values from -0.125 to 0.125
- v_weight: bfloat16 [2048, 512], P(('fsdp', 'cp')), may hold values from -0.125 to 0.125
- o_weight: bfloat16 [2048, 2048], P(('fsdp', 'cp')), may hold values from -2 to 2
- ffn_gain: bfloat16 [2048], P(('fsdp', 'cp')), may hold values from 0.5 to 1.5
- gate_weight: bfloat16 [2048, 8192], P(('fsdp', 'cp')), may hold values from -0.125 to 0.125
- up_weight: bfloat16 [2048, 8192], P(('fsdp', 'cp')), may hold values from -0.125 to 0.125
- down_weight: bfloat16 [2048, 8192], P(('fsdp', 'cp')), may hold values from -0.0625 to 0.0625
Outputs:
- block_out: bfloat16 [4, 1024, 2048], P('fsdp', 'cp')
- input_grad: bfloat16 [4, 1024, 2048], P('fsdp', 'cp')
- attn_gain_grad: float32 [2048], P(('fsdp', 'cp'))
- q_weight_grad: float32 [2048, 2048], P(('fsdp', 'cp'))
- k_weight_grad: float32 [2048, 512], P(('fsdp', 'cp'))
- v_weight_grad: float32 [2048, 512], P(('fsdp', 'cp'))
- o_weight_grad: float32 [2048, 2048], P(('fsdp', 'cp'))
- ffn_gain_grad: float32 [2048], P(('fsdp', 'cp'))
- gate_weight_grad: float32 [2048, 8192], P(('fsdp', 'cp'))
- up_weight_grad: float32 [2048, 8192], P(('fsdp', 'cp'))
- down_weight_grad: float32 [2048, 8192], P(('fsdp', 'cp'))
All inputs are finite; a program needn't handle non-finite values.
Results may differ from a plain program's by a relative error of at most 0.014.
Values may be sent and summed in bfloat16 or wider, within the bound.
A program may use at most 960 MiB of HBM per device.

v0:
```python
import jax
import jax.numpy as jnp
from jax import lax
from jax.sharding import PartitionSpec as P

HEADS = 32
KV_HEADS = 8
HEAD_DIM = 64


NORM_EPS = 1e-05
ROPE_BASE = 500000.0


def dealt_positions(row_ids, block_len, cp_size):
    owner = row_ids // (2 * block_len)
    within = row_ids % (2 * block_len)
    return jnp.where(
        within < block_len,
        owner * block_len + within,
        (2 * cp_size - 1 - owner) * block_len + within - block_len,
    )


def rotary_tables(positions, head_width):
    half_width = head_width // 2
    freq_index = jnp.arange(half_width, dtype=jnp.float32)
    inverse = ROPE_BASE ** (-(2.0 * freq_index) / head_width)
    angle = positions.astype(jnp.float32)[:, None] * inverse[None, :]
    return (jnp.cos(angle), jnp.sin(angle))


def rotate(vector, cosine, sine):
    half_width = vector.shape[-1] // 2
    first = vector[..., :half_width]
    second = vector[..., half_width:]
    cos_wide = cosine[:, None, :]
    sin_wide = sine[:, None, :]
    return jnp.concatenate(
        [first * cos_wide - second * sin_wide, second * cos_wide + first * sin_wide], axis=-1
    )


def unrotate(vector, cosine, sine):
    half_width = vector.shape[-1] // 2
    first = vector[..., :half_width]
    second = vector[..., half_width:]
    cos_wide = cosine[:, None, :]
    sin_wide = sine[:, None, :]
    return jnp.concatenate(
        [first * cos_wide + second * sin_wide, second * cos_wide - first * sin_wide], axis=-1
    )


def contract_rows(left, right):
    return lax.dot_general(
        left, right, (((0,), (0,)), ((), ())), preferred_element_type=jnp.float32
    )


def contract_cols(left, right):
    return lax.dot_general(
        left, right, (((1,), (1,)), ((), ())), preferred_element_type=jnp.float32
    )


def body(
    tokens,
    cotangent,
    attn_gain,
    q_weight,
    k_weight,
    v_weight,
    o_weight,
    ffn_gain,
    gate_weight,
    up_weight,
    down_weight,
):
    gathered = (
        lax.all_gather(attn_gain, ("fsdp", "cp"), axis=0, tiled=True),
        lax.all_gather(q_weight, ("fsdp", "cp"), axis=0, tiled=True),
        lax.all_gather(k_weight, ("fsdp", "cp"), axis=0, tiled=True),
        lax.all_gather(v_weight, ("fsdp", "cp"), axis=0, tiled=True),
        lax.all_gather(o_weight, ("fsdp", "cp"), axis=0, tiled=True),
        lax.all_gather(ffn_gain, ("fsdp", "cp"), axis=0, tiled=True),
        lax.all_gather(gate_weight, ("fsdp", "cp"), axis=0, tiled=True),
        lax.all_gather(up_weight, ("fsdp", "cp"), axis=0, tiled=True),
        lax.all_gather(down_weight, ("fsdp", "cp"), axis=0, tiled=True),
    )
    gain_one, q_full, k_full, v_full, o_full, gain_two, gate_full, up_full, down_full = gathered
    seq_count, row_count, width = tokens.shape
    block_len = row_count // 2
    cp_size = lax.axis_size("cp")
    seq_len = row_count * cp_size
    token_count = seq_count * row_count
    group_size = HEADS // KV_HEADS
    kv_width = KV_HEADS * HEAD_DIM
    score_scale = HEAD_DIM ** (-0.5)
    key_block = row_count * min(cp_size, 8)
    block_count = seq_len // key_block
    own_rows = lax.axis_index("cp") * row_count + jnp.arange(row_count, dtype=jnp.int32)
    query_pos = dealt_positions(own_rows, block_len, cp_size)
    key_pos = dealt_positions(jnp.arange(seq_len, dtype=jnp.int32), block_len, cp_size)
    cosine, sine = rotary_tables(query_pos, HEAD_DIM)
    x_float = tokens.astype(jnp.float32)
    inv_one = lax.rsqrt(jnp.mean(x_float * x_float, axis=-1, keepdims=True) + NORM_EPS)
    normed_one = (x_float * inv_one).reshape(token_count, width)
    inv_one_flat = inv_one.reshape(token_count, 1)
    attn_in = (normed_one * gain_one.astype(jnp.float32)).astype(jnp.bfloat16)
    q_proj = jnp.dot(attn_in, q_full, preferred_element_type=jnp.float32)
    k_proj = jnp.dot(attn_in, k_full, preferred_element_type=jnp.float32)
    v_proj = jnp.dot(attn_in, v_full, preferred_element_type=jnp.float32)
    q_rot = rotate(q_proj.reshape(seq_count, row_count, HEADS, HEAD_DIM), cosine, sine).astype(
        jnp.bfloat16
    )
    q_heads = q_rot.reshape(seq_count, row_count, KV_HEADS, group_size, HEAD_DIM)
    k_rot = (
        rotate(k_proj.reshape(seq_count, row_count, KV_HEADS, HEAD_DIM), cosine, sine)
        .astype(jnp.bfloat16)
        .reshape(seq_count, row_count, kv_width)
    )
    v_low = v_proj.astype(jnp.bfloat16).reshape(seq_count, row_count, kv_width)
    key_all, value_all = (
        lax.all_gather(k_rot, "cp", axis=1, tiled=True),
        lax.all_gather(v_low, "cp", axis=1, tiled=True),
    )

    def key_slice(source, index):
        piece = lax.dynamic_slice_in_dim(source, index * key_block, key_block, 1)
        return piece.reshape(seq_count, key_block, KV_HEADS, HEAD_DIM)

    def block_scores(index):
        keys = key_slice(key_all, index)
        places = lax.dynamic_slice_in_dim(key_pos, index * key_block, key_block, 0)
        raw = (
            jnp.einsum("srkgd,stkd->skgrt", q_heads, keys, preferred_element_type=jnp.float32)
            * score_scale
        )
        return jnp.where(query_pos[:, None] >= places[None, :], raw, -1e30)

    def stats_step(carry, index):
        peak, total = carry
        scores = block_scores(index)
        new_peak = jnp.maximum(peak, jnp.max(scores, axis=-1))
        total = total * jnp.exp(peak - new_peak) + jnp.sum(
            jnp.exp(scores - new_peak[..., None]), axis=-1
        )
        return ((new_peak, total), None)

    stat_shape = (seq_count, KV_HEADS, group_size, row_count)
    block_ids = jnp.arange(block_count, dtype=jnp.int32)
    (peak, total), _ = lax.scan(
        stats_step,
        (jnp.full(stat_shape, -1e30, jnp.float32), jnp.zeros(stat_shape, jnp.float32)),
        block_ids,
    )

    def block_probs(index):
        return jnp.exp(block_scores(index) - peak[..., None]) / total[..., None]

    def mix_step(accum, index):
        probs = block_probs(index).astype(jnp.bfloat16)
        values = key_slice(value_all, index)
        return (
            accum
            + jnp.einsum("skgrt,stkd->srkgd", probs, values, preferred_element_type=jnp.float32),
            None,
        )

    head_shape = (seq_count, row_count, KV_HEADS, group_size, HEAD_DIM)
    mixed, _ = lax.scan(mix_step, jnp.zeros(head_shape, jnp.float32), block_ids)
    attn_mix = mixed.reshape(token_count, width).astype(jnp.bfloat16)
    resid = x_float.reshape(token_count, width) + jnp.dot(
        attn_mix, o_full, preferred_element_type=jnp.float32
    )
    inv_two = lax.rsqrt(jnp.mean(resid * resid, axis=-1, keepdims=True) + NORM_EPS)
    normed_two = resid * inv_two
    ffn_in = (normed_two * gain_two.astype(jnp.float32)).astype(jnp.bfloat16)
    gate = jnp.dot(ffn_in, gate_full, preferred_element_type=jnp.float32)
    up_val = jnp.dot(ffn_in, up_full, preferred_element_type=jnp.float32)
    sigma = jax.nn.sigmoid(gate)
    silu_val = gate * sigma
    hidden = (silu_val * up_val).astype(jnp.bfloat16)
    block_out = (
        (resid + contract_cols(hidden, down_full))
        .astype(jnp.bfloat16)
        .reshape(seq_count, row_count, width)
    )
    regathered = (
        lax.all_gather(attn_gain, ("fsdp", "cp"), axis=0, tiled=True),
        lax.all_gather(q_weight, ("fsdp", "cp"), axis=0, tiled=True),
        lax.all_gather(k_weight, ("fsdp", "cp"), axis=0, tiled=True),
        lax.all_gather(v_weight, ("fsdp", "cp"), axis=0, tiled=True),
        lax.all_gather(o_weight, ("fsdp", "cp"), axis=0, tiled=True),
        lax.all_gather(ffn_gain, ("fsdp", "cp"), axis=0, tiled=True),
        lax.all_gather(gate_weight, ("fsdp", "cp"), axis=0, tiled=True),
        lax.all_gather(up_weight, ("fsdp", "cp"), axis=0, tiled=True),
        lax.all_gather(down_weight, ("fsdp", "cp"), axis=0, tiled=True),
    )
    gain_one, q_full, k_full, v_full, o_full, gain_two, gate_full, up_full, down_full = regathered
    dy_low = cotangent.reshape(token_count, width)
    hidden_grad = jnp.dot(dy_low, down_full, preferred_element_type=jnp.float32)
    gate_grad = (hidden_grad * up_val * (sigma + gate * sigma * (1.0 - sigma))).astype(jnp.bfloat16)
    up_grad = (hidden_grad * silu_val).astype(jnp.bfloat16)
    ffn_in_grad = contract_cols(gate_grad, gate_full) + contract_cols(up_grad, up_full)
    ffn_gain_part = jnp.sum(ffn_in_grad * normed_two, axis=0)
    scaled_two = ffn_in_grad * gain_two.astype(jnp.float32)
    resid_grad = dy_low.astype(jnp.float32) + inv_two * (
        scaled_two - normed_two * jnp.mean(scaled_two * normed_two, axis=-1, keepdims=True)
    )
    branch_grad = resid_grad.astype(jnp.bfloat16)
    o_term = contract_rows(attn_mix, branch_grad)
    mix_grad = contract_cols(branch_grad, o_full).astype(jnp.bfloat16).reshape(head_shape)

    def delta_step(delta, index):
        probs = block_probs(index)
        values = key_slice(value_all, index)
        dprob = jnp.einsum(
            "srkgd,stkd->skgrt", mix_grad, values, preferred_element_type=jnp.float32
        )
        return (delta + jnp.sum(probs * dprob, axis=-1), None)

    delta, _ = lax.scan(delta_step, jnp.zeros(stat_shape, jnp.float32), block_ids)

    def grad_step(carry, index):
        q_accum, key_buffer, value_buffer = carry
        probs = block_probs(index)
        keys = key_slice(key_all, index)
        values = key_slice(value_all, index)
        dprob = jnp.einsum(
            "srkgd,stkd->skgrt", mix_grad, values, preferred_element_type=jnp.float32
        )
        score_grad = (probs * (dprob - delta[..., None])).astype(jnp.bfloat16)
        q_accum = q_accum + jnp.einsum(
            "skgrt,stkd->srkgd", score_grad, keys, preferred_element_type=jnp.float32
        )
        key_part = (
            jnp.einsum("skgrt,srkgd->stkd", score_grad, q_heads, preferred_element_type=jnp.float32)
            * score_scale
        )
        value_part = jnp.einsum(
            "skgrt,srkgd->stkd",
            probs.astype(jnp.bfloat16),
            mix_grad,
            preferred_element_type=jnp.float32,
        )
        key_buffer = lax.dynamic_update_slice_in_dim(
            key_buffer, key_part.reshape(seq_count, key_block, kv_width), index * key_block, 1
        )
        value_buffer = lax.dynamic_update_slice_in_dim(
            value_buffer, value_part.reshape(seq_count, key_block, kv_width), index * key_block, 1
        )
        return ((q_accum, key_buffer, value_buffer), None)

    kv_shape = (seq_count, seq_len, kv_width)
    (q_accum, key_buffer, value_buffer), _ = lax.scan(
        grad_step,
        (
            jnp.zeros(head_shape, jnp.float32),
            jnp.zeros(kv_shape, jnp.float32),
            jnp.zeros(kv_shape, jnp.float32),
        ),
        block_ids,
    )
    key_sum, value_sum = (
        lax.psum_scatter(key_buffer, "cp", scatter_dimension=1, tiled=True),
        lax.psum_scatter(value_buffer, "cp", scatter_dimension=1, tiled=True),
    )
    q_grad = (
        unrotate(
            (q_accum * score_scale).reshape(seq_count, row_count, HEADS, HEAD_DIM), cosine, sine
        )
        .astype(jnp.bfloat16)
        .reshape(token_count, width)
    )
    k_grad = (
        unrotate(key_sum.reshape(seq_count, row_count, KV_HEADS, HEAD_DIM), cosine, sine)
        .astype(jnp.bfloat16)
        .reshape(token_count, kv_width)
    )
    v_grad = value_sum.astype(jnp.bfloat16).reshape(token_count, kv_width)
    attn_in_grad = (
        contract_cols(q_grad, q_full)
        + contract_cols(k_grad, k_full)
        + contract_cols(v_grad, v_full)
    )
    attn_gain_part = jnp.sum(attn_in_grad * normed_one, axis=0)
    scaled_one = attn_in_grad * gain_one.astype(jnp.float32)
    input_grad = resid_grad + inv_one_flat * (
        scaled_one - normed_one * jnp.mean(scaled_one * normed_one, axis=-1, keepdims=True)
    )
    input_grad = input_grad.astype(jnp.bfloat16).reshape(seq_count, row_count, width)
    q_term = contract_rows(attn_in, q_grad)
    k_term = contract_rows(attn_in, k_grad)
    v_term = contract_rows(attn_in, v_grad)
    summed = (
        lax.psum_scatter(attn_gain_part, ("fsdp", "cp"), scatter_dimension=0, tiled=True),
        lax.psum_scatter(q_term, ("fsdp", "cp"), scatter_dimension=0, tiled=True),
        lax.psum_scatter(k_term, ("fsdp", "cp"), scatter_dimension=0, tiled=True),
        lax.psum_scatter(v_term, ("fsdp", "cp"), scatter_dimension=0, tiled=True),
        lax.psum_scatter(o_term, ("fsdp", "cp"), scatter_dimension=0, tiled=True),
        lax.psum_scatter(ffn_gain_part, ("fsdp", "cp"), scatter_dimension=0, tiled=True),
    )
    ffn_sums = lax.psum_scatter(
        jnp.concatenate(
            [
                contract_rows(ffn_in, gate_grad),
                contract_rows(ffn_in, up_grad),
                contract_rows(dy_low, hidden),
            ],
            axis=1,
        ),
        ("fsdp", "cp"),
        scatter_dimension=0,
        tiled=True,
    )
    ff_width = gate.shape[1]
    return (
        block_out,
        input_grad,
        summed[0],
        summed[1],
        summed[2],
        summed[3],
        summed[4],
        summed[5],
        ffn_sums[:, :ff_width],
        ffn_sums[:, ff_width : 2 * ff_width],
        ffn_sums[:, 2 * ff_width :],
    )


def solution(mesh):
    placed = (
        P("fsdp", "cp", None),
        P("fsdp", "cp", None),
        P(("fsdp", "cp")),
        P(("fsdp", "cp"), None),
        P(("fsdp", "cp"), None),
        P(("fsdp", "cp"), None),
        P(("fsdp", "cp"), None),
        P(("fsdp", "cp")),
        P(("fsdp", "cp"), None),
        P(("fsdp", "cp"), None),
        P(("fsdp", "cp"), None),
    )
    return jax.shard_map(
        body,
        mesh=mesh,
        in_specs=placed,
        out_specs=(
            P("fsdp", "cp", None),
            P("fsdp", "cp", None),
            P(("fsdp", "cp")),
            P(("fsdp", "cp"), None),
            P(("fsdp", "cp"), None),
            P(("fsdp", "cp"), None),
            P(("fsdp", "cp"), None),
            P(("fsdp", "cp")),
            P(("fsdp", "cp"), None),
            P(("fsdp", "cp"), None),
            P(("fsdp", "cp"), None),
        ),
        check_vma=False,
    )
```

profile of v0, /device:TPU:0, one launch (start us, length us, event | category | flops | bytes accessed | tf_op | source)
XLA Modules:
  0.0 3588.5 jit_solution(12352071852157480683)
XLA Ops:
  10.4 42.1 %all-reduce.6 = (bf16[2048]{0:T(1024)(128)(2,1)S(1)}, bf16[2048]{0:T(1024)(128)(2,1)S(1)}) all-reduce(bf16[2048]{0:T(1024)(128)(2,1)S(1)} %dynamic-update-slice, bf16[2048]{0:T(1024)(128)(2,1)S(1)} %dynamic-update-slice.1), channel_id=1, replica_groups=mesh['fsdp'=2,'cp'=16] {'fsdp','cp'}, use_global_device_ids=true, to_apply=%add | all-reduce | flops 4096 | bytes 16384
  56.1 13.9 all-gather.10.cloned.1.call-done
  73.2 55.1 %all-gather.14.cloned.1.call-done = bf16[2048,512]{1,0:T(8,128)(2,1)} async-done(((bf16[64,512]{1,0:T(8,128)(2,1)}), bf16[2048,512]{1,0:T(8,128)(2,1)}) %all-gather.14.cloned.1.call-update) | async-done | bytes 2097168 | tf_op jit(solution)/shard_map/all_gather | solution.py:83
  136.6 34.7 all-gather.12.cloned.1.call-done
  177.4 36.6 %all-gather.16.cloned.1.call-done = bf16[2,1024,512]{2,0,1:T(2,128)(2,1)} async-done(((bf16[2,64,512]{2,0,1:T(2,128)(2,1)}), bf16[2,1024,512]{2,0,1:T(2,128)(2,1)}) %all-gather.16.cloned.1.call-update) | async-done | bytes 2097168 | tf_op jit(solution)/shard_map/all_gather | solution.py:125
  218.8 74.4 %all-gather.18.cloned.1.call-done = bf16[2048,2048]{1,0:T(8,128)(2,1)} async-done(((bf16[64,2048]{1,0:T(8,128)(2,1)}), bf16[2048,2048]{1,0:T(8,128)(2,1)}) %all-gather.18.cloned.1.call-update) | async-done | bytes 8388624 | tf_op jit(solution)/shard_map/all_gather | solution.py:82
  293.2 12.4 copy.55
  324.1 21.5 while.51
  354.8 17.3 all-gather.20.cloned.1.call-done
  379.0 189.4 %all-gather.24.cloned.1.call-done = bf16[2048,8192]{1,0:T(8,128)(2,1)} async-done(((bf16[64,8192]{1,0:T(8,128)(2,1)}), bf16[2048,8192]{1,0:T(8,128)(2,1)}) %all-gather.24.cloned.1.call-update) | async-done | bytes 33554448 | tf_op jit(solution)/shard_map/all_gather | solution.py:88
  568.4 17.9 fusion.68
  586.4 177.9 %all-gather.22.cloned.1.call-done = bf16[2048,8192]{1,0:T(8,128)(2,1)} async-done(((bf16[64,8192]{1,0:T(8,128)(2,1)}), bf16[2048,8192]{1,0:T(8,128)(2,1)}) %all-gather.22.cloned.1.call-update) | async-done | bytes 33554448 | tf_op jit(solution)/shard_map/all_gather | solution.py:87
  764.3 18.1 fusion.67
  782.4 177.8 %all-gather.26.cloned.1.call-done = bf16[2048,8192]{1,0:T(8,128)(2,1)} async-done(((bf16[64,8192]{1,0:T(8,128)(2,1)}), bf16[2048,8192]{1,0:T(8,128)(2,1)}) %all-gather.26.cloned.1.call-update) | async-done | bytes 33554448 | tf_op jit(solution)/shard_map/all_gather | solution.py:89
  960.2 19.6 multiply_convert_fusion
  979.8 17.3 fusion.69
  997.2 18.5 multiply_reduce_fusion
  1034.2 25.7 fusion.74
  1059.9 15.4 while.52
  1081.0 64.0 %while.53 = (s32[]{:T(128)}, f32[2,64,8,4,64]{1,4,3,2,0:T(8,128)}, f32[2,1024,512]{2,0,1:T(2,128)}, f32[2,1024,512]{2,1,0:T(8,128)}, s32[2]{0:T(128)S(1)}, /*ind...) while((s32[]{:T(128)}, f32[2,64,8,4,64]{1,4,3,2,0:T(8,128)}, ...), condition=%wide.region_13.14_spmd.clone, body=%wide.region_12.13_spmd.clone.sunk | while | flops 1360037632 | bytes 103930760 | solution.py:257
  1146.7 24.0 convolution_bitcast_fusion
  1170.7 23.7 fusion.73
  1194.5 134.9 %pad_maximum_fusion = f32[2048,24576]{1,0:T(8,128)} fusion(f32[2048,8192]{1,0:T(8,128)} %convolution_bitcast_fusion, f32[2048,8192]{1,0:T(8,128)} %fusion.74, f32[2048,8192]{1,0:T(8,128)} %fusion.73), kind=kLoop, calls=%fused_computation.75 | loop fusion | flops 100663296 | bytes 402653184 | tf_op jit(solution)/shard_map/concatenate | solution.py:306
  1339.8 11.6 fusion.46
  1358.7 12.0 fusion.71
  1379.6 22.5 fusion.34
  1406.8 38.4 %all-reduce.5 = (f32[2048]{0:T(1024)S(1)}, f32[2048]{0:T(1024)S(1)}) all-reduce(f32[2048]{0:T(1024)S(1)} %get-tuple-element.528, f32[2048]{0:T(1024)S(1)} %copy-done.33), channel_id=4, replica_groups=mesh['fsdp'=2,'cp'=16] {'fsdp','cp'}, use_global_device_ids=true, to_apply=%region_18.19.clone | all-reduce | flops 4096 | bytes 32768
  1447.5 1479.8 %reduce-scatter.17.cloned.1.call-done = f32[64,24576]{1,0:T(8,128)} async-done(((f32[2048,24576]{1,0:T(8,128)}), f32[64,24576]{1,0:T(8,128)}) %reduce-scatter.17.cloned.1.call-update) | async-done | bytes 6291472 | tf_op jit(solution)/shard_map/reduce_scatter | solution.py:305
  2933.0 138.1 %reduce-scatter.11.cloned.1.call-done = f32[64,512]{1,0:T(8,128)} async-done(((f32[2048,512]{1,0:T(8,128)}), f32[64,512]{1,0:T(8,128)}) %reduce-scatter.11.cloned.1.call-update) | async-done | bytes 131088 | tf_op jit(solution)/shard_map/reduce_scatter | solution.py:300
  3071.1 140.4 %reduce-scatter.13.cloned.1.call-done = f32[64,512]{1,0:T(8,128)} async-done(((f32[2048,512]{1,0:T(8,128)}), f32[64,512]{1,0:T(8,128)}) %reduce-scatter.13.cloned.1.call-update) | async-done | bytes 131088 | tf_op jit(solution)/shard_map/reduce_scatter | solution.py:301
  3211.6 182.4 %reduce-scatter.15.cloned.1.call-done = f32[64,2048]{1,0:T(8,128)} async-done(((f32[2048,2048]{1,0:T(8,128)}), f32[64,2048]{1,0:T(8,128)}) %reduce-scatter.15.cloned.1.call-update) | async-done | bytes 524304 | tf_op jit(solution)/shard_map/reduce_scatter | solution.py:302
  3393.9 187.6 %reduce-scatter.9.cloned.1.call-done = f32[64,2048]{1,0:T(8,128)} async-done(((f32[2048,2048]{1,0:T(8,128)}), f32[64,2048]{1,0:T(8,128)}) %reduce-scatter.9.cloned.1.call-update) | async-done | bytes 524304 | tf_op jit(solution)/shard_map/reduce_scatter | solution.py:299
  (271 shorter events, 233.1 us)
Async XLA Ops:
  7.2 62.9 %all-gather.10.cloned.1.call-start = ((), (), s32[]{:S(2)}) async-start(), calls=%async_computation.6 | async-start | bytes 2162688 | tf_op jit(solution)/shard_map/all_gather | solution.py:84
  7.9 120.3 %all-gather.14.cloned.1.call-start = ((), (), s32[]{:S(2)}) async-start(), calls=%async_computation.8 | async-start | bytes 2162688 | tf_op jit(solution)/shard_map/all_gather | solution.py:83
  8.7 162.6 %all-gather.12.cloned.1.call-start = ((), (), s32[]{:S(2)}) async-start(), calls=%async_computation.7 | async-start | bytes 2228224 | tf_op jit(solution)/shard_map/all_gather | solution.py:126
  55.0 250.5 %copy-start.18 = (bf16[2,64,2048]{2,1,0:T(8,128)(2,1)}, bf16[2,64,2048]{2,1,0:T(8,128)(2,1)S(1)}, u32[]{:S(2)}) copy-start(bf16[2,64,2048]{2,1,0:T(8,128)(2,1)S(1)} %get-tuple-element.642) | copy-start | bytes 1572868
  72.9 141.1 %all-gather.16.cloned.1.call-start = ((), (), s32[]{:S(2)}) async-start(), calls=%async_computation.9 | async-start | bytes 2228224 | tf_op jit(solution)/shard_map/all_gather | solution.py:125
  73.2 237.3 %copy-start.27 = (f32[64,32]{0,1:T(8,128)}, f32[64,32]{0,1:T(8,128)S(1)}, u32[]{:S(2)}) copy-start(f32[64,32]{0,1:T(8,128)S(1)} %get-tuple-element.644) | copy-start | bytes 24580
  73.2 237.3 %copy-start.29 = (f32[64,32]{0,1:T(8,128)}, f32[64,32]{0,1:T(8,128)S(1)}, u32[]{:S(2)}) copy-start(f32[64,32]{0,1:T(8,128)S(1)} %get-tuple-element.645) | copy-start | bytes 24580
  132.9 160.3 %all-gather.18.cloned.1.call-start = ((), (), s32[]{:S(2)}) async-start(), calls=%async_computation.10 | async-start | bytes 8650752 | tf_op jit(solution)/shard_map/all_gather | solution.py:82
  133.5 238.6 %all-gather.20.cloned.1.call-start = ((), (), s32[]{:S(2)}) async-start(), calls=%async_computation.11 | async-start | bytes 8650752 | tf_op jit(solution)/shard_map/all_gather | solution.py:85
  134.1 434.4 %all-gather.24.cloned.1.call-start = ((), (), s32[]{:S(2)}) async-start(), calls=%async_computation.13 | async-start | bytes 34603008 | tf_op jit(solution)/shard_map/all_gather | solution.py:88
  134.8 629.5 %all-gather.22.cloned.1.call-start = ((), (), s32[]{:S(2)}) async-start(), calls=%async_computation.12 | async-start | bytes 34603008 | tf_op jit(solution)/shard_map/all_gather | solution.py:87
  135.6 824.6 %all-gather.26.cloned.1.call-start = ((), (), s32[]{:S(2)}) async-start(), calls=%async_computation.14 | async-start | bytes 34603008 | tf_op jit(solution)/shard_map/all_gather | solution.py:89
  136.3 1195.0 %all-reduce.9.cloned.1.call-start = ((), (), s32[]{:S(2)}) async-start(), calls=%async_computation.21 | async-start | bytes 8388608
  979.8 17.4 copy-start.8
  997.2 18.5 copy-start.24
  1034.2 25.7 copy-start.23
  1075.3 5.7 copy-start.2
  1095.0 6.1 copy-start
  1095.0 6.1 copy-start.6
  1126.6 6.8 copy-start
  1126.6 6.8 copy-start.6
  1145.0 190.9 %reduce-scatter.7.cloned.1.call-start = ((), (), s32[]{:S(2)}) async-start(), calls=%async_computation.15 | async-start | bytes 4456448 | tf_op jit(solution)/shard_map/reduce_scatter | solution.py:268
  1146.7 24.0 copy-start.14
  1146.7 24.0 copy-start.17
  1194.4 1732.9 %reduce-scatter.17.cloned.1.call-start = ((), (), s32[]{:S(2)}) async-start(), calls=%async_computation.20 | async-start | bytes 207618048 | tf_op jit(solution)/shard_map/reduce_scatter | solution.py:305
  1329.5 1741.7 %reduce-scatter.11.cloned.1.call-start = ((), (), s32[]{:S(2)}) async-start(), calls=%async_computation.17 | async-start | bytes 4325376 | tf_op jit(solution)/shard_map/reduce_scatter | solution.py:300
  1335.9 1875.7 %reduce-scatter.13.cloned.1.call-start = ((), (), s32[]{:S(2)}) async-start(), calls=%async_computation.18 | async-start | bytes 4325376 | tf_op jit(solution)/shard_map/reduce_scatter | solution.py:301
  1339.8 2054.2 %reduce-scatter.15.cloned.1.call-start = ((), (), s32[]{:S(2)}) async-start(), calls=%async_computation.19 | async-start | bytes 17301504 | tf_op jit(solution)/shard_map/reduce_scatter | solution.py:302
  1351.4 2230.0 %reduce-scatter.9.cloned.1.call-start = ((), (), s32[]{:S(2)}) async-start(), calls=%async_computation.16 | async-start | bytes 17301504 | tf_op jit(solution)/shard_map/reduce_scatter | solution.py:299
  1353.7 5.0 copy-start.20
  1371.4 8.2 copy-start.9
  1371.4 8.2 copy-start.16
  (27 other events, 65.6 us)
Sparse Core Ops, SparseCore 0:
  10.9 59.1 all-gather.9
  72.9 55.2 all-gather.13
  131.0 40.2 all-gather.11
  173.9 40.1 all-gather.15
  216.8 76.3 all-gather.17
  295.9 76.1 all-gather.19
  375.0 193.4 all-gather.23
  571.3 192.9 all-gather.21
  767.2 192.9 all-gather.25
  1145.1 109.5 all-reduce.8
  1259.1 71.2 reduce-scatter.6
  1336.7 1590.5 reduce-scatter.16
  2930.2 140.9 reduce-scatter.10
  3073.8 137.6 reduce-scatter.12
  3214.3 179.6 reduce-scatter.14
  3396.7 184.7 reduce-scatter.8
where the time goes:
time: 3590 us
  waiting for transfers between devices  2910 us (81%)
  matrix products  307 us (9%)
  other arithmetic  153 us (4%)
  local copies, waits for them, and re-layouts  116 us (3%)
  blocking collectives  80.5 us (2%)
    reduce_scatter x1, waiting for transfers between devices, body(): lax.psum_scatter(jnp.concatenate([contract_rows(ffn_in, gate_grad), contr...  1480 us
    all_gather x1, waiting for transfers between devices, body(): lax.all_gather(up_weight, ('fsdp', 'cp'), axis=0, tiled=True)  189 us
    reduce_scatter x1, waiting for transfers between devices, body(): lax.psum_scatter(q_term, ('fsdp', 'cp'), scatter_dimension=0, tiled=True)  188 us
    reduce_scatter x1, waiting for transfers between devices, body(): lax.psum_scatter(o_term, ('fsdp', 'cp'), scatter_dimension=0, tiled=True)  182 us
    all_gather x1, waiting for transfers between devices, body(): lax.all_gather(gate_weight, ('fsdp', 'cp'), axis=0, tiled=True)  178 us
    all_gather x1, waiting for transfers between devices, body(): lax.all_gather(down_weight, ('fsdp', 'cp'), axis=0, tiled=True)  178 us
    reduce_scatter x1, waiting for transfers between devices, body(): lax.psum_scatter(v_term, ('fsdp', 'cp'), scatter_dimension=0, tiled=True)  140 us
    reduce_scatter x1, waiting for transfers between devices, body(): lax.psum_scatter(k_term, ('fsdp', 'cp'), scatter_dimension=0, tiled=True)  138 us
  transfers between devices with their start and end apart: 16, of which 14 were waited for; matrix products, arithmetic and copies ran while one was open for 11% of the time, Pallas kernels for 0%

commit v1 on v0

v1 whole, which is shorter than its diff:
```python
import functools

import jax
import jax.numpy as jnp
from jax import lax
from jax.experimental import pallas as pl
from jax.experimental.pallas import tpu as pltpu
from jax.sharding import PartitionSpec as P

HEADS = 32
KV_HEADS = 8
HEAD_DIM = 64
HALF = HEAD_DIM // 2
NORM_EPS = 1e-05
ROPE_BASE = 500000.0
BOTH = ("fsdp", "cp")
F32 = jnp.float32
BF16 = jnp.bfloat16


def dot(left, right):
    return jnp.dot(left, right, preferred_element_type=F32)


def contract_rows(left, right):
    return lax.dot_general(left, right, (((0,), (0,)), ((), ())), preferred_element_type=F32)


def contract_cols(left, right):
    return lax.dot_general(left, right, (((1,), (1,)), ((), ())), preferred_element_type=F32)


def swap_halves(wide):
    pieces = []
    for start in range(0, wide.shape[-1], HEAD_DIM):
        pieces.append(wide[:, start + HALF : start + HEAD_DIM])
        pieces.append(wide[:, start : start + HALF])
    return jnp.concatenate(pieces, axis=-1)


def diagonal_mask(rows_of, cols_of, team, block_len, later):
    def place(index):
        owner, within = index // block_len, index % block_len
        return (team - 1 - owner) * block_len + within if later else index

    return place(rows_of) >= place(cols_of)


QUARTER_OF = (0, 3, 1, 2)


def attention_forward(team, block_len, q_width, t_ref, proj_ref, cos_ref, sin_ref, mix_ref, rot_ref, wide_ref):
    t = t_ref[0]
    quarter = team * block_len
    heads = q_width // HEAD_DIM

    def place_chunk(owner, carry):
        diff = owner ^ t
        spot = diff // 2 + (diff % 2) * (team // 2)
        rows = pl.ds(pl.multiple_of(owner * block_len, block_len), block_len)
        for slot in range(4):
            wide_ref[QUARTER_OF[slot], rows, :] = proj_ref[spot, slot * block_len : (slot + 1) * block_len, :]
        return carry

    lax.fori_loop(0, team, place_chunk, 0)
    for part in range(4):
        wide = wide_ref[part]
        cosine, sine = cos_ref[part], sin_ref[part]
        qk = wide[:, : q_width + HEAD_DIM]
        turned = qk * cosine + swap_halves(qk) * sine
        rot_ref[part] = jnp.concatenate([turned, wide[:, q_width + HEAD_DIM :]], axis=-1).astype(BF16)

    for part in range(4):
        span = (part + 1) * quarter
        keys = rot_ref[: part + 1, :, q_width : q_width + HEAD_DIM].reshape(span, HEAD_DIM)
        values = rot_ref[: part + 1, :, q_width + HEAD_DIM :].reshape(span, HEAD_DIM)
        row = lax.broadcasted_iota(jnp.int32, (quarter, quarter), 0)
        col = lax.broadcasted_iota(jnp.int32, (quarter, quarter), 1)
        allowed = diagonal_mask(row, col, team, block_len, part >= 2)
        outs = []
        for head in range(heads):
            query = rot_ref[part, :, head * HEAD_DIM : (head + 1) * HEAD_DIM]
            scores = contract_cols(query, keys)
            last = jnp.where(allowed, scores[:, part * quarter :], -1e30)
            scores = jnp.concatenate([scores[:, : part * quarter], last], axis=-1) if part else last
            peak = jnp.max(scores, axis=-1, keepdims=True)
            expo = jnp.exp(scores - peak)
            total = jnp.sum(expo, axis=-1, keepdims=True)
            outs.append(dot(expo.astype(BF16), values) / total)
        mixed = jnp.concatenate(outs, axis=-1).astype(BF16)
        slot = QUARTER_OF.index(part)
        for owner in range(team):
            mix_ref[owner, slot * block_len : (slot + 1) * block_len, :] = mixed[
                owner * block_len : (owner + 1) * block_len, :
            ]


def attention_backward(
    team, block_len, q_width, t_ref, rot_ref, grad_ref, cos_ref, sin_ref, out_ref, wide_ref, dq_ref, dkv_ref
):
    t = t_ref[0]
    quarter = team * block_len
    heads = q_width // HEAD_DIM
    dkv_ref[...] = jnp.zeros_like(dkv_ref)
    for owner in range(team):
        for slot in range(4):
            wide_ref[QUARTER_OF[slot], owner * block_len : (owner + 1) * block_len, :] = grad_ref[
                owner, slot * block_len : (slot + 1) * block_len, :
            ]

    for part in range(4):
        span = (part + 1) * quarter
        keys = rot_ref[: part + 1, :, q_width : q_width + HEAD_DIM].reshape(span, HEAD_DIM)
        values = rot_ref[: part + 1, :, q_width + HEAD_DIM :].reshape(span, HEAD_DIM)
        row = lax.broadcasted_iota(jnp.int32, (quarter, quarter), 0)
        col = lax.broadcasted_iota(jnp.int32, (quarter, quarter), 1)
        allowed = diagonal_mask(row, col, team, block_len, part >= 2)
        for head in range(heads):
            cols = slice(head * HEAD_DIM, (head + 1) * HEAD_DIM)
            query = rot_ref[part, :, cols]
            grad = wide_ref[part, :, cols]
            scores = contract_cols(query, keys)
            last = jnp.where(allowed, scores[:, part * quarter :], -1e30)
            scores = jnp.concatenate([scores[:, : part * quarter], last], axis=-1) if part else last
            peak = jnp.max(scores, axis=-1, keepdims=True)
            expo = jnp.exp(scores - peak)
            probs = expo / jnp.sum(expo, axis=-1, keepdims=True)
            dprob = contract_cols(grad, values)
            delta = jnp.sum(probs * dprob, axis=-1, keepdims=True)
            score_grad = (probs * (dprob - delta)).astype(BF16)
            dq_ref[part, :, cols] = dot(score_grad, keys)
            dk = contract_rows(score_grad, query)
            dv = contract_rows(probs.astype(BF16), grad)
            both = jnp.concatenate([dk, dv], axis=-1).reshape(part + 1, quarter, 2 * HEAD_DIM)
            dkv_ref[: part + 1] += both

    for part in range(4):
        qk = jnp.concatenate([dq_ref[part], dkv_ref[part][:, :HEAD_DIM]], axis=-1)
        turned = qk * cos_ref[part] - swap_halves(qk) * sin_ref[part]
        dq_ref[part] = turned[:, :q_width]
        dkv_ref[part] = jnp.concatenate([turned[:, q_width:], dkv_ref[part][:, HEAD_DIM:]], axis=-1)

    def place_chunk(owner, carry):
        diff = owner ^ t
        spot = diff // 2 + (diff % 2) * (team // 2)
        rows = pl.ds(pl.multiple_of(owner * block_len, block_len), block_len)
        for slot in range(4):
            piece = jnp.concatenate([dq_ref[QUARTER_OF[slot], rows, :], dkv_ref[QUARTER_OF[slot], rows, :]], axis=-1)
            out_ref[spot, slot * block_len : (slot + 1) * block_len, :] = piece.astype(BF16)
        return carry

    lax.fori_loop(0, team, place_chunk, 0)


def vmem():
    return pl.BlockSpec(memory_space=pltpu.VMEM)


def smem():
    return pl.BlockSpec(memory_space=pltpu.SMEM)


def body(
    tokens,
    cotangent,
    attn_gain,
    q_weight,
    k_weight,
    v_weight,
    o_weight,
    ffn_gain,
    gate_weight,
    up_weight,
    down_weight,
):
    fsdp_size, cp_size = lax.axis_size("fsdp"), lax.axis_size("cp")
    devices = fsdp_size * cp_size
    teams, row_count, width = tokens.shape
    team = cp_size // teams
    block_len = row_count // 2
    chunk = teams * row_count
    token_count = team * chunk
    quarter = team * block_len
    f = lax.axis_index("fsdp")
    c = lax.axis_index("cp")
    side, t = c // team, c % team
    q_width = HEADS // team * HEAD_DIM
    copies = team // KV_HEADS
    qkv_width = q_width + 2 * HEAD_DIM
    team_groups = [[k * team + i for i in range(team)] for k in range(teams)]

    def swap(value, mask):
        return lax.ppermute(value, BOTH, [(i, i ^ mask) for i in range(devices)])

    def to_team(value):
        return lax.all_to_all(value, "cp", 0, 0, axis_index_groups=team_groups, tiled=True)

    def reorder(value):
        blocks = value.reshape(-1, fsdp_size, teams, width // (fsdp_size * teams))
        blocks = jnp.where(f == 1, blocks[:, ::-1], blocks)
        blocks = jnp.where(side == 1, blocks[:, :, ::-1], blocks)
        return blocks.reshape(value.shape)

    def own_rows(value):
        mine = jnp.where(side == 0, value[0], value[1])
        other = jnp.where(side == 0, value[1], value[0])
        theirs = swap(other, team)
        return jnp.concatenate([jnp.where(side == 0, mine, theirs), jnp.where(side == 0, theirs, mine)], axis=0)

    def give_rows(value):
        first, second = value[:row_count], value[row_count:]
        mine = jnp.where(side == 0, first, second)
        theirs = swap(jnp.where(side == 0, second, first), team)
        return jnp.stack([jnp.where(side == 0, mine, theirs), jnp.where(side == 0, theirs, mine)], axis=0)

    def team_gather(value):
        evens = jnp.concatenate([value] + [swap(value, m) for m in range(2, team, 2)], axis=0)
        return jnp.concatenate([evens, swap(evens, 1)], axis=0)

    def team_reduce(make):
        half = token_count // 2
        theirs = swap(make(1), 1)
        evens = (make(0).astype(F32) + theirs.astype(F32)).astype(BF16).reshape(team // 2, chunk, width)
        total = evens[0].astype(F32)
        for m in range(2, team, 2):
            total = total + swap(evens[m // 2], m).astype(F32)
        return total

    def gather_small(value):
        for bit in range(devices.bit_length() - 1):
            mask = 1 << bit
            index = (f * cp_size + c) & mask
            theirs = swap(value, mask)
            value = jnp.where(
                index == 0, jnp.concatenate([value, theirs], -1), jnp.concatenate([theirs, value], -1)
            )
        return value

    def scatter_small(value):
        for bit in reversed(range(devices.bit_length() - 1)):
            mask = 1 << bit
            index = (f * cp_size + c) & mask
            half = value.shape[-1] // 2
            low, high = value[..., :half], value[..., half:]
            theirs = swap(jnp.where(index == 0, high, low), mask)
            value = jnp.where(index == 0, low, high) + theirs
        return value

    def spread(pieces):
        own = to_team(pieces).reshape(team * pieces.shape[1], pieces.shape[2])
        beside = swap(own, team)
        return jnp.concatenate([own, beside, swap(own, cp_size), swap(beside, cp_size)], axis=0)

    def collect(value):
        cols = value.shape[1]
        blocks = value.reshape(fsdp_size, teams, -1, cols)
        theirs = swap(blocks[1], cp_size)
        blocks = (blocks[0].astype(F32) + theirs.astype(F32)).astype(BF16)
        theirs = swap(blocks[1], team)
        own = (blocks[0].astype(F32) + theirs.astype(F32)).astype(BF16)
        return to_team(own.reshape(team, -1, cols))

    def cut(weight):
        rows = weight.shape[0]
        return weight.reshape(rows, team, -1).transpose(1, 0, 2)

    def join(pieces):
        return pieces.transpose(1, 0, 2).reshape(pieces.shape[1], -1).astype(F32)

    def repeat_heads(weight):
        heads = weight.reshape(weight.shape[0], KV_HEADS, HEAD_DIM)
        return jnp.repeat(heads, copies, axis=1).reshape(weight.shape[0], -1)

    def sum_heads(pieces):
        grouped = pieces.astype(F32).reshape(KV_HEADS, copies, -1, HEAD_DIM).sum(axis=1)
        return grouped.transpose(1, 0, 2).reshape(grouped.shape[1], -1)

    x_float = own_rows(tokens).astype(F32)
    gains = gather_small(jnp.stack([attn_gain, ffn_gain]))
    gain_one, gain_two = gains[0:1].astype(F32), gains[1:2].astype(F32)
    qkv_team = spread(
        jnp.concatenate([cut(q_weight), cut(repeat_heads(k_weight)), cut(repeat_heads(v_weight))], axis=-1)
    )
    dy_low = own_rows(cotangent)
    o_full = lax.all_gather(o_weight, BOTH, axis=0, tiled=True)
    gate_team = spread(cut(gate_weight))
    up_team = spread(cut(up_weight))
    down_team = spread(cut(down_weight))

    inv_one = lax.rsqrt(jnp.mean(x_float * x_float, axis=-1, keepdims=True) + NORM_EPS)
    normed_one = x_float * inv_one
    attn_in = team_gather(reorder((normed_one * gain_one).astype(BF16)))
    proj = dot(attn_in, qkv_team)

    spots = jnp.arange(quarter, dtype=jnp.int32)
    owner, within = spots // block_len, spots % block_len
    flipped = (team - 1 - owner) * block_len + within
    places = jnp.stack([spots, quarter + spots, 2 * quarter + flipped, 3 * quarter + flipped])
    inverse = ROPE_BASE ** (-(2.0 * jnp.arange(HALF, dtype=F32)) / HEAD_DIM)
    angle = places.astype(F32)[:, :, None] * inverse
    cosine, sine = jnp.cos(angle), jnp.sin(angle)
    turn_heads = q_width // HEAD_DIM + 1
    scale = HEAD_DIM ** (-0.5)
    scales = jnp.concatenate([jnp.full((q_width,), scale, F32), jnp.ones((HEAD_DIM,), F32)])
    cos_table = jnp.tile(jnp.concatenate([cosine, cosine], -1), (1, 1, turn_heads)) * scales
    sin_table = jnp.tile(jnp.concatenate([-sine, sine], -1), (1, 1, turn_heads)) * scales
    t_scalar = t.astype(jnp.int32).reshape(1)

    mix_parts, rot = pl.pallas_call(
        functools.partial(attention_forward, team, block_len, q_width),
        out_shape=(
            jax.ShapeDtypeStruct((team, chunk, q_width), BF16),
            jax.ShapeDtypeStruct((4, quarter, qkv_width), BF16),
        ),
        in_specs=[smem(), vmem(), vmem(), vmem()],
        out_specs=(vmem(), vmem()),
        scratch_shapes=[pltpu.VMEM((4, quarter, qkv_width), F32)],
        compiler_params=pltpu.CompilerParams(vmem_limit_bytes=60 << 20),
        name="attention_forward",
    )(t_scalar, proj.reshape(team, chunk, qkv_width), cos_table, sin_table)

    attn_mix = to_team(mix_parts).transpose(1, 0, 2).reshape(chunk, width)
    resid = x_float + dot(attn_mix, o_full)
    inv_two = lax.rsqrt(jnp.mean(resid * resid, axis=-1, keepdims=True) + NORM_EPS)
    normed_two = resid * inv_two
    ffn_in = team_gather(reorder((normed_two * gain_two).astype(BF16)))
    dy_team = team_gather(reorder(dy_low))

    gate = dot(ffn_in, gate_team)
    up_val = dot(ffn_in, up_team)
    sigma = jax.nn.sigmoid(gate)
    silu_val = gate * sigma
    hidden = (silu_val * up_val).astype(BF16)
    hidden_grad = dot(dy_team, down_team)
    gate_grad = (hidden_grad * up_val * (sigma + gate * sigma * (1.0 - sigma))).astype(BF16)
    up_grad = (hidden_grad * silu_val).astype(BF16)

    half = token_count // 2

    def half_of(value, odd):
        return value[half * odd : half * (odd + 1)]

    ffn_in_grad = reorder(
        team_reduce(
            lambda odd: (
                contract_cols(half_of(gate_grad, odd), gate_team) + contract_cols(half_of(up_grad, odd), up_team)
            ).astype(BF16)
        )
    )
    down_sum = reorder(team_reduce(lambda odd: contract_cols(half_of(hidden, odd), down_team).astype(BF16)))
    block_out = give_rows((resid + down_sum).astype(BF16))

    ffn_gain_grad = scatter_small(jnp.sum(ffn_in_grad * normed_two, axis=0))
    scaled_two = ffn_in_grad * gain_two
    resid_grad = dy_low.astype(F32) + inv_two * (
        scaled_two - normed_two * jnp.mean(scaled_two * normed_two, axis=-1, keepdims=True)
    )
    branch_grad = resid_grad.astype(BF16)
    mix_grad = contract_cols(branch_grad, o_full).astype(BF16)
    mix_grad = to_team(mix_grad.reshape(chunk, team, q_width).transpose(1, 0, 2))
    o_weight_grad = lax.psum_scatter(
        contract_rows(attn_mix, branch_grad).astype(BF16), BOTH, scatter_dimension=0, tiled=True
    ).astype(F32)

    down_weight_grad = join(collect(contract_rows(dy_team, hidden).astype(BF16)))
    gate_weight_grad = join(collect(contract_rows(ffn_in, gate_grad).astype(BF16)))
    up_weight_grad = join(collect(contract_rows(ffn_in, up_grad).astype(BF16)))

    proj_grad = pl.pallas_call(
        functools.partial(attention_backward, team, block_len, q_width),
        out_shape=jax.ShapeDtypeStruct((team, chunk, qkv_width), BF16),
        in_specs=[smem(), vmem(), vmem(), vmem(), vmem()],
        out_specs=vmem(),
        scratch_shapes=[
            pltpu.VMEM((4, quarter, q_width), BF16),
            pltpu.VMEM((4, quarter, q_width), F32),
            pltpu.VMEM((4, quarter, 2 * HEAD_DIM), F32),
        ],
        compiler_params=pltpu.CompilerParams(vmem_limit_bytes=60 << 20),
        name="attention_backward",
    )(t_scalar, rot, mix_grad, cos_table, sin_table).reshape(token_count, qkv_width)

    attn_in_grad = reorder(
        team_reduce(lambda odd: contract_cols(half_of(proj_grad, odd), qkv_team).astype(BF16))
    )
    attn_gain_grad = scatter_small(jnp.sum(attn_in_grad * normed_one, axis=0))
    scaled_one = attn_in_grad * gain_one
    input_grad = resid_grad + inv_one * (
        scaled_one - normed_one * jnp.mean(scaled_one * normed_one, axis=-1, keepdims=True)
    )
    input_grad = give_rows(input_grad.astype(BF16))

    qkv_grad = collect(contract_rows(attn_in, proj_grad).astype(BF16))
    q_weight_grad = join(qkv_grad[:, :, :q_width])
    k_weight_grad = sum_heads(qkv_grad[:, :, q_width : q_width + HEAD_DIM])
    v_weight_grad = sum_heads(qkv_grad[:, :, q_width + HEAD_DIM :])

    return (
        block_out,
        input_grad,
        attn_gain_grad,
        q_weight_grad,
        k_weight_grad,
        v_weight_grad,
        o_weight_grad,
        ffn_gain_grad,
        gate_weight_grad,
        up_weight_grad,
        down_weight_grad,
    )


def solution(mesh):
    rows = P(BOTH, None)
    placed = P("fsdp", "cp", None)
    gain = P(BOTH)
    return jax.shard_map(
        body,
        mesh=mesh,
        in_specs=(placed, placed, gain, rows, rows, rows, rows, gain, rows, rows, rows),
        out_specs=(placed, placed, gain, rows, rows, rows, rows, gain, rows, rows, rows),
        check_vma=False,
    )
```

time: 3590 us -> 938 us (0.26)
  waiting for transfers between devices: 2910 us -> 482 us
  matrix products: 307 us -> 102 us
  starting transfers between devices: 0.81 us -> 122 us
  blocking collectives: 80.5 us -> 0 us
  other arithmetic: 153 us -> 77.2 us
    reduce_scatter x6 -> x1, waiting for transfers between devices: 2130 us -> 0.01 us  [body(): lax.psum_scatter(contract_rows(attn_mix, branch_grad).astype(BF16), BOTH,...]
    all_gather x9 -> x1, waiting for transfers between devices: 777 us -> 0.02 us  [body(): o_full = lax.all_gather(o_weight, BOTH, axis=0, tiled=True)]
    ppermute x0 -> x63, waiting for transfers between devices: none -> 480 us  [swap(): return lax.ppermute(value, BOTH, [(i, i ^ mask) for i in range(devices)])]
    concatenate x3 -> x7, other arithmetic: 136 us -> 6.2 us  [the longest x3 6.01 us: team_gather(): jnp.concatenate([value] + [swap(value, m) for m in range(2, team, 2)], ax...]
    dot_general x25 -> x5, matrix products: 127 us -> 36.1 us  [dot(): return jnp.dot(left, right, preferred_element_type=F32)]
    unnamed x2 -> x0, blocking collectives: 80.5 us -> none
    dot_general x7 -> x5, matrix products: 103 us -> 25.2 us  [contract_rows(): lax.dot_general(left, right, (((0,), (0,)), ((), ())), preferred_element_...]
    ppermute x0 -> x63, starting transfers between devices: none -> 75.8 us  [swap(): return lax.ppermute(value, BOTH, [(i, i ^ mask) for i in range(devices)])]
  transfers between devices with their start and end apart: 16 -> 75, of which waited for: 14 -> 31; matrix products, arithmetic and copies ran while one was open for 11% -> 27% of each run, Pallas kernels for 0% -> 3%
where the time goes in v1:
time: 938 us; the launch traced here: 929 us
  waiting for transfers between devices  482 us (51%)
  starting transfers between devices  122 us (13%)
  local copies, waits for them, and re-layouts  103 us (11%)
  matrix products  102 us (11%)
  other arithmetic  77.2 us (8%)
  Pallas kernels  28 us (3%)
  between operations  15.8 us (2%)
    ppermute x63, waiting for transfers between devices, swap(): return lax.ppermute(value, BOTH, [(i, i ^ mask) for i in range(devices)])  480 us
    ppermute x63, starting transfers between devices, swap(): return lax.ppermute(value, BOTH, [(i, i ^ mask) for i in range(devices)])  75.8 us
    all_to_all x10, starting transfers between devices, to_team(): lax.all_to_all(value, 'cp', 0, 0, axis_index_groups=team_groups, tiled=True)  45.6 us
    dot_general x9, matrix products, contract_cols(): lax.dot_general(left, right, (((1,), (1,)), ((), ())), preferred_element_...  40.7 us
    dot_general x5, matrix products, dot(): return jnp.dot(left, right, preferred_element_type=F32)  36.1 us
    dot_general x5, matrix products, contract_rows(): lax.dot_general(left, right, (((0,), (0,)), ((), ())), preferred_element_...  25.2 us
    rev x6, local copies, waits for them, and re-layouts, reorder(): blocks = jnp.where(side == 1, blocks[:, :, ::-1], blocks)  21 us
  transfers between devices with their start and end apart: 75, of which 31 were waited for; matrix products, arithmetic and copies ran while one was open for 27% of the time, Pallas kernels for 3%

profile of v1, /device:TPU:0, one launch (start us, length us, event | category | flops | bytes accessed | tf_op | source)
XLA Modules:
  0.0 929.4 jit_solution(1651941877118843523)
XLA Ops:
  31.6 15.2 %collective-permute-done = bf16[64,2048]{1,0:T(8,128)(2,1)S(1)} collective-permute-done((bf16[64,2048]{1,0:T(8,128)(2,1)S(1)}, bf16[64,2048]{1,0:T(8,128)(2,1)S(1)}, u32[]{:S(2)}, u32[]{:S(2)}) %collective-permute-start) | collective-permute-done | bytes 262176 | tf_op jit(solution)/shard_map/ppermute | solution.py:193
  58.2 26.5 %collective-permute-done.8 = bf16[128,2048]{1,0:T(8,128)(2,1)S(1)} collective-permute-done((bf16[128,2048]{1,0:T(8,128)(2,1)S(1)}, bf16[128,2048]{1,0:T(8,128)(2,1)S(1)}, u32[]{:S(2)}, u32[]{:S(2)}) %collective-permute-start.8) | collective-permute-done | bytes 524320 | tf_op jit(solution)/shard_map/ppermute | solution.py:193
  84.7 25.6 %collective-permute-done.7 = bf16[128,2048]{1,0:T(8,128)(2,1)S(1)} collective-permute-done((bf16[128,2048]{1,0:T(8,128)(2,1)S(1)}, bf16[128,2048]{1,0:T(8,128)(2,1)S(1)}, u32[]{:S(2)}, u32[]{:S(2)}) %collective-permute-start.7) | collective-permute-done | bytes 524320 | tf_op jit(solution)/shard_map/ppermute | solution.py:193
  133.9 18.6 %collective-permute-done.10 = bf16[512,384]{1,0:T(8,128)(2,1)S(1)} collective-permute-done((bf16[512,384]{1,0:T(8,128)(2,1)}, bf16[512,384]{1,0:T(8,128)(2,1)S(1)}, u32[]{:S(2)}, u32[]{:S(2)}) %collective-permute-start.10) | collective-permute-done | bytes 393248 | tf_op jit(solution)/shard_map/ppermute | solution.py:193
  157.0 5.9 collective-permute-done.12
  167.5 10.1 %attention_forward.1 = (bf16[8,128,256]{2,1,0:T(8,128)(2,1)}, bf16[4,256,384]{2,1,0:T(8,128)(2,1)}) custom-call(s32[1]{0:T(128)} %bitcast.2.t_ref, f32[8,128,384]{2,1,0:T(8,128)} %bitcast.164, f32[4,256,320]{2,1,0:T(8,128)} %get-tuple-element.62.cos_ref, f32[4,256,320]{2,1,0:T(8,128)} %get-tuple-element.61.sin_ref), custom_call_target="tpu_custom_call" | custom-call | tf_op jit(solution)/shard_map/attention_forward/pallas_call | solution.py:309
  204.5 11.8 %collective-permute-done.33 = bf16[128,2048]{1,0:T(8,128)(2,1)S(1)} collective-permute-done((bf16[128,2048]{1,0:T(8,128)(2,1)S(1)}, bf16[128,2048]{1,0:T(8,128)(2,1)S(1)}, u32[]{:S(2)}, u32[]{:S(2)}) %collective-permute-start.33) | collective-permute-done | bytes 524320 | tf_op jit(solution)/shard_map/ppermute | solution.py:193
  220.3 4.9 multiply_reduce_fusion.4
  238.6 44.2 %collective-permute-done.15 = bf16[128,2048]{1,0:T(8,128)(2,1)S(1)} collective-permute-done((bf16[128,2048]{1,0:T(8,128)(2,1)S(1)}, bf16[128,2048]{1,0:T(8,128)(2,1)S(1)}, u32[]{:S(2)}, u32[]{:S(2)}) %collective-permute-start.15) | collective-permute-done | bytes 524320 | tf_op jit(solution)/shard_map/ppermute | solution.py:193
  282.9 9.8 %collective-permute-done.14 = bf16[128,2048]{1,0:T(8,128)(2,1)S(1)} collective-permute-done((bf16[128,2048]{1,0:T(8,128)(2,1)S(1)}, bf16[128,2048]{1,0:T(8,128)(2,1)S(1)}, u32[]{:S(2)}, u32[]{:S(2)}) %collective-permute-start.14) | collective-permute-done | bytes 524320 | tf_op jit(solution)/shard_map/ppermute | solution.py:193
  307.8 60.6 %collective-permute-done.23 = bf16[512,1024]{1,0:T(8,128)(2,1)} collective-permute-done((bf16[512,1024]{1,0:T(8,128)(2,1)}, bf16[512,1024]{1,0:T(8,128)(2,1)}, u32[]{:S(2)}, u32[]{:S(2)}) %collective-permute-start.23) | collective-permute-done | bytes 1048608 | tf_op jit(solution)/shard_map/ppermute | solution.py:193
  370.4 20.3 %collective-permute-done.17 = bf16[512,1024]{1,0:T(8,128)(2,1)S(1)} collective-permute-done((bf16[512,1024]{1,0:T(8,128)(2,1)}, bf16[512,1024]{1,0:T(8,128)(2,1)S(1)}, u32[]{:S(2)}, u32[]{:S(2)}) %collective-permute-start.17) | collective-permute-done | bytes 1048608 | tf_op jit(solution)/shard_map/ppermute | solution.py:193
  392.3 8.3 fusion.36
  400.7 37.9 %collective-permute-done.19 = bf16[512,1024]{1,0:T(8,128)(2,1)S(1)} collective-permute-done((bf16[512,1024]{1,0:T(8,128)(2,1)S(1)}, bf16[512,1024]{1,0:T(8,128)(2,1)S(1)}, u32[]{:S(2)}, u32[]{:S(2)}) %collective-permute-start.19) | collective-permute-done | bytes 1048608 | tf_op jit(solution)/shard_map/ppermute | solution.py:193
  438.6 7.7 fusion.37
  446.3 10.6 %multiply_convert_fusion.1 = (bf16[1024,1024]{1,0:T(8,128)(2,1)}, bf16[1024,1024]{1,0:T(8,128)(2,1)S(1)}, bf16[1024,1024]{1,0:T(8,128)(2,1)}) fusion(f32[1024,1024]{1,0:T(8,128)} %fusion.36, f32[1024,1024]{1,0:T(8,128)} %fusion.37, bf16[1024,2048]{1,0:T(8,128)(2,1)S(1)} %copy-done.41, bf16[512,1024]{1,0:T(8,128)(2,1)S(1)} %collective-permute-done.25, ...), kind=kOutput, calls=%fused_computation.15 | convolution fusion | flops 4326424576 | bytes 23068672 | tf_op jit(solution)/shard_map/dot_general | solution.py:22
  474.9 5.1 convolution_convert_fusion.2
  482.8 6.2 fusion.14
  489.0 5.0 add_convert_fusion.2
  494.2 6.2 fusion.17
  520.0 18.5 %collective-permute-done.27 = bf16[128,2048]{1,0:T(8,128)(2,1)S(1)} collective-permute-done((bf16[128,2048]{1,0:T(8,128)(2,1)S(1)}, bf16[128,2048]{1,0:T(8,128)(2,1)S(1)}, u32[]{:S(2)}, u32[]{:S(2)}) %collective-permute-start.27) | collective-permute-done | bytes 524320 | tf_op jit(solution)/shard_map/ppermute | solution.py:193
  544.2 19.4 %collective-permute-done.37 = bf16[128,2048]{1,0:T(8,128)(2,1)S(1)} collective-permute-done((bf16[128,2048]{1,0:T(8,128)(2,1)}, bf16[128,2048]{1,0:T(8,128)(2,1)S(1)}, u32[]{:S(2)}, u32[]{:S(2)}) %collective-permute-start.37) | collective-permute-done | bytes 524320 | tf_op jit(solution)/shard_map/ppermute | solution.py:193
  592.1 5.6 convolution_convert_fusion
  625.4 92.4 %collective-permute-done.53 = f32[512]{0:T(512)S(1)} collective-permute-done((f32[512]{0:T(512)S(1)}, f32[512]{0:T(512)S(1)}, u32[]{:S(2)}, u32[]{:S(2)}) %collective-permute-start.53) | collective-permute-done | bytes 2080 | tf_op jit(solution)/shard_map/ppermute | solution.py:193
  717.8 6.6 collective-permute-start.54
  744.5 16.9 %collective-permute-done.30 = bf16[64,2048]{1,0:T(8,128)(2,1)S(1)} collective-permute-done((bf16[64,2048]{1,0:T(8,128)(2,1)S(1)}, bf16[64,2048]{1,0:T(8,128)(2,1)S(1)}, u32[]{:S(2)}, u32[]{:S(2)}) %collective-permute-start.30) | collective-permute-done | bytes 262176 | tf_op jit(solution)/shard_map/ppermute | solution.py:193
  765.7 17.9 %attention_backward.1 = bf16[8,128,384]{2,1,0:T(8,128)(2,1)} custom-call(s32[1]{0:T(128)} %bitcast.2.t_ref, bf16[4,256,384]{2,1,0:T(8,128)(2,1)} %get-tuple-element.14.rot_ref, bf16[8,128,256]{2,1,0:T(8,128)(2,1)} %all-to-all-done.5.grad_ref, f32[4,256,320]{2,1,0:T(8,128)} %get-tuple-element.62.cos_ref, f32[4,256,320]{2,1,0:T(8,128)} %get-tuple-element.61.sin_ref), custom_call_target="tpu_custom_call" | custom-call | tf_op jit(solution)/shard_map/attention_backward/pallas_call | solution.py:369
  783.7 6.9 all-to-all-start.7
  801.7 7.8 collective-permute-done.60
  825.5 11.6 %collective-permute-done.51 = bf16[512,384]{1,0:T(8,128)(2,1)} collective-permute-done((bf16[512,384]{1,0:T(8,128)(2,1)}, bf16[512,384]{1,0:T(8,128)(2,1)}, u32[]{:S(2)}, u32[]{:S(2)}) %collective-permute-start.51) | collective-permute-done | bytes 393248 | tf_op jit(solution)/shard_map/ppermute | solution.py:193
  859.2 20.5 %collective-permute-done.41 = bf16[128,2048]{1,0:T(8,128)(2,1)} collective-permute-done((bf16[128,2048]{1,0:T(8,128)(2,1)}, bf16[128,2048]{1,0:T(8,128)(2,1)}, u32[]{:S(2)}, u32[]{:S(2)}) %collective-permute-start.41) | collective-permute-done | bytes 524320 | tf_op jit(solution)/shard_map/ppermute | solution.py:193
  912.1 7.4 collective-permute-done.44
  (426 shorter events, 341.5 us)
Async XLA Ops:
  7.2 213.1 %all-gather.2.cloned.1.call-start = ((), (), s32[]{:S(2)}) async-start(), calls=%async_computation.11 | async-start | bytes 8650752 | tf_op jit(solution)/shard_map/all_gather | solution.py:285
  23.7 99.5 %all-to-all-start = ((bf16[8,64,384]{2,1,0:T(8,128)(2,1)}), bf16[8,64,384]{2,1,0:T(8,128)(2,1)}, u32[]{:S(2)}, u32[]{:S(2)}) async-start(bf16[8,64,384]{2,1,0:T(8,128)(2,1)} %copy.72), calls=%async_computation | async-start | bytes 786432 | tf_op jit(solution)/shard_map/all_to_all | solution.py:196
  52.9 57.4 %collective-permute-start.7 = (bf16[128,2048]{1,0:T(8,128)(2,1)S(1)}, bf16[128,2048]{1,0:T(8,128)(2,1)S(1)}, u32[]{:S(2)}, u32[]{:S(2)}) collective-permute-start(bf16[128,2048]{1,0:T(8,128)(2,1)S(1)} %reshape.383), channel_id=1, source_target_pairs={{0,4},{1,5},{2,6},{3,7},{4,0},{5,1},{6,2},{7,3},{8,12},{9,13},{10,... | collective-permute-start | bytes 1572872 | tf_op jit(solution)/shard_map/ppermute | solution.py:193
  56.2 54.1 %collective-permute-start.6 = (bf16[128,2048]{1,0:T(8,128)(2,1)S(1)}, bf16[128,2048]{1,0:T(8,128)(2,1)S(1)}, u32[]{:S(2)}, u32[]{:S(2)}) collective-permute-start(bf16[128,2048]{1,0:T(8,128)(2,1)S(1)} %reshape.383), channel_id=1, source_target_pairs={{0,2},{1,3},{2,0},{3,1},{4,6},{5,7},{6,4},{7,5},{8,10},{9,11},{10,... | collective-permute-start | bytes 1572872 | tf_op jit(solution)/shard_map/ppermute | solution.py:193
  57.1 124.8 %collective-permute-start.31 = (bf16[64,2048]{1,0:T(8,128)(2,1)}, bf16[64,2048]{1,0:T(8,128)(2,1)}, u32[]{:S(2)}, u32[]{:S(2)}) collective-permute-start(bf16[64,2048]{1,0:T(8,128)(2,1)} %select_bitcast_fusion.2), channel_id=1, source_target_pairs={{0,8},{1,9},{2,10},{3,11},{4,12},{5,13},{6,14},{7,15},{8,0},{9,1},... | collective-permute-start | bytes 786440 | tf_op jit(solution)/shard_map/ppermute | solution.py:193
  112.0 43.3 %collective-permute-start.9 = (bf16[512,2048]{1,0:T(8,128)(2,1)}, bf16[512,2048]{1,0:T(8,128)(2,1)}, u32[]{:S(2)}, u32[]{:S(2)}) collective-permute-start(bf16[512,2048]{1,0:T(8,128)(2,1)} %pad_maximum_fusion.3), channel_id=1, source_target_pairs={{0,1},{1,0},{2,3},{3,2},{4,5},{5,4},{6,7},{7,6},{8,9},{9,8},{10,11... | collective-permute-start | bytes 6291464 | tf_op jit(solution)/shard_map/ppermute | solution.py:193
  123.2 54.4 %all-to-all-start.3 = ((bf16[8,64,1024]{2,1,0:T(8,128)(2,1)}), bf16[8,64,1024]{2,1,0:T(8,128)(2,1)}, u32[]{:S(2)}, u32[]{:S(2)}) async-start(bf16[8,64,1024]{2,1,0:T(8,128)(2,1)} %copy.79), calls=%async_computation.3 | async-start | bytes 2097152 | tf_op jit(solution)/shard_map/all_to_all | solution.py:196
  219.0 78.7 %collective-permute-start.35 = (bf16[512,2048]{1,0:T(8,128)(2,1)}, bf16[512,2048]{1,0:T(8,128)(2,1)}, u32[]{:S(2)}, u32[]{:S(2)}) collective-permute-start(bf16[512,2048]{1,0:T(8,128)(2,1)} %pad_maximum_fusion.5), channel_id=1, source_target_pairs={{0,1},{1,0},{2,3},{3,2},{4,5},{5,4},{6,7},{7,6},{8,9},{9,8},{10,11... | collective-permute-start | bytes 6291464 | tf_op jit(solution)/shard_map/ppermute | solution.py:193
  229.1 68.5 %all-to-all-start.2 = ((bf16[8,64,1024]{2,1,0:T(8,128)(2,1)}), bf16[8,64,1024]{2,1,0:T(8,128)(2,1)}, u32[]{:S(2)}, u32[]{:S(2)}) async-start(bf16[8,64,1024]{2,1,0:T(8,128)(2,1)} %copy.78), calls=%async_computation.2 | async-start | bytes 2097152 | tf_op jit(solution)/shard_map/all_to_all | solution.py:196
  233.4 687.0 %reduce-scatter.2.cloned.1.call-start = ((), (), s32[]{:S(2)}) async-start(), calls=%async_computation.12 | async-start | bytes 8650752 | tf_op jit(solution)/shard_map/reduce_scatter | solution.py:361
  234.9 47.9 %collective-permute-start.15 = (bf16[128,2048]{1,0:T(8,128)(2,1)S(1)}, bf16[128,2048]{1,0:T(8,128)(2,1)S(1)}, u32[]{:S(2)}, u32[]{:S(2)}) collective-permute-start(bf16[128,2048]{1,0:T(8,128)(2,1)S(1)} %reshape.389), channel_id=1, source_target_pairs={{0,6},{1,7},{2,4},{3,5},{4,2},{5,3},{6,0},{7,1},{8,14},{9,15},{10,... | collective-permute-start | bytes 1572872 | tf_op jit(solution)/shard_map/ppermute | solution.py:193
  237.8 54.9 %collective-permute-start.14 = (bf16[128,2048]{1,0:T(8,128)(2,1)S(1)}, bf16[128,2048]{1,0:T(8,128)(2,1)S(1)}, u32[]{:S(2)}, u32[]{:S(2)}) collective-permute-start(bf16[128,2048]{1,0:T(8,128)(2,1)S(1)} %reshape.389), channel_id=1, source_target_pairs={{0,4},{1,5},{2,6},{3,7},{4,0},{5,1},{6,2},{7,3},{8,12},{9,13},{10,... | collective-permute-start | bytes 1572872 | tf_op jit(solution)/shard_map/ppermute | solution.py:193
  238.3 54.4 %collective-permute-start.13 = (bf16[128,2048]{1,0:T(8,128)(2,1)S(1)}, bf16[128,2048]{1,0:T(8,128)(2,1)S(1)}, u32[]{:S(2)}, u32[]{:S(2)}) collective-permute-start(bf16[128,2048]{1,0:T(8,128)(2,1)S(1)} %reshape.389), channel_id=1, source_target_pairs={{0,2},{1,3},{2,0},{3,1},{4,6},{5,7},{6,4},{7,5},{8,10},{9,11},{10,... | collective-permute-start | bytes 1572872 | tf_op jit(solution)/shard_map/ppermute | solution.py:193
  238.5 65.2 %collective-permute-start.20 = (bf16[512,1024]{1,0:T(8,128)(2,1)}, bf16[512,1024]{1,0:T(8,128)(2,1)}, u32[]{:S(2)}, u32[]{:S(2)}) collective-permute-start(bf16[512,1024]{1,0:T(8,128)(2,1)} %bitcast.18), channel_id=1, source_target_pairs={{0,8},{1,9},{2,10},{3,11},{4,12},{5,13},{6,14},{7,15},{8,0},{9,1},... | collective-permute-start | bytes 3145736 | tf_op jit(solution)/shard_map/ppermute | solution.py:193
  295.7 74.3 %collective-permute-start.21 = (bf16[512,1024]{1,0:T(8,128)(2,1)}, bf16[512,1024]{1,0:T(8,128)(2,1)}, u32[]{:S(2)}, u32[]{:S(2)}) collective-permute-start(bf16[512,1024]{1,0:T(8,128)(2,1)} %bitcast.18), channel_id=1, source_target_pairs={{0,16},{1,17},{2,18},{3,19},{4,20},{5,21},{6,22},{7,23},{8,24},{9,... | collective-permute-start | bytes 3145736 | tf_op jit(solution)/shard_map/ppermute | solution.py:193
  297.6 70.7 %collective-permute-start.23 = (bf16[512,1024]{1,0:T(8,128)(2,1)}, bf16[512,1024]{1,0:T(8,128)(2,1)}, u32[]{:S(2)}, u32[]{:S(2)}) collective-permute-start(bf16[512,1024]{1,0:T(8,128)(2,1)} %bitcast.20), channel_id=1, source_target_pairs={{0,8},{1,9},{2,10},{3,11},{4,12},{5,13},{6,14},{7,15},{8,0},{9,1},... | collective-permute-start | bytes 3145736 | tf_op jit(solution)/shard_map/ppermute | solution.py:193
  297.6 93.0 %collective-permute-start.17 = (bf16[512,1024]{1,0:T(8,128)(2,1)}, bf16[512,1024]{1,0:T(8,128)(2,1)S(1)}, u32[]{:S(2)}, u32[]{:S(2)}) collective-permute-start(bf16[512,1024]{1,0:T(8,128)(2,1)} %bitcast.16), channel_id=1, source_target_pairs={{0,8},{1,9},{2,10},{3,11},{4,12},{5,13},{6,14},{7,15},{8,0},{9,1},... | collective-permute-start | bytes 3145736 | tf_op jit(solution)/shard_map/ppermute | solution.py:193
  303.7 88.6 %collective-permute-start.22 = (bf16[512,1024]{1,0:T(8,128)(2,1)}, bf16[512,1024]{1,0:T(8,128)(2,1)S(1)}, u32[]{:S(2)}, u32[]{:S(2)}) collective-permute-start(bf16[512,1024]{1,0:T(8,128)(2,1)} %collective-permute-done.20), channel_id=1, source_target_pairs={{0,16},{1,17},{2,18},{3,19},{4,20},{5,21},{6,22},{7,23},{8,24},{9,... | collective-permute-start | bytes 3145736 | tf_op jit(solution)/shard_map/ppermute | solution.py:193
  305.6 140.7 %collective-permute-start.24 = (bf16[512,1024]{1,0:T(8,128)(2,1)}, bf16[512,1024]{1,0:T(8,128)(2,1)S(1)}, u32[]{:S(2)}, u32[]{:S(2)}) collective-permute-start(bf16[512,1024]{1,0:T(8,128)(2,1)} %bitcast.20), channel_id=1, source_target_pairs={{0,16},{1,17},{2,18},{3,19},{4,20},{5,21},{6,22},{7,23},{8,24},{9,... | collective-permute-start | bytes 3145736 | tf_op jit(solution)/shard_map/ppermute | solution.py:193
  370.0 76.3 %collective-permute-start.25 = (bf16[512,1024]{1,0:T(8,128)(2,1)}, bf16[512,1024]{1,0:T(8,128)(2,1)S(1)}, u32[]{:S(2)}, u32[]{:S(2)}) collective-permute-start(bf16[512,1024]{1,0:T(8,128)(2,1)} %collective-permute-done.23), channel_id=1, source_target_pairs={{0,16},{1,17},{2,18},{3,19},{4,20},{5,21},{6,22},{7,23},{8,24},{9,... | collective-permute-start | bytes 3145736 | tf_op jit(solution)/shard_map/ppermute | solution.py:193
  390.7 47.9 %collective-permute-start.19 = (bf16[512,1024]{1,0:T(8,128)(2,1)S(1)}, bf16[512,1024]{1,0:T(8,128)(2,1)S(1)}, u32[]{:S(2)}, u32[]{:S(2)}) collective-permute-start(bf16[512,1024]{1,0:T(8,128)(2,1)S(1)} %collective-permute-done.17), channel_id=1, source_target_pairs={{0,16},{1,17},{2,18},{3,19},{4,20},{5,21},{6,22},{7,23},{8,24},{9,... | collective-permute-start | bytes 3145736 | tf_op jit(solution)/shard_map/ppermute | solution.py:193
  468.3 43.5 %collective-permute-start.26 = (bf16[512,2048]{1,0:T(8,128)(2,1)S(1)}, bf16[512,2048]{1,0:T(8,128)(2,1)S(1)}, u32[]{:S(2)}, u32[]{:S(2)}) collective-permute-start(bf16[512,2048]{1,0:T(8,128)(2,1)S(1)} %convolution_convert_fusion.4), channel_id=1, source_target_pairs={{0,1},{1,0},{2,3},{3,2},{4,5},{5,4},{6,7},{7,6},{8,9},{9,8},{10,11... | collective-permute-start | bytes 6291464 | tf_op jit(solution)/shard_map/ppermute | solution.py:193
  468.4 129.3 %collective-permute-start.61 = (bf16[2,512,1024]{2,1,0:T(8,128)(2,1)}, bf16[2,512,1024]{2,1,0:T(8,128)(2,1)}, u32[]{:S(2)}, u32[]{:S(2)}) collective-permute-start(bf16[2,512,1024]{2,1,0:T(8,128)(2,1)} %bitcast.54), channel_id=1, source_target_pairs={{0,16},{1,17},{2,18},{3,19},{4,20},{5,21},{6,22},{7,23},{8,24},{9,... | collective-permute-start | bytes 6291464 | tf_op jit(solution)/shard_map/ppermute | solution.py:193
  482.4 122.8 %collective-permute-start.57 = (bf16[2,512,1024]{2,1,0:T(8,128)(2,1)}, bf16[2,512,1024]{2,1,0:T(8,128)(2,1)}, u32[]{:S(2)}, u32[]{:S(2)}) collective-permute-start(bf16[2,512,1024]{2,1,0:T(8,128)(2,1)} %bitcast.42), channel_id=1, source_target_pairs={{0,16},{1,17},{2,18},{3,19},{4,20},{5,21},{6,22},{7,23},{8,24},{9,... | collective-permute-start | bytes 6291464 | tf_op jit(solution)/shard_map/ppermute | solution.py:193
  563.6 160.8 %collective-permute-start.59 = (bf16[2,512,1024]{2,1,0:T(8,128)(2,1)}, bf16[2,512,1024]{2,1,0:T(8,128)(2,1)}, u32[]{:S(2)}, u32[]{:S(2)}) collective-permute-start(bf16[2,512,1024]{2,1,0:T(8,128)(2,1)} %bitcast.163), channel_id=1, source_target_pairs={{0,16},{1,17},{2,18},{3,19},{4,20},{5,21},{6,22},{7,23},{8,24},{9,... | collective-permute-start | bytes 6291464 | tf_op jit(solution)/shard_map/ppermute | solution.py:193
  603.1 127.2 %collective-permute-start.62 = (bf16[512,1024]{1,0:T(8,128)(2,1)}, bf16[512,1024]{1,0:T(8,128)(2,1)}, u32[]{:S(2)}, u32[]{:S(2)}) collective-permute-start(bf16[512,1024]{1,0:T(8,128)(2,1)} %slice_bitcast_fusion), channel_id=1, source_target_pairs={{0,8},{1,9},{2,10},{3,11},{4,12},{5,13},{6,14},{7,15},{8,0},{9,1},... | collective-permute-start | bytes 3145736 | tf_op jit(solution)/shard_map/ppermute | solution.py:193
  610.4 152.7 %collective-permute-start.58 = (bf16[512,1024]{1,0:T(8,128)(2,1)}, bf16[512,1024]{1,0:T(8,128)(2,1)}, u32[]{:S(2)}, u32[]{:S(2)}) collective-permute-start(bf16[512,1024]{1,0:T(8,128)(2,1)} %slice_bitcast_fusion.4), channel_id=1, source_target_pairs={{0,8},{1,9},{2,10},{3,11},{4,12},{5,13},{6,14},{7,15},{8,0},{9,1},... | collective-permute-start | bytes 3145736 | tf_op jit(solution)/shard_map/ppermute | solution.py:193
  611.6 106.2 %collective-permute-start.53 = (f32[512]{0:T(512)S(1)}, f32[512]{0:T(512)S(1)}, u32[]{:S(2)}, u32[]{:S(2)}) collective-permute-start(f32[512]{0:T(512)S(1)} %slice_select_fusion.1), channel_id=1, source_target_pairs={{0,8},{1,9},{2,10},{3,11},{4,12},{5,13},{6,14},{7,15},{8,0},{9,1},... | collective-permute-start | bytes 6152 | tf_op jit(solution)/shard_map/ppermute | solution.py:193
  621.2 111.7 %all-to-all-start.5 = ((bf16[8,128,256]{2,1,0:T(8,128)(2,1)}), bf16[8,128,256]{2,1,0:T(8,128)(2,1)}, u32[]{:S(2)}, u32[]{:S(2)}) async-start(bf16[8,128,256]{2,1,0:T(8,128)(2,1)} %bitcast.161), calls=%async_computation.5 | async-start | bytes 1048576 | tf_op jit(solution)/shard_map/all_to_all | solution.py:196
  732.9 50.7 %all-to-all-start.9 = ((bf16[8,64,1024]{2,1,0:T(8,128)(2,1)}), bf16[8,64,1024]{2,1,0:T(8,128)(2,1)}, u32[]{:S(2)}, u32[]{:S(2)}) async-start(bf16[8,64,1024]{2,1,0:T(8,128)(2,1)} %bitcast.152), calls=%async_computation.10 | async-start | bytes 2097152 | tf_op jit(solution)/shard_map/all_to_all | solution.py:196
  743.4 66.0 %collective-permute-start.60 = (bf16[512,1024]{1,0:T(8,128)(2,1)}, bf16[512,1024]{1,0:T(8,128)(2,1)}, u32[]{:S(2)}, u32[]{:S(2)}) collective-permute-start(bf16[512,1024]{1,0:T(8,128)(2,1)} %slice_bitcast_fusion.2), channel_id=1, source_target_pairs={{0,8},{1,9},{2,10},{3,11},{4,12},{5,13},{6,14},{7,15},{8,0},{9,1},... | collective-permute-start | bytes 3145736 | tf_op jit(solution)/shard_map/ppermute | solution.py:193
  801.4 42.2 %collective-permute-start.40 = (bf16[512,2048]{1,0:T(8,128)(2,1)}, bf16[512,2048]{1,0:T(8,128)(2,1)}, u32[]{:S(2)}, u32[]{:S(2)}) collective-permute-start(bf16[512,2048]{1,0:T(8,128)(2,1)} %convolution_convert_fusion.6), channel_id=1, source_target_pairs={{0,1},{1,0},{2,3},{3,2},{4,5},{5,4},{6,7},{7,6},{8,9},{9,8},{10,11... | collective-permute-start | bytes 6291464 | tf_op jit(solution)/shard_map/ppermute | solution.py:193
  (101 other events, 2048.4 us)
Sparse Core Ops, SparseCore 0:
  10.9 99.2 all-gather.1
  597.8 182.1 reduce-scatter.1

commit v2 on v1

v2 whole, which is shorter than its diff:
```python
import functools

import jax
import jax.numpy as jnp
from jax import lax
from jax.experimental import pallas as pl
from jax.experimental.pallas import tpu as pltpu
from jax.sharding import PartitionSpec as P

HEADS = 32
KV_HEADS = 8
HEAD_DIM = 64
HALF = HEAD_DIM // 2
NORM_EPS = 1e-05
ROPE_BASE = 500000.0
BOTH = ("fsdp", "cp")
F32 = jnp.float32
BF16 = jnp.bfloat16
MESH = pl.DeviceIdType.MESH
VMEM_BYTES = 60 << 20


def dot(left, right):
    return jnp.dot(left, right, preferred_element_type=F32)


def contract_rows(left, right):
    return lax.dot_general(left, right, (((0,), (0,)), ((), ())), preferred_element_type=F32)


def contract_cols(left, right):
    return lax.dot_general(left, right, (((1,), (1,)), ((), ())), preferred_element_type=F32)


def flip(index, mask):
    bit = 1
    out = index
    while bit <= mask:
        if mask & bit:
            out = out + bit - 2 * bit * ((index // bit) % 2)
        bit *= 2
    return out


def spot_of(diff, team):
    return diff // 2 + (diff % 2) * (team // 2)


def chunk_blocks(member, team):
    second = team + flip(member, team // 2)
    last = 4 * team - 1
    return member, last - member, second, last - second


def natural_unit(mine, index):
    block = flip(mine, index // 2)
    turned = block % 2
    return block * 2 + (index % 2) + turned * (1 - 2 * (index % 2))


def swap_halves(wide):
    pieces = []
    for start in range(0, wide.shape[-1], HEAD_DIM):
        pieces.append(wide[:, start + HALF : start + HEAD_DIM])
        pieces.append(wide[:, start : start + HALF])
    return jnp.concatenate(pieces, axis=-1)


def over_row_blocks(token_count, step):
    quarter = token_count // 4
    rows = min(256, (1 << 18) // token_count)
    for first in range(0, token_count, quarter):
        if rows == quarter:
            step(first, first + quarter, first, rows)
        else:

            def block(index, carry, first=first):
                step(first, first + quarter, pl.multiple_of(first + index * rows, rows), rows)
                return carry

            lax.fori_loop(0, quarter // rows, block, 0)


def masked_scores(query, keys, first, start):
    rows, span = query.shape[0], keys.shape[0] - first
    scores = contract_cols(query, keys)
    row = lax.broadcasted_iota(jnp.int32, (rows, span), 0) + (start - first)
    col = lax.broadcasted_iota(jnp.int32, (rows, span), 1)
    last = jnp.where(row >= col, scores[:, first:], -1e30)
    return jnp.concatenate([scores[:, :first], last], axis=-1) if first else last


def differ(left, right, size):
    out = 0
    bit = 1
    while bit < size:
        out = out + ((left // bit + right // bit) % 2) * bit
        bit *= 2
    return out


class Links:
    def __init__(self, cp_size, send, recv, local):
        self.f, self.c = lax.axis_index("fsdp"), lax.axis_index("cp")
        self.cp_size, self.send, self.recv, self.local = cp_size, send, recv, local
        self.used = self.used_local = 0

    def device(self, mask):
        return (flip(self.f, mask // self.cp_size), flip(self.c, mask % self.cp_size))

    def barrier(self, masks):
        sem = pltpu.get_barrier_semaphore()
        for mask in masks:
            pl.semaphore_signal(sem, inc=1, device_id=self.device(mask), device_id_type=MESH)
        pl.semaphore_wait(sem, len(masks))

    def copy(self, src, dst, mask):
        index = self.used
        self.used += 1
        return pltpu.make_async_remote_copy(
            src_ref=src,
            dst_ref=dst,
            send_sem=self.send.at[index],
            recv_sem=self.recv.at[index],
            device_id=self.device(mask),
            device_id_type=MESH,
        )

    def inside(self, src, dst):
        index = self.used_local
        self.used_local += 1
        return pltpu.make_async_copy(src, dst, self.local.at[index])


class TeamGather:
    def __init__(self, links, team, src, dst):
        self.evens = range(2, team, 2)
        self.dst, self.team = dst, team
        self.sends = [links.copy(src, dst.at[spot_of(m, team)], m) for m in self.evens]
        self.passes = [links.copy(src, dst.at[spot_of(1, team)], 1)]
        for m in self.evens:
            self.passes.append(links.copy(dst.at[spot_of(m, team)], dst.at[spot_of(m + 1, team)], 1))
        self.own = links.inside(src, dst.at[0])

    def start(self):
        for send in self.sends:
            send.start()
        self.passes[0].start()
        self.own.start()

    def forward(self, index):
        self.sends[index].wait_recv()
        self.passes[index + 1].start()

    def finish(self):
        for passed in self.passes:
            passed.wait_recv()
        for send in self.sends + self.passes:
            send.wait_send()
        self.own.wait()


class Spread:
    def __init__(self, links, team, t, inner, pieces, full, above, below):
        self.inner, self.team = inner, team
        near, mirror = team // 2, team + team // 2
        across = links.cp_size
        self.own = links.inside(pieces(0), full.at[0, t])
        self.cuts = [links.copy(pieces(m), full.at[0, t], m) for m in range(1, team)]
        self.far = [links.copy(full.at[0], full.at[2], across), links.copy(full.at[1], full.at[3], across)]
        self.straight = links.copy(full.at[0], full.at[1], mirror)
        self.up = links.copy(full.at[0], above, near)
        self.over = links.copy(above, below, mirror)
        self.down = links.copy(below, full.at[1], near)

    def cut(self):
        self.own.start()
        for piece in self.cuts:
            piece.start()

    def leave(self):
        self.own.wait()
        for piece in self.cuts:
            piece.wait_recv()
        self.far[0].start()

        @pl.when(self.inner)
        def _():
            self.straight.start()

        @pl.when(jnp.logical_not(self.inner))
        def _():
            self.up.start()

    def relay(self):
        @pl.when(self.inner)
        def _():
            self.up.wait_recv()
            self.over.start()

    def arrive(self):
        @pl.when(self.inner)
        def _():
            self.straight.wait_recv()
            self.far[1].start()
            self.over.wait_recv()
            self.down.start()

        @pl.when(jnp.logical_not(self.inner))
        def _():
            self.down.wait_recv()
            self.far[1].start()

    def finish(self):
        for copy in self.far:
            copy.wait_recv()
        for copy in self.cuts + self.far:
            copy.wait_send()

        @pl.when(self.inner)
        def _():
            self.straight.wait_send()
            self.over.wait_send()
            self.down.wait_send()

        @pl.when(jnp.logical_not(self.inner))
        def _():
            self.up.wait_send()


def entry_kernel(
    fsdp_size,
    cp_size,
    tokens,
    cotangent,
    gains_in,
    qkv_cut,
    o_cut,
    gate_in,
    up_in,
    down_in,
    cos_ref,
    sin_ref,
    x_ref,
    gains_ref,
    attn_in_ref,
    qkv_full,
    o_wide,
    rot_ref,
    mix_ref,
    resid_ref,
    ffn_in_ref,
    dy_ref,
    gate_full,
    up_full,
    down_full,
    o_full,
    *rest,
):
    relays, scratch = rest[:10], rest[10:]
    (send, recv, local, swapped, dy_swapped, slots, chunk_ref, dy_chunk, acts, wqkv, mixed, o_pieces, taken, parts) = scratch
    links = Links(cp_size, send, recv, local)
    f, c = links.f, links.c
    team = cp_size // 2
    near, mirror = team // 2, team + team // 2
    side = c // team
    t = c % team + side * (flip(c, near) - c)
    inner = t // near == 1
    row_count, width = tokens.shape[1], tokens.shape[2]
    block_len = row_count // 2
    unit = width // 8
    token_count, q_width = mixed.shape
    heads = q_width // HEAD_DIM
    cols = gate_full.shape[-1]
    mine = f * 2 + side

    links.barrier(list(range(1, team)) + [mirror, cp_size])
    swap = links.copy(tokens.at[1 - side], swapped, mirror)
    swap.start()
    slots[0] = gains_in[...]
    stages = []
    size = 1
    for mask in [1 << k for k in range(team.bit_length() - 1)] + [mirror, cp_size]:
        stages.append(links.copy(slots.at[pl.ds(0, size)], slots.at[pl.ds(size, size)], mask))
        size *= 2

    def columns_of(weight):
        return lambda m: weight.at[:, pl.ds(pl.multiple_of(flip(t, m) * cols, cols), cols)]

    def spread(pieces, full, index):
        return Spread(links, team, t, inner, pieces, full, relays[2 * index], relays[2 * index + 1])

    qkv_spread = spread(lambda m: qkv_cut.at[flip(t, m)], qkv_full, 0)
    o_spread = spread(lambda m: o_cut.at[flip(t, m)], o_full, 1)
    gate_spread = spread(columns_of(gate_in), gate_full, 2)
    up_spread = spread(columns_of(up_in), up_full, 3)
    down_spread = spread(columns_of(down_in), down_full, 4)

    stages[0].start()
    qkv_spread.cut()
    o_spread.cut()
    for step in range(1, len(stages)):
        stages[step - 1].wait_recv()
        stages[step].start()
    gate_spread.cut()

    def fill(dst, source, theirs):
        here = pl.ds(pl.multiple_of(side * row_count, row_count), row_count)
        there = pl.ds(pl.multiple_of((1 - side) * row_count, row_count), row_count)
        for index in range(8):
            cols = slice(index * unit, (index + 1) * unit)
            natural = pl.ds(pl.multiple_of(natural_unit(mine, index) * unit, unit), unit)
            dst[here, cols] = source[side, :, natural].astype(dst.dtype)
            dst[there, cols] = theirs[:, natural].astype(dst.dtype)

    stages[-1].wait_recv()
    pieces = []
    for b in range(4):
        for member in range(team):
            pieces.append(slots[b * team + flip(t, member)][:8, : width // (4 * team)])
    gains = jnp.concatenate(pieces, axis=-1).astype(F32)
    gains_ref[...] = gains
    swap.wait_recv()
    fill(x_ref, tokens, swapped)
    x = x_ref[...]
    inv_one = lax.rsqrt(jnp.mean(x * x, axis=-1, keepdims=True) + NORM_EPS)
    chunk_ref[...] = (x * inv_one * gains[0:1]).astype(BF16)
    gather_one = TeamGather(links, team, chunk_ref, acts)
    gather_one.start()
    dy_swap = links.copy(cotangent.at[1 - side], dy_swapped, mirror)
    dy_swap.start()
    qkv_spread.leave()
    o_spread.leave()
    up_spread.cut()
    down_spread.cut()
    for index in range(len(gather_one.sends) - 1):
        gather_one.forward(index)
    qkv_spread.relay()
    o_spread.relay()
    gather_one.forward(len(gather_one.sends) - 1)
    gate_spread.leave()
    qkv_spread.arrive()
    o_spread.arrive()
    gate_spread.relay()
    qkv_spread.finish()
    load = links.inside(qkv_full, wqkv)
    load.start()
    gather_one.finish()
    attn_out = links.inside(acts, attn_in_ref)
    attn_out.start()
    o_spread.finish()

    o_rows = o_full.shape[2]

    def o_source(m):
        count = q_width // o_rows
        first = flip(t, m) * count
        owners, start = first // team, first % team
        block = ((owners // 2 + mine // 2) % 2) * 2 + (owners + mine) % 2
        return o_full.at[block, pl.ds(start + (owners % 2) * (flip(start, near) - start), count)]

    o_own = links.inside(o_source(0), o_pieces.at[t])
    o_sends = [links.copy(o_source(m), o_pieces.at[t], m) for m in range(1, team)]
    o_own.start()
    for copy in o_sends:
        copy.start()
    up_spread.leave()

    load.wait()
    weights = wqkv[...].reshape(width, wqkv.shape[-1])

    def project(m, carry):
        proj = dot(acts[spot_of(m, team)], weights)
        qk = proj[:, : q_width + HEAD_DIM]
        qk_swapped = swap_halves(qk)
        blocks = chunk_blocks(differ(t, m, team), team)
        for slot in range(4):
            piece = slice(slot * block_len, (slot + 1) * block_len)
            rows = pl.ds(pl.multiple_of(blocks[slot] * block_len, block_len), block_len)
            turned = qk[piece] * cos_ref[rows, :] + qk_swapped[piece] * sin_ref[rows, :]
            rot_ref[rows, :] = jnp.concatenate([turned, proj[piece, q_width + HEAD_DIM :]], axis=-1).astype(BF16)
        return carry

    lax.fori_loop(0, team, project, 0)
    gate_spread.arrive()

    dy_swap.wait_recv()
    fill(dy_chunk, cotangent, dy_swapped)
    gather_dy = TeamGather(links, team, dy_chunk, dy_ref)
    gather_dy.start()
    up_spread.relay()

    def attend(first, span, start, rows):
        keys = rot_ref[:span, q_width : q_width + HEAD_DIM]
        values = rot_ref[:span, q_width + HEAD_DIM :]
        outs = []
        for head in range(heads):
            query = rot_ref[pl.ds(start, rows), head * HEAD_DIM : (head + 1) * HEAD_DIM]
            scores = masked_scores(query, keys, first, start)
            peak = jnp.max(scores, axis=-1, keepdims=True)
            expo = jnp.exp(scores - peak)
            total = jnp.sum(expo, axis=-1, keepdims=True)
            outs.append(dot(expo.astype(BF16), values) / total)
        mixed[pl.ds(start, rows), :] = jnp.concatenate(outs, axis=-1).astype(BF16)

    over_row_blocks(token_count, attend)
    gather_dy.forward(0)

    def collect_mix(m, carry):
        blocks = chunk_blocks(differ(t, m, team), team)
        for slot in range(4):
            where = pl.ds(pl.multiple_of(blocks[slot] * block_len, block_len), block_len)
            mix_ref[spot_of(m, team), slot * block_len : (slot + 1) * block_len, :] = mixed[where, :]
        return carry

    lax.fori_loop(0, team, collect_mix, 0)
    for copy in o_sends:
        copy.wait_recv()
    o_own.wait()
    span = width // team
    for index in range(8):
        for piece in range(team // 8):
            start = index * unit + piece * span
            source = natural_unit(mine, index) * (team // 8) + piece
            o_wide[:, start : start + span] = o_pieces[source].reshape(q_width, span)

    attn_out.wait()
    half = team // 2
    crossed = []
    for spot in range(half, team):
        acts[spot] = dot(mix_ref[spot], o_wide[...]).astype(BF16)
        copy = links.copy(acts.at[spot], taken.at[spot - half], 1)
        copy.start()
        crossed.append(copy)
    for index in range(1, len(gather_dy.sends)):
        gather_dy.forward(index)
    down_spread.leave()
    given = []
    for spot in list(range(1, half)) + [0]:
        part = dot(mix_ref[spot], o_wide[...])
        crossed[spot].wait_recv()
        if spot:
            acts[spot] = (part + taken[spot].astype(F32)).astype(BF16)
            copy = links.copy(acts.at[spot], parts.at[spot - 1], 2 * spot)
            copy.start()
            given.append(copy)
        else:
            resid_ref[...] = x_ref[...] + part + taken[0].astype(F32)
    up_spread.arrive()
    down_spread.relay()
    for index, copy in enumerate(given):
        copy.wait_recv()
        resid_ref[...] += parts[index].astype(F32)
    resid = resid_ref[...]
    inv_two = lax.rsqrt(jnp.mean(resid * resid, axis=-1, keepdims=True) + NORM_EPS)
    chunk_ref[...] = (resid * inv_two * gains_ref[1:2]).astype(BF16)
    gather_two = TeamGather(links, team, chunk_ref, ffn_in_ref)
    gather_two.start()
    gather_dy.finish()
    for index in range(len(gather_two.sends)):
        gather_two.forward(index)
    gate_spread.finish()
    down_spread.arrive()
    gather_two.finish()
    up_spread.finish()
    down_spread.finish()
    swap.wait_send()
    dy_swap.wait_send()
    for copy in stages + o_sends + crossed + given:
        copy.wait_send()


def attention_backward(
    team, block_len, q_width, where_ref, rot_ref, grad_ref, cos_ref, sin_ref, out_ref, wide_ref, dq_ref, dkv_ref
):
    t = where_ref[0]
    token_count = wide_ref.shape[0]
    heads = q_width // HEAD_DIM
    dkv_ref[...] = jnp.zeros_like(dkv_ref)

    def place_grad(m, carry):
        blocks = chunk_blocks(differ(t, m, team), team)
        for slot in range(4):
            where = pl.ds(pl.multiple_of(blocks[slot] * block_len, block_len), block_len)
            wide_ref[where, :] = grad_ref[spot_of(m, team), slot * block_len : (slot + 1) * block_len, :]
        return carry

    lax.fori_loop(0, team, place_grad, 0)

    def attend(first, span, start, count):
        rows = pl.ds(start, count)
        keys = rot_ref[:span, q_width : q_width + HEAD_DIM]
        values = rot_ref[:span, q_width + HEAD_DIM :]
        for head in range(heads):
            cols = slice(head * HEAD_DIM, (head + 1) * HEAD_DIM)
            query = rot_ref[rows, cols]
            grad = wide_ref[rows, cols]
            scores = masked_scores(query, keys, first, start)
            peak = jnp.max(scores, axis=-1, keepdims=True)
            expo = jnp.exp(scores - peak)
            probs = expo / jnp.sum(expo, axis=-1, keepdims=True)
            dprob = contract_cols(grad, values)
            delta = jnp.sum(probs * dprob, axis=-1, keepdims=True)
            score_grad = (probs * (dprob - delta)).astype(BF16)
            dq_ref[rows, cols] = dot(score_grad, keys)
            dk = contract_rows(score_grad, query)
            dv = contract_rows(probs.astype(BF16), grad)
            dkv_ref[:span, :] += jnp.concatenate([dk, dv], axis=-1)

    over_row_blocks(token_count, attend)

    for start in range(0, token_count, token_count // 4):
        rows = slice(start, start + token_count // 4)
        qk = jnp.concatenate([dq_ref[rows, :], dkv_ref[rows, :HEAD_DIM]], axis=-1)
        turned = qk * cos_ref[rows, :] - swap_halves(qk) * sin_ref[rows, :]
        dq_ref[rows, :] = turned[:, :q_width]
        dkv_ref[rows, :] = jnp.concatenate([turned[:, q_width:], dkv_ref[rows, HEAD_DIM:]], axis=-1)

    def give_chunk(m, carry):
        blocks = chunk_blocks(differ(t, m, team), team)
        for slot in range(4):
            rows = pl.ds(pl.multiple_of(blocks[slot] * block_len, block_len), block_len)
            piece = jnp.concatenate([dq_ref[rows, :], dkv_ref[rows, :]], axis=-1)
            out_ref[spot_of(m, team), slot * block_len : (slot + 1) * block_len, :] = piece.astype(BF16)
        return carry

    lax.fori_loop(0, team, give_chunk, 0)


def vmem():
    return pl.BlockSpec(memory_space=pltpu.VMEM)


def smem():
    return pl.BlockSpec(memory_space=pltpu.SMEM)


def anywhere():
    return pl.BlockSpec(memory_space=pl.ANY)


def body(
    tokens,
    cotangent,
    attn_gain,
    q_weight,
    k_weight,
    v_weight,
    o_weight,
    ffn_gain,
    gate_weight,
    up_weight,
    down_weight,
):
    fsdp_size, cp_size = lax.axis_size("fsdp"), lax.axis_size("cp")
    devices = fsdp_size * cp_size
    teams, row_count, width = tokens.shape
    team = cp_size // teams
    mirror = team + team // 2
    block_len = row_count // 2
    chunk = teams * row_count
    token_count = team * chunk
    f = lax.axis_index("fsdp")
    c = lax.axis_index("cp")
    side = c // team
    t = c % team ^ (team // 2 * side)
    q_width = HEADS // team * HEAD_DIM
    copies = team // KV_HEADS
    qkv_width = q_width + 2 * HEAD_DIM
    weight_rows = q_weight.shape[0]
    hidden_cols = gate_weight.shape[1] // team
    team_groups = [[k * team + i for i in range(team)] for k in range(teams)]

    def swap(value, mask):
        return lax.ppermute(value, BOTH, [(i, i ^ mask) for i in range(devices)])

    def turn(value):
        half = team // 2
        return jnp.where(side == 1, jnp.concatenate([value[half:], value[:half]], axis=0), value)

    def to_team(value):
        return turn(lax.all_to_all(turn(value), "cp", 0, 0, axis_index_groups=team_groups, tiled=True))

    def swap_blocks(blocks):
        blocks = jnp.where(f == 1, blocks[:, ::-1], blocks)
        return jnp.where(side == 1, blocks[:, :, ::-1], blocks)

    def turn_second(blocks):
        return jnp.concatenate([blocks[:, :, :1], blocks[:, :, 1:, ::-1]], axis=2)

    def reorder_rows(value):
        blocks = value.reshape(1, 2, 2, 2, width // 8, -1)
        return swap_blocks(turn_second(blocks)).reshape(value.shape)

    def restore(value):
        blocks = value.reshape(-1, 2, 2, 2, width // 8)
        return turn_second(swap_blocks(blocks)).reshape(value.shape)

    def give_rows(value):
        first, second = value[:row_count], value[row_count:]
        mine = jnp.where(side == 0, first, second)
        theirs = swap(jnp.where(side == 0, second, first), mirror)
        return jnp.stack([jnp.where(side == 0, mine, theirs), jnp.where(side == 0, theirs, mine)], axis=0)

    def team_gather(value):
        evens = jnp.concatenate([value] + [swap(value, m) for m in range(2, team, 2)], axis=0)
        return jnp.concatenate([evens, swap(evens, 1)], axis=0)

    def team_reduce(make):
        theirs = swap(make(1), 1)
        evens = (make(0).astype(F32) + theirs.astype(F32)).astype(BF16).reshape(team // 2, chunk, width)
        total = evens[0].astype(F32)
        for m in range(2, team, 2):
            total = total + swap(evens[m // 2], m).astype(F32)
        return total

    def scatter_small(value):
        for bit in reversed(range(devices.bit_length() - 1)):
            mask = 1 << bit
            index = (f * cp_size + c) & mask
            half = value.shape[-1] // 2
            low, high = value[..., :half], value[..., half:]
            theirs = swap(jnp.where(index == 0, high, low), mask)
            value = jnp.where(index == 0, low, high) + theirs
        return value

    def collect(value):
        cols = value.shape[-1]
        blocks = value.reshape(fsdp_size, teams, -1, cols)
        theirs = swap(blocks[1], cp_size)
        blocks = (blocks[0].astype(F32) + theirs.astype(F32)).astype(BF16)
        theirs = swap(blocks[1], mirror)
        own = (blocks[0].astype(F32) + theirs.astype(F32)).astype(BF16)
        return to_team(own.reshape(team, -1, cols))

    def cut(weight):
        return weight.reshape(weight_rows, team, -1).transpose(1, 0, 2)

    def join(pieces):
        return pieces.transpose(1, 0, 2).reshape(pieces.shape[1], -1).astype(F32)

    def repeat_heads(weight):
        heads = weight.reshape(weight_rows, KV_HEADS, HEAD_DIM)
        return jnp.repeat(heads, copies, axis=1).reshape(weight_rows, -1)

    def sum_heads(pieces):
        grouped = pieces.astype(F32).reshape(KV_HEADS, copies, -1, HEAD_DIM).sum(axis=1)
        return grouped.transpose(1, 0, 2).reshape(grouped.shape[1], -1)

    inverse = ROPE_BASE ** (-(2.0 * jnp.arange(HALF, dtype=F32)) / HEAD_DIM)
    angle = jnp.arange(token_count, dtype=jnp.int32).astype(F32)[:, None] * inverse[None, :]
    cosine, sine = jnp.cos(angle), jnp.sin(angle)
    turn_heads = q_width // HEAD_DIM + 1
    scale = HEAD_DIM ** (-0.5)
    scales = jnp.concatenate([jnp.full((q_width,), scale, F32), jnp.ones((HEAD_DIM,), F32)])
    cos_table = jnp.tile(jnp.concatenate([cosine, cosine], -1), (1, turn_heads)) * scales
    sin_table = jnp.tile(jnp.concatenate([-sine, sine], -1), (1, turn_heads)) * scales

    qkv_cut = jnp.concatenate([cut(q_weight), cut(repeat_heads(k_weight)), cut(repeat_heads(v_weight))], axis=-1)
    o_cut = cut(o_weight)
    gains_in = jnp.pad(jnp.stack([attn_gain, ffn_gain]), ((0, 14), (0, 128 - weight_rows)))

    def hbm(*shape):
        return jax.ShapeDtypeStruct(shape, BF16)

    out_shape = (
        jax.ShapeDtypeStruct((chunk, width), F32),
        jax.ShapeDtypeStruct((8, width), F32),
        hbm(team, chunk, width),
        hbm(4, team, weight_rows, qkv_width),
        hbm(q_width, width),
        hbm(token_count, qkv_width),
        hbm(team, chunk, q_width),
        jax.ShapeDtypeStruct((chunk, width), F32),
        hbm(team, chunk, width),
        hbm(team, chunk, width),
        hbm(4, team, weight_rows, hidden_cols),
        hbm(4, team, weight_rows, hidden_cols),
        hbm(4, team, weight_rows, hidden_cols),
        hbm(4, team, weight_rows, width // team),
    )
    relay_cols = (qkv_width, width // team, hidden_cols, hidden_cols, hidden_cols)
    relays = tuple(hbm(team, weight_rows, cols) for cols in relay_cols for _ in range(2))
    spaces = [vmem(), vmem(), anywhere(), anywhere(), vmem(), vmem(), vmem(), vmem()] + [anywhere()] * 16
    outs = pl.pallas_call(
        functools.partial(entry_kernel, fsdp_size, cp_size),
        out_shape=out_shape + relays,
        in_specs=[vmem(), vmem(), vmem()] + [anywhere()] * 5 + [vmem()] * 2,
        out_specs=tuple(spaces),
        scratch_shapes=[
            pltpu.SemaphoreType.DMA((10 * team + 48,)),
            pltpu.SemaphoreType.DMA((10 * team + 48,)),
            pltpu.SemaphoreType.DMA((16,)),
            pltpu.VMEM((row_count, width), BF16),
            pltpu.VMEM((row_count, width), BF16),
            pltpu.VMEM((devices, 16, 128), BF16),
            pltpu.VMEM((chunk, width), BF16),
            pltpu.VMEM((chunk, width), BF16),
            pltpu.VMEM((team, chunk, width), BF16),
            pltpu.VMEM((4, team, weight_rows, qkv_width), BF16),
            pltpu.VMEM((token_count, q_width), BF16),
            pltpu.VMEM((team, q_width // weight_rows, weight_rows, width // team), BF16),
            pltpu.VMEM((team // 2, chunk, width), BF16),
            pltpu.VMEM((team // 2 - 1, chunk, width), BF16),
        ],
        compiler_params=pltpu.CompilerParams(
            collective_id=0, has_side_effects=True, vmem_limit_bytes=VMEM_BYTES
        ),
        name="entry",
    )(tokens, cotangent, gains_in, qkv_cut, o_cut, gate_weight, up_weight, down_weight, cos_table, sin_table)
    x_float, gains, attn_in, qkv_team, o_team, rot, mix, resid, ffn_in, dy_team, gate_team, up_team, down_team = outs[:13]
    gain_one, gain_two = gains[0:1], gains[1:2]
    attn_in = attn_in.reshape(token_count, width)
    ffn_in = ffn_in.reshape(token_count, width)
    dy_low = dy_team[0]
    dy_team = dy_team.reshape(token_count, width)
    qkv_team = qkv_team.reshape(width, qkv_width)
    gate_team, up_team, down_team = (w.reshape(width, hidden_cols) for w in (gate_team, up_team, down_team))
    mix = mix.reshape(token_count, q_width)

    inv_one = lax.rsqrt(jnp.mean(x_float * x_float, axis=-1, keepdims=True) + NORM_EPS)
    normed_one = x_float * inv_one
    inv_two = lax.rsqrt(jnp.mean(resid * resid, axis=-1, keepdims=True) + NORM_EPS)
    normed_two = resid * inv_two

    gate = dot(ffn_in, gate_team)
    up_val = dot(ffn_in, up_team)
    sigma = jax.nn.sigmoid(gate)
    silu_val = gate * sigma
    hidden = (silu_val * up_val).astype(BF16)
    hidden_grad = dot(dy_team, down_team)
    gate_grad = (hidden_grad * up_val * (sigma + gate * sigma * (1.0 - sigma))).astype(BF16)
    up_grad = (hidden_grad * silu_val).astype(BF16)

    half = token_count // 2

    def half_of(value, odd):
        return value[half * odd : half * (odd + 1)]

    ffn_in_grad = team_reduce(
        lambda odd: (
            contract_cols(half_of(gate_grad, odd), gate_team) + contract_cols(half_of(up_grad, odd), up_team)
        ).astype(BF16)
    )
    down_sum = team_reduce(lambda odd: contract_cols(half_of(hidden, odd), down_team).astype(BF16))
    block_out = give_rows(restore((resid + down_sum).astype(BF16)))

    ffn_gain_grad = scatter_small(restore(jnp.sum(ffn_in_grad * normed_two, axis=0)))
    scaled_two = ffn_in_grad * gain_two
    resid_grad = dy_low.astype(F32) + inv_two * (
        scaled_two - normed_two * jnp.mean(scaled_two * normed_two, axis=-1, keepdims=True)
    )
    branch_grad = team_gather(resid_grad.astype(BF16))
    mix_grad = contract_cols(branch_grad, o_team).astype(BF16).reshape(team, chunk, q_width)

    down_weight_grad = join(collect(contract_rows(dy_team, hidden).astype(BF16)))
    gate_weight_grad = join(collect(contract_rows(ffn_in, gate_grad).astype(BF16)))
    up_weight_grad = join(collect(contract_rows(ffn_in, up_grad).astype(BF16)))

    proj_grad = pl.pallas_call(
        functools.partial(attention_backward, team, block_len, q_width),
        out_shape=jax.ShapeDtypeStruct((team, chunk, qkv_width), BF16),
        in_specs=[smem(), vmem(), vmem(), vmem(), vmem()],
        out_specs=vmem(),
        scratch_shapes=[
            pltpu.VMEM((token_count, q_width), BF16),
            pltpu.VMEM((token_count, q_width), F32),
            pltpu.VMEM((token_count, 2 * HEAD_DIM), F32),
        ],
        compiler_params=pltpu.CompilerParams(vmem_limit_bytes=VMEM_BYTES),
        name="attention_backward",
    )(t.astype(jnp.int32).reshape(1), rot, mix_grad, cos_table, sin_table).reshape(token_count, qkv_width)

    attn_in_grad = team_reduce(lambda odd: contract_cols(half_of(proj_grad, odd), qkv_team).astype(BF16))
    attn_gain_grad = scatter_small(restore(jnp.sum(attn_in_grad * normed_one, axis=0)))
    scaled_one = attn_in_grad * gain_one
    input_grad = resid_grad + inv_one * (
        scaled_one - normed_one * jnp.mean(scaled_one * normed_one, axis=-1, keepdims=True)
    )
    input_grad = give_rows(restore(input_grad.astype(BF16)))

    qkv_grad = collect(contract_rows(attn_in, proj_grad).astype(BF16))
    q_weight_grad = join(qkv_grad[:, :, :q_width])
    k_weight_grad = sum_heads(qkv_grad[:, :, q_width : q_width + HEAD_DIM])
    v_weight_grad = sum_heads(qkv_grad[:, :, q_width + HEAD_DIM :])

    o_grad = restore(contract_rows(mix, branch_grad)).astype(BF16)
    o_grad = to_team(o_grad.reshape(q_width, team, -1).transpose(1, 0, 2)).reshape(width, -1)
    o_weight_grad = join(collect(reorder_rows(o_grad)))

    return (
        block_out,
        input_grad,
        attn_gain_grad,
        q_weight_grad,
        k_weight_grad,
        v_weight_grad,
        o_weight_grad,
        ffn_gain_grad,
        gate_weight_grad,
        up_weight_grad,
        down_weight_grad,
    )


def solution(mesh):
    rows = P(BOTH, None)
    placed = P("fsdp", "cp", None)
    gain = P(BOTH)
    return jax.shard_map(
        body,
        mesh=mesh,
        in_specs=(placed, placed, gain, rows, rows, rows, rows, gain, rows, rows, rows),
        out_specs=(placed, placed, gain, rows, rows, rows, rows, gain, rows, rows, rows),
        check_vma=False,
    )
```

time: 938 us -> 869 us (0.926)
  Pallas kernels: 28 us -> 320 us
  waiting for transfers between devices: 482 us -> 202 us
  local copies, waits for them, and re-layouts: 103 us -> 68.6 us
  matrix products: 102 us -> 76.9 us
  other arithmetic: 77.2 us -> 54.8 us
  starting transfers between devices: 122 us -> 140 us
  between operations: 15.8 us -> 2.43 us
    ppermute x63 -> x38, waiting for transfers between devices: 480 us -> 188 us  [swap(): return lax.ppermute(value, BOTH, [(i, i ^ mask) for i in range(devices)])]
    pallas_call x1, Pallas kernels: 10.1 us -> 302 us  [body(): pl.pallas_call(functools.partial(entry_kernel, fsdp_size, cp_size), out_s...]
    ppermute x63 -> x38, starting transfers between devices: 75.8 us -> 112 us  [swap(): return lax.ppermute(value, BOTH, [(i, i ^ mask) for i in range(devices)])]
    all_to_all x10 -> x6, starting transfers between devices: 45.6 us -> 27.1 us  [to_team(): lax.all_to_all(turn(value), 'cp', 0, 0, axis_index_groups=team_groups, ti...]
    rev x6, local copies, waits for them, and re-layouts: 21 us -> 3.06 us  [turn_second(): return jnp.concatenate([blocks[:, :, :1], blocks[:, :, 1:, ::-1]], axis=2)]
    dot_general x5 -> x3, matrix products: 36.1 us -> 21.9 us  [dot(): return jnp.dot(left, right, preferred_element_type=F32)]
    all_to_all x10 -> x6, waiting for transfers between devices: 0.82 us -> 14.1 us  [to_team(): lax.all_to_all(turn(value), 'cp', 0, 0, axis_index_groups=team_groups, ti...]
    reshape x12 -> x6, local copies, waits for them, and re-layouts: 18.2 us -> 6.35 us  [the longest x4 3.71 us: restore(): blocks = value.reshape(-1, 2, 2, 2, width // 8)]
  transfers between devices with their start and end apart: 75 -> 44, of which waited for: 31 -> 23; matrix products, arithmetic and copies ran while one was open for 27% -> 16% of each run, Pallas kernels for 3% -> 0%
where the time goes in v2:
time: 869 us; the launch traced here: 865 us
  Pallas kernels  320 us (37%)
  waiting for transfers between devices  202 us (23%)
  starting transfers between devices  140 us (16%)
  matrix products  76.9 us (9%)
  local copies, waits for them, and re-layouts  68.6 us (8%)
  other arithmetic  54.8 us (6%)
    pallas_call x1, Pallas kernels, body(): pl.pallas_call(functools.partial(entry_kernel, fsdp_size, cp_size), out_s...  302 us
    ppermute x38, waiting for transfers between devices, swap(): return lax.ppermute(value, BOTH, [(i, i ^ mask) for i in range(devices)])  188 us
    ppermute x38, starting transfers between devices, swap(): return lax.ppermute(value, BOTH, [(i, i ^ mask) for i in range(devices)])  112 us
    dot_general x9, matrix products, contract_cols(): lax.dot_general(left, right, (((1,), (1,)), ((), ())), preferred_element_...  32.2 us
    all_to_all x6, starting transfers between devices, to_team(): lax.all_to_all(turn(value), 'cp', 0, 0, axis_index_groups=team_groups, ti...  27.1 us
    dot_general x5, matrix products, contract_rows(): lax.dot_general(left, right, (((0,), (0,)), ((), ())), preferred_element_...  22.8 us
    dot_general x3, matrix products, dot(): return jnp.dot(left, right, preferred_element_type=F32)  21.9 us
    pallas_call x1, Pallas kernels, body(): pl.pallas_call(functools.partial(attention_backward, team, block_len, q_w...  18.7 us
  transfers between devices with their start and end apart: 44, of which 23 were waited for; matrix products, arithmetic and copies ran while one was open for 16% of the time, Pallas kernels for 0%

profile of v2, /device:TPU:0, one launch (start us, length us, event | category | flops | bytes accessed | tf_op | source)
XLA Modules:
  0.0 864.5 jit_solution(15810840733220311278)
XLA Ops:
  14.5 301.7 %entry.1 = (f32[128,2048]{1,0:T(8,128)}, f32[8,2048]{1,0:T(8,128)}, bf16[8,128,2048]{2,1,0:T(8,128)(2,1)}, bf16[4,8,64,384]{3,2,1,0:T(8,128)(2,1)}, bf16[256,204...) custom-call(bf16[2,64,2048]{2,1,0:T(8,128)(2,1)} %tokens.1, ...), custom_call_target="tpu_custom_call" | custom-call | tf_op jit(solution)/shard_map/entry/pallas_call | solution.py:685
  316.3 8.1 fusion.64
  324.4 6.1 fusion.65
  330.5 7.7 multiply_convert_fusion
  338.2 3.7 convolution_convert_fusion.3
  341.9 4.8 convolution_convert_fusion
  349.1 4.8 convolution_convert_fusion.1
  357.7 5.0 convolution_convert_fusion.2
  368.8 3.7 add_convert_fusion.2
  372.8 4.4 fusion.12
  378.2 5.7 add_convert_fusion.4
  385.8 11.4 %collective-permute-done.36 = bf16[2,512,1024]{2,1,0:T(8,128)(2,1)} collective-permute-done((bf16[2,512,1024]{2,1,0:T(8,128)(2,1)}, bf16[2,512,1024]{2,1,0:T(8,128)(2,1)}, u32[]{:S(2)}, u32[]{:S(2)}) %collective-permute-start.36) | collective-permute-done | bytes 2097184 | tf_op jit(solution)/shard_map/ppermute | solution.py:575
  403.0 4.1 add_convert_fusion.1
  407.6 34.5 %collective-permute-done.34 = bf16[2,512,1024]{2,1,0:T(8,128)(2,1)} collective-permute-done((bf16[2,512,1024]{2,1,0:T(8,128)(2,1)}, bf16[2,512,1024]{2,1,0:T(8,128)(2,1)}, u32[]{:S(2)}, u32[]{:S(2)}) %collective-permute-start.34) | collective-permute-done | bytes 2097184 | tf_op jit(solution)/shard_map/ppermute | solution.py:575
  447.6 39.1 %collective-permute-done.32 = bf16[2,512,1024]{2,1,0:T(8,128)(2,1)} collective-permute-done((bf16[2,512,1024]{2,1,0:T(8,128)(2,1)}, bf16[2,512,1024]{2,1,0:T(8,128)(2,1)}, u32[]{:S(2)}, u32[]{:S(2)}) %collective-permute-start.32) | collective-permute-done | bytes 2097184 | tf_op jit(solution)/shard_map/ppermute | solution.py:575
  502.5 10.6 %collective-permute-done.7 = bf16[128,2048]{1,0:T(8,128)(2,1)S(1)} collective-permute-done((bf16[128,2048]{1,0:T(8,128)(2,1)S(1)}, bf16[128,2048]{1,0:T(8,128)(2,1)S(1)}, u32[]{:S(2)}, u32[]{:S(2)}) %collective-permute-start.7) | collective-permute-done | bytes 524320 | tf_op jit(solution)/shard_map/ppermute | solution.py:575
  519.9 3.6 constant_dynamic-update-slice_fusion.4
  526.4 69.9 %collective-permute-start.28 = (f32[512]{0:T(512)S(1)}, f32[512]{0:T(512)S(1)}, u32[]{:S(2)}, u32[]{:S(2)}) collective-permute-start(f32[512]{0:T(512)S(1)} %slice_select_fusion), channel_id=1, source_target_pairs={{0,8},{1,9},{2,10},{3,11},{4,12},{5,13},{6,14},{7,15},{8,0},{9,1},... | collective-permute-start | bytes 6152 | tf_op jit(solution)/shard_map/ppermute | solution.py:575
  597.8 34.5 %collective-permute-done.28 = f32[512]{0:T(512)S(1)} collective-permute-done((f32[512]{0:T(512)S(1)}, f32[512]{0:T(512)S(1)}, u32[]{:S(2)}, u32[]{:S(2)}) %collective-permute-start.28) | collective-permute-done | bytes 2080 | tf_op jit(solution)/shard_map/ppermute | solution.py:575
  641.1 4.4 collective-permute-done.29
  650.6 4.9 collective-permute-done.30
  661.1 3.6 all-to-all-start.4
  670.5 10.6 %collective-permute-done.9 = bf16[128,2048]{1,0:T(8,128)(2,1)S(1)} collective-permute-done((bf16[128,2048]{1,0:T(8,128)(2,1)}, bf16[128,2048]{1,0:T(8,128)(2,1)S(1)}, u32[]{:S(2)}, u32[]{:S(2)}) %collective-permute-start.9) | collective-permute-done | bytes 524320 | tf_op jit(solution)/shard_map/ppermute | solution.py:575
  699.0 5.3 all-to-all-done.3
  711.2 6.5 copy.127
  721.6 18.7 %attention_backward.1 = bf16[8,128,384]{2,1,0:T(8,128)(2,1)} custom-call(s32[1]{0:T(128)} %bitcast.17.where_ref, bf16[1024,384]{1,0:T(8,128)(2,1)} %get-tuple-element.32.rot_ref, bf16[8,128,256]{2,1,0:T(8,128)(2,1)} %bitcast.224, f32[1024,320]{1,0:T(8,128)} %get-tuple-element.125.cos_ref, f32[1024,320]{1,0:T(8,128)} %get-tuple-element.124.sin_ref), custom_call_target="tpu_custom_call" | custom-call | tf_op jit(solution)/shard_map/attention_backward/pallas_call | solution.py:760
  740.2 4.8 bitcast_convert_fusion
  748.0 3.7 all-to-all-start.1
  751.7 13.7 %collective-permute-done.23 = bf16[2,512,384]{2,1,0:T(8,128)(2,1)} collective-permute-done((bf16[2,512,384]{2,1,0:T(8,128)(2,1)}, bf16[2,512,384]{2,1,0:T(8,128)(2,1)}, u32[]{:S(2)}, u32[]{:S(2)}) %collective-permute-start.23) | collective-permute-done | bytes 786464 | tf_op jit(solution)/shard_map/ppermute | solution.py:575
  772.3 6.2 collective-permute-done.24
  779.5 9.2 %all-to-all-start = ((bf16[8,64,384]{2,1,0:T(8,128)(2,1)}), bf16[8,64,384]{2,1,0:T(8,128)(2,1)S(1)}, u32[]{:S(2)}, u32[]{:S(2)}) async-start(bf16[8,64,384]{2,1,0:T(8,128)(2,1)} %maximum_select_fusion.8), calls=%async_computation | async-start | bytes 786432 | tf_op jit(solution)/shard_map/all_to_all | solution.py:582
  817.2 10.2 %collective-permute-done.14 = bf16[128,2048]{1,0:T(8,128)(2,1)} collective-permute-done((bf16[128,2048]{1,0:T(8,128)(2,1)}, bf16[128,2048]{1,0:T(8,128)(2,1)}, u32[]{:S(2)}, u32[]{:S(2)}) %collective-permute-start.14) | collective-permute-done | bytes 524320 | tf_op jit(solution)/shard_map/ppermute | solution.py:575
  (301 shorter events, 197.0 us)
Async XLA Ops:
  341.9 36.3 %collective-permute-start = (bf16[512,2048]{1,0:T(8,128)(2,1)}, bf16[512,2048]{1,0:T(8,128)(2,1)}, u32[]{:S(2)}, u32[]{:S(2)}) collective-permute-start(bf16[512,2048]{1,0:T(8,128)(2,1)} %convolution_convert_fusion.3), channel_id=1, source_target_pairs={{0,1},{1,0},{2,3},{3,2},{4,5},{5,4},{6,7},{7,6},{8,9},{9,8},{10,11... | collective-permute-start | bytes 6291464 | tf_op jit(solution)/shard_map/ppermute | solution.py:575
  348.5 48.7 %collective-permute-start.36 = (bf16[2,512,1024]{2,1,0:T(8,128)(2,1)}, bf16[2,512,1024]{2,1,0:T(8,128)(2,1)}, u32[]{:S(2)}, u32[]{:S(2)}) collective-permute-start(bf16[2,512,1024]{2,1,0:T(8,128)(2,1)} %bitcast.69), channel_id=1, source_target_pairs={{0,16},{1,17},{2,18},{3,19},{4,20},{5,21},{6,22},{7,23},{8,24},{9,... | collective-permute-start | bytes 6291464 | tf_op jit(solution)/shard_map/ppermute | solution.py:575
  356.2 85.9 %collective-permute-start.34 = (bf16[2,512,1024]{2,1,0:T(8,128)(2,1)}, bf16[2,512,1024]{2,1,0:T(8,128)(2,1)}, u32[]{:S(2)}, u32[]{:S(2)}) collective-permute-start(bf16[2,512,1024]{2,1,0:T(8,128)(2,1)} %bitcast.61), channel_id=1, source_target_pairs={{0,16},{1,17},{2,18},{3,19},{4,20},{5,21},{6,22},{7,23},{8,24},{9,... | collective-permute-start | bytes 6291464 | tf_op jit(solution)/shard_map/ppermute | solution.py:575
  365.3 121.5 %collective-permute-start.32 = (bf16[2,512,1024]{2,1,0:T(8,128)(2,1)}, bf16[2,512,1024]{2,1,0:T(8,128)(2,1)}, u32[]{:S(2)}, u32[]{:S(2)}) collective-permute-start(bf16[2,512,1024]{2,1,0:T(8,128)(2,1)} %bitcast.53), channel_id=1, source_target_pairs={{0,16},{1,17},{2,18},{3,19},{4,20},{5,21},{6,22},{7,23},{8,24},{9,... | collective-permute-start | bytes 6291464 | tf_op jit(solution)/shard_map/ppermute | solution.py:575
  372.5 27.3 %collective-permute-start.5 = (bf16[512,2048]{1,0:T(8,128)(2,1)}, bf16[512,2048]{1,0:T(8,128)(2,1)}, u32[]{:S(2)}, u32[]{:S(2)}) collective-permute-start(bf16[512,2048]{1,0:T(8,128)(2,1)} %add_convert_fusion.2), channel_id=1, source_target_pairs={{0,1},{1,0},{2,3},{3,2},{4,5},{5,4},{6,7},{7,6},{8,9},{9,8},{10,11... | collective-permute-start | bytes 6291464 | tf_op jit(solution)/shard_map/ppermute | solution.py:575
  384.1 105.2 %collective-permute-start.1 = (bf16[128,2048]{1,0:T(8,128)(2,1)S(1)}, bf16[128,2048]{1,0:T(8,128)(2,1)S(1)}, u32[]{:S(2)}, u32[]{:S(2)}) collective-permute-start(bf16[128,2048]{1,0:T(8,128)(2,1)S(1)} %get-tuple-element.63), channel_id=1, source_target_pairs={{0,2},{1,3},{2,0},{3,1},{4,6},{5,7},{6,4},{7,5},{8,10},{9,11},{10,... | collective-permute-start | bytes 1572872 | tf_op jit(solution)/shard_map/ppermute | solution.py:575
  397.2 97.4 %collective-permute-start.3 = (bf16[128,2048]{1,0:T(8,128)(2,1)S(1)}, bf16[128,2048]{1,0:T(8,128)(2,1)S(1)}, u32[]{:S(2)}, u32[]{:S(2)}) collective-permute-start(bf16[128,2048]{1,0:T(8,128)(2,1)S(1)} %get-tuple-element.64), channel_id=1, source_target_pairs={{0,6},{1,7},{2,4},{3,5},{4,2},{5,3},{6,0},{7,1},{8,14},{9,15},{10,... | collective-permute-start | bytes 1572872 | tf_op jit(solution)/shard_map/ppermute | solution.py:575
  399.8 98.3 %collective-permute-start.2 = (bf16[128,2048]{1,0:T(8,128)(2,1)S(1)}, bf16[128,2048]{1,0:T(8,128)(2,1)S(1)}, u32[]{:S(2)}, u32[]{:S(2)}) collective-permute-start(bf16[128,2048]{1,0:T(8,128)(2,1)S(1)} %get-tuple-element.65), channel_id=1, source_target_pairs={{0,4},{1,5},{2,6},{3,7},{4,0},{5,1},{6,2},{7,3},{8,12},{9,13},{10,... | collective-permute-start | bytes 1572872 | tf_op jit(solution)/shard_map/ppermute | solution.py:575
  442.2 56.3 %collective-permute-start.6 = (bf16[128,2048]{1,0:T(8,128)(2,1)S(1)}, bf16[128,2048]{1,0:T(8,128)(2,1)S(1)}, u32[]{:S(2)}, u32[]{:S(2)}) collective-permute-start(bf16[128,2048]{1,0:T(8,128)(2,1)S(1)} %get-tuple-element.60), channel_id=1, source_target_pairs={{0,2},{1,3},{2,0},{3,1},{4,6},{5,7},{6,4},{7,5},{8,10},{9,11},{10,... | collective-permute-start | bytes 1572872 | tf_op jit(solution)/shard_map/ppermute | solution.py:575
  486.7 15.7 %collective-permute-start.8 = (bf16[128,2048]{1,0:T(8,128)(2,1)S(1)}, bf16[128,2048]{1,0:T(8,128)(2,1)S(1)}, u32[]{:S(2)}, u32[]{:S(2)}) collective-permute-start(bf16[128,2048]{1,0:T(8,128)(2,1)S(1)} %get-tuple-element.61), channel_id=1, source_target_pairs={{0,6},{1,7},{2,4},{3,5},{4,2},{5,3},{6,0},{7,1},{8,14},{9,15},{10,... | collective-permute-start | bytes 1572872 | tf_op jit(solution)/shard_map/ppermute | solution.py:575
  489.3 23.7 %collective-permute-start.7 = (bf16[128,2048]{1,0:T(8,128)(2,1)S(1)}, bf16[128,2048]{1,0:T(8,128)(2,1)S(1)}, u32[]{:S(2)}, u32[]{:S(2)}) collective-permute-start(bf16[128,2048]{1,0:T(8,128)(2,1)S(1)} %get-tuple-element.62), channel_id=1, source_target_pairs={{0,4},{1,5},{2,6},{3,7},{4,0},{5,1},{6,2},{7,3},{8,12},{9,13},{10,... | collective-permute-start | bytes 1572872 | tf_op jit(solution)/shard_map/ppermute | solution.py:575
  494.7 137.6 %collective-permute-start.37 = (bf16[512,1024]{1,0:T(8,128)(2,1)}, bf16[512,1024]{1,0:T(8,128)(2,1)}, u32[]{:S(2)}, u32[]{:S(2)}) collective-permute-start(bf16[512,1024]{1,0:T(8,128)(2,1)} %slice_bitcast_fusion), channel_id=1, source_target_pairs={{0,12},{1,13},{2,14},{3,15},{4,8},{5,9},{6,10},{7,11},{8,4},{9,5},... | collective-permute-start | bytes 3145736 | tf_op jit(solution)/shard_map/ppermute | solution.py:575
  498.2 159.5 %collective-permute-start.35 = (bf16[512,1024]{1,0:T(8,128)(2,1)}, bf16[512,1024]{1,0:T(8,128)(2,1)}, u32[]{:S(2)}, u32[]{:S(2)}) collective-permute-start(bf16[512,1024]{1,0:T(8,128)(2,1)} %slice_bitcast_fusion.2), channel_id=1, source_target_pairs={{0,12},{1,13},{2,14},{3,15},{4,8},{5,9},{6,10},{7,11},{8,4},{9,5},... | collective-permute-start | bytes 3145736 | tf_op jit(solution)/shard_map/ppermute | solution.py:575
  498.5 168.8 %collective-permute-start.33 = (bf16[512,1024]{1,0:T(8,128)(2,1)}, bf16[512,1024]{1,0:T(8,128)(2,1)}, u32[]{:S(2)}, u32[]{:S(2)}) collective-permute-start(bf16[512,1024]{1,0:T(8,128)(2,1)} %slice_bitcast_fusion.4), channel_id=1, source_target_pairs={{0,12},{1,13},{2,14},{3,15},{4,8},{5,9},{6,10},{7,11},{8,4},{9,5},... | collective-permute-start | bytes 3145736 | tf_op jit(solution)/shard_map/ppermute | solution.py:575
  525.3 145.1 %collective-permute-start.11 = (bf16[128,2048]{1,0:T(8,128)(2,1)}, bf16[128,2048]{1,0:T(8,128)(2,1)}, u32[]{:S(2)}, u32[]{:S(2)}) collective-permute-start(bf16[128,2048]{1,0:T(8,128)(2,1)} %get-tuple-element.44), channel_id=1, source_target_pairs={{0,6},{1,7},{2,4},{3,5},{4,2},{5,3},{6,0},{7,1},{8,14},{9,15},{10,... | collective-permute-start | bytes 1572872 | tf_op jit(solution)/shard_map/ppermute | solution.py:575
  526.4 105.9 %collective-permute-start.28 = (f32[512]{0:T(512)S(1)}, f32[512]{0:T(512)S(1)}, u32[]{:S(2)}, u32[]{:S(2)}) collective-permute-start(f32[512]{0:T(512)S(1)} %slice_select_fusion), channel_id=1, source_target_pairs={{0,8},{1,9},{2,10},{3,11},{4,12},{5,13},{6,14},{7,15},{8,0},{9,1},... | collective-permute-start | bytes 6152 | tf_op jit(solution)/shard_map/ppermute | solution.py:575
  632.3 38.2 %collective-permute-start.10 = (bf16[128,2048]{1,0:T(8,128)(2,1)}, bf16[128,2048]{1,0:T(8,128)(2,1)}, u32[]{:S(2)}, u32[]{:S(2)}) collective-permute-start(bf16[128,2048]{1,0:T(8,128)(2,1)} %get-tuple-element.44), channel_id=1, source_target_pairs={{0,4},{1,5},{2,6},{3,7},{4,0},{5,1},{6,2},{7,3},{8,12},{9,13},{10,... | collective-permute-start | bytes 1572872 | tf_op jit(solution)/shard_map/ppermute | solution.py:575
  632.3 13.2 %collective-permute-start.29 = (f32[256]{0:T(256)S(1)}, f32[256]{0:T(256)S(1)}, u32[]{:S(2)}, u32[]{:S(2)}) collective-permute-start(f32[256]{0:T(256)S(1)} %broadcast_select_fusion.8), channel_id=1, source_target_pairs={{0,4},{1,5},{2,6},{3,7},{4,0},{5,1},{6,2},{7,3},{8,12},{9,13},{10,... | collective-permute-start | bytes 3080 | tf_op jit(solution)/shard_map/ppermute | solution.py:575
  637.5 23.6 %all-to-all-start.5 = ((bf16[8,64,1024]{2,1,0:T(8,128)(2,1)}), bf16[8,64,1024]{2,1,0:T(8,128)(2,1)S(1)}, u32[]{:S(2)}, u32[]{:S(2)}) async-start(bf16[8,64,1024]{2,1,0:T(8,128)(2,1)} %maximum_select_fusion.6), calls=%async_computation.5 | async-start | bytes 2097152 | tf_op jit(solution)/shard_map/all_to_all | solution.py:582
  660.5 20.5 %collective-permute-start.9 = (bf16[128,2048]{1,0:T(8,128)(2,1)}, bf16[128,2048]{1,0:T(8,128)(2,1)S(1)}, u32[]{:S(2)}, u32[]{:S(2)}) collective-permute-start(bf16[128,2048]{1,0:T(8,128)(2,1)} %get-tuple-element.44), channel_id=1, source_target_pairs={{0,2},{1,3},{2,0},{3,1},{4,6},{5,7},{6,4},{7,5},{8,10},{9,11},{10,... | collective-permute-start | bytes 1572872 | tf_op jit(solution)/shard_map/ppermute | solution.py:575
  661.1 25.2 %all-to-all-start.4 = ((bf16[8,64,1024]{2,1,0:T(8,128)(2,1)}), bf16[8,64,1024]{2,1,0:T(8,128)(2,1)S(1)}, u32[]{:S(2)}, u32[]{:S(2)}) async-start(bf16[8,64,1024]{2,1,0:T(8,128)(2,1)} %maximum_select_fusion.4), calls=%async_computation.4 | async-start | bytes 2097152 | tf_op jit(solution)/shard_map/all_to_all | solution.py:582
  684.2 21.8 %collective-permute-start.12 = (bf16[512,2048]{1,0:T(8,128)(2,1)}, bf16[512,2048]{1,0:T(8,128)(2,1)}, u32[]{:S(2)}, u32[]{:S(2)}) collective-permute-start(bf16[512,2048]{1,0:T(8,128)(2,1)} %pad_maximum_fusion), channel_id=1, source_target_pairs={{0,1},{1,0},{2,3},{3,2},{4,5},{5,4},{6,7},{7,6},{8,9},{9,8},{10,11... | collective-permute-start | bytes 6291464 | tf_op jit(solution)/shard_map/ppermute | solution.py:575
  686.3 17.9 %all-to-all-start.3 = ((bf16[8,64,1024]{2,1,0:T(8,128)(2,1)}), bf16[8,64,1024]{2,1,0:T(8,128)(2,1)S(1)}, u32[]{:S(2)}, u32[]{:S(2)}) async-start(bf16[8,64,1024]{2,1,0:T(8,128)(2,1)} %maximum_select_fusion.2), calls=%async_computation.3 | async-start | bytes 2097152 | tf_op jit(solution)/shard_map/all_to_all | solution.py:582
  746.0 19.4 %collective-permute-start.23 = (bf16[2,512,384]{2,1,0:T(8,128)(2,1)}, bf16[2,512,384]{2,1,0:T(8,128)(2,1)}, u32[]{:S(2)}, u32[]{:S(2)}) collective-permute-start(bf16[2,512,384]{2,1,0:T(8,128)(2,1)} %bitcast.27), channel_id=1, source_target_pairs={{0,16},{1,17},{2,18},{3,19},{4,20},{5,21},{6,22},{7,23},{8,24},{9,... | collective-permute-start | bytes 2359304 | tf_op jit(solution)/shard_map/ppermute | solution.py:575
  748.0 31.4 %all-to-all-start.1 = ((bf16[8,256,256]{2,1,0:T(8,128)(2,1)}), bf16[8,256,256]{2,1,0:T(8,128)(2,1)S(1)}, u32[]{:S(2)}, u32[]{:S(2)}) async-start(bf16[8,256,256]{2,1,0:T(8,128)(2,1)} %maximum_select_fusion), calls=%async_computation.1 | async-start | bytes 2097152 | tf_op jit(solution)/shard_map/all_to_all | solution.py:582
  772.3 24.0 %collective-permute-start.13 = (bf16[512,2048]{1,0:T(8,128)(2,1)}, bf16[512,2048]{1,0:T(8,128)(2,1)S(1)}, u32[]{:S(2)}, u32[]{:S(2)}) collective-permute-start(bf16[512,2048]{1,0:T(8,128)(2,1)} %convolution_convert_fusion.5), channel_id=1, source_target_pairs={{0,1},{1,0},{2,3},{3,2},{4,5},{5,4},{6,7},{7,6},{8,9},{9,8},{10,11... | collective-permute-start | bytes 6291464 | tf_op jit(solution)/shard_map/ppermute | solution.py:575
  779.5 16.7 %all-to-all-start = ((bf16[8,64,384]{2,1,0:T(8,128)(2,1)}), bf16[8,64,384]{2,1,0:T(8,128)(2,1)S(1)}, u32[]{:S(2)}, u32[]{:S(2)}) async-start(bf16[8,64,384]{2,1,0:T(8,128)(2,1)} %maximum_select_fusion.8), calls=%async_computation | async-start | bytes 786432 | tf_op jit(solution)/shard_map/all_to_all | solution.py:582
  792.4 19.6 %collective-permute-start.25 = (bf16[2,512,256]{2,1,0:T(8,128)(2,1)}, bf16[2,512,256]{2,1,0:T(8,128)(2,1)}, u32[]{:S(2)}, u32[]{:S(2)}) collective-permute-start(bf16[2,512,256]{2,1,0:T(8,128)(2,1)} %bitcast.45), channel_id=1, source_target_pairs={{0,16},{1,17},{2,18},{3,19},{4,20},{5,21},{6,22},{7,23},{8,24},{9,... | collective-permute-start | bytes 1572872 | tf_op jit(solution)/shard_map/ppermute | solution.py:575
  802.4 25.0 %collective-permute-start.14 = (bf16[128,2048]{1,0:T(8,128)(2,1)}, bf16[128,2048]{1,0:T(8,128)(2,1)}, u32[]{:S(2)}, u32[]{:S(2)}) collective-permute-start(bf16[128,2048]{1,0:T(8,128)(2,1)} %get-tuple-element.57), channel_id=1, source_target_pairs={{0,2},{1,3},{2,0},{3,1},{4,6},{5,7},{6,4},{7,5},{8,10},{9,11},{10,... | collective-permute-start | bytes 1572872 | tf_op jit(solution)/shard_map/ppermute | solution.py:575
  803.9 23.6 %collective-permute-start.16 = (bf16[128,2048]{1,0:T(8,128)(2,1)}, bf16[128,2048]{1,0:T(8,128)(2,1)}, u32[]{:S(2)}, u32[]{:S(2)}) collective-permute-start(bf16[128,2048]{1,0:T(8,128)(2,1)} %get-tuple-element.58), channel_id=1, source_target_pairs={{0,6},{1,7},{2,4},{3,5},{4,2},{5,3},{6,0},{7,1},{8,14},{9,15},{10,... | collective-permute-start | bytes 1572872 | tf_op jit(solution)/shard_map/ppermute | solution.py:575
  805.3 24.0 %collective-permute-start.15 = (bf16[128,2048]{1,0:T(8,128)(2,1)}, bf16[128,2048]{1,0:T(8,128)(2,1)}, u32[]{:S(2)}, u32[]{:S(2)}) collective-permute-start(bf16[128,2048]{1,0:T(8,128)(2,1)} %get-tuple-element.59), channel_id=1, source_target_pairs={{0,4},{1,5},{2,6},{3,7},{4,0},{5,1},{6,2},{7,3},{8,12},{9,13},{10,... | collective-permute-start | bytes 1572872 | tf_op jit(solution)/shard_map/ppermute | solution.py:575
  814.9 23.0 %collective-permute-start.26 = (bf16[512,256]{1,0:T(8,128)(2,1)}, bf16[512,256]{1,0:T(8,128)(2,1)S(1)}, u32[]{:S(2)}, u32[]{:S(2)}) collective-permute-start(bf16[512,256]{1,0:T(8,128)(2,1)} %slice_bitcast_fusion.8), channel_id=1, source_target_pairs={{0,12},{1,13},{2,14},{3,15},{4,8},{5,9},{6,10},{7,11},{8,4},{9,5},... | collective-permute-start | bytes 786440 | tf_op jit(solution)/shard_map/ppermute | solution.py:575
  (46 other events, 712.3 us)

commit v3 on v2

--- a/solution.py
+++ b/solution.py
@@ -66,9 +66,9 @@
     return jnp.concatenate(pieces, axis=-1)
 
 
-def over_row_blocks(token_count, step):
+def over_row_blocks(token_count, most, step):
     quarter = token_count // 4
-    rows = min(256, (1 << 18) // token_count)
+    rows = min(most, (1 << 18) // token_count)
     for first in range(0, token_count, quarter):
         if rows == quarter:
             step(first, first + quarter, first, rows)
@@ -79,6 +79,16 @@
                 return carry
 
             lax.fori_loop(0, quarter // rows, block, 0)
+
+
+def turn_by(wide, cosine, sine):
+    swapped = swap_halves(wide)
+    pieces = []
+    for start in range(0, wide.shape[-1], 2 * HEAD_DIM):
+        piece = slice(start, start + 2 * HEAD_DIM)
+        span = wide[:, piece].shape[-1]
+        pieces.append(wide[:, piece] * cosine[:, :span] + swapped[:, piece] * sine[:, :span])
+    return jnp.concatenate(pieces, axis=-1)
 
 
 def masked_scores(query, keys, first, start):
@@ -134,44 +144,119 @@
 
 class TeamGather:
     def __init__(self, links, team, src, dst):
-        self.evens = range(2, team, 2)
-        self.dst, self.team = dst, team
-        self.sends = [links.copy(src, dst.at[spot_of(m, team)], m) for m in self.evens]
-        self.passes = [links.copy(src, dst.at[spot_of(1, team)], 1)]
-        for m in self.evens:
-            self.passes.append(links.copy(dst.at[spot_of(m, team)], dst.at[spot_of(m + 1, team)], 1))
+        near = team // 2
+        row = range(2, near, 2)
+
+        def place(mask):
+            return dst.at[spot_of(mask, team)]
+
+        self.to_near = links.copy(src, place(near), near)
+        self.to_row = [links.copy(src, place(m), m) for m in row]
+        self.on = [links.copy(place(near), place(near + m), m) for m in row]
+        self.to_core = links.copy(src, place(1), 1)
+        self.near_core = links.copy(place(near), place(near + 1), 1)
+        self.row_core = [links.copy(place(m), place(m + 1), 1) for m in row]
+        self.on_core = [links.copy(place(near + m), place(near + m + 1), 1) for m in row]
         self.own = links.inside(src, dst.at[0])
 
     def start(self):
-        for send in self.sends:
-            send.start()
-        self.passes[0].start()
+        self.to_near.start()
+        for copy in self.to_row:
+            copy.start()
+        self.to_core.start()
         self.own.start()
 
-    def forward(self, index):
-        self.sends[index].wait_recv()
-        self.passes[index + 1].start()
+    def pass_near(self):
+        self.to_near.wait_recv()
+        for copy in self.on:
+            copy.start()
+        self.near_core.start()
+
+    def pass_row(self):
+        for copy, core in zip(self.to_row, self.row_core):
+            copy.wait_recv()
+            core.start()
+
+    def pass_on(self):
+        for copy, core in zip(self.on, self.on_core):
+            copy.wait_recv()
+            core.start()
 
     def finish(self):
-        for passed in self.passes:
-            passed.wait_recv()
-        for send in self.sends + self.passes:
-            send.wait_send()
+        core = [self.to_core, self.near_core] + self.row_core + self.on_core
+        for copy in core:
+            copy.wait_recv()
+        for copy in [self.to_near] + self.to_row + self.on + core:
+            copy.wait_send()
         self.own.wait()
 
 
+class TeamSum:
+    def __init__(self, links, team, parts, taken, row_in, near_in):
+        self.team, self.parts, self.taken, self.row_in, self.near_in = team, parts, taken, row_in, near_in
+        near = team // 2
+        self.row = list(range(2, near, 2))
+        half = team // 2
+        self.cross = [links.copy(parts.at[half + e], taken.at[e], 1) for e in range(half)]
+        self.far = [links.copy(parts.at[(near + m) // 2], row_in.at[0, i], m) for i, m in enumerate(self.row)]
+        self.here = [links.copy(parts.at[m // 2], row_in.at[1, i], m) for i, m in enumerate(self.row)]
+        self.last = links.copy(parts.at[near // 2], near_in, near)
+
+    def start(self, make, near_sum, own_sum):
+        half, rows, width = self.taken.shape
+        pieces = [slice(start, start + 512) for start in range(0, width, 512)]
+        for low in range(half - 2, -1, -2):
+            for cols in pieces:
+                value = make(pl.ds((half + low) * rows, 2 * rows), cols).astype(BF16)
+                for k in range(2):
+                    self.parts[half + low + k, :, cols] = value[k * rows : (k + 1) * rows]
+            self.cross[low + 1].start()
+            self.cross[low].start()
+        for low in range(half - 2, -1, -2):
+            self.cross[low + 1].wait_recv()
+            self.cross[low].wait_recv()
+            for cols in pieces:
+                value = make(pl.ds(low * rows, 2 * rows), cols)
+                for k in range(2):
+                    spot = low + k
+                    part = value[k * rows : (k + 1) * rows] + self.taken[spot, :, cols].astype(F32)
+                    if spot == half // 2:
+                        near_sum[:, cols] = part
+                    elif spot == 0:
+                        own_sum[:, cols] = part
+                    else:
+                        self.parts[spot, :, cols] = part.astype(BF16)
+            for spot in (low + 1, low):
+                if spot > half // 2:
+                    self.far[spot - half // 2 - 1].start()
+                elif 0 < spot < half // 2:
+                    self.here[spot - 1].start()
+
+    def pass_near(self, value):
+        for index, copy in enumerate(self.far):
+            copy.wait_recv()
+            value = value + self.row_in[0, index].astype(F32)
+        self.parts[self.team // 4] = value.astype(BF16)
+        self.last.start()
+
+    def total(self, value):
+        for index, copy in enumerate(self.here):
+            copy.wait_recv()
+            value = value + self.row_in[1, index].astype(F32)
+        self.last.wait_recv()
+        return value + self.near_in[...].astype(F32)
+
+    def finish(self):
+        for copy in self.cross + self.far + self.here + [self.last]:
+            copy.wait_send()
+
+
 class Spread:
-    def __init__(self, links, team, t, inner, pieces, full, above, below):
-        self.inner, self.team = inner, team
-        near, mirror = team // 2, team + team // 2
-        across = links.cp_size
+    def __init__(self, links, team, t, pieces, full):
         self.own = links.inside(pieces(0), full.at[0, t])
         self.cuts = [links.copy(pieces(m), full.at[0, t], m) for m in range(1, team)]
-        self.far = [links.copy(full.at[0], full.at[2], across), links.copy(full.at[1], full.at[3], across)]
-        self.straight = links.copy(full.at[0], full.at[1], mirror)
-        self.up = links.copy(full.at[0], above, near)
-        self.over = links.copy(above, below, mirror)
-        self.down = links.copy(below, full.at[1], near)
+        self.far = [links.copy(full.at[b], full.at[b + 2], links.cp_size) for b in range(2)]
+        self.side = links.copy(full.at[0], full.at[1], team + team // 2)
 
     def cut(self):
         self.own.start()
@@ -183,49 +268,38 @@
         for piece in self.cuts:
             piece.wait_recv()
         self.far[0].start()
-
-        @pl.when(self.inner)
-        def _():
-            self.straight.start()
-
-        @pl.when(jnp.logical_not(self.inner))
-        def _():
-            self.up.start()
-
-    def relay(self):
-        @pl.when(self.inner)
-        def _():
-            self.up.wait_recv()
-            self.over.start()
+        self.side.start()
 
     def arrive(self):
-        @pl.when(self.inner)
-        def _():
-            self.straight.wait_recv()
-            self.far[1].start()
-            self.over.wait_recv()
-            self.down.start()
-
-        @pl.when(jnp.logical_not(self.inner))
-        def _():
-            self.down.wait_recv()
-            self.far[1].start()
+        self.side.wait_recv()
+        self.far[1].start()
 
     def finish(self):
         for copy in self.far:
             copy.wait_recv()
-        for copy in self.cuts + self.far:
+        for copy in self.cuts + self.far + [self.side]:
             copy.wait_send()
 
-        @pl.when(self.inner)
-        def _():
-            self.straight.wait_send()
-            self.over.wait_send()
-            self.down.wait_send()
-
-        @pl.when(jnp.logical_not(self.inner))
-        def _():
-            self.up.wait_send()
+
+class Collect:
+    def __init__(self, links, team, t, grad, far_in, side_in, final, out):
+        self.grad, self.far_in, self.side_in, self.final = grad, far_in, side_in, final
+        self.far = links.copy(grad.at[pl.ds(2, 2)], far_in, links.cp_size)
+        self.side = links.copy(grad.at[1], side_in, team + team // 2)
+        self.own = links.inside(final.at[t], out.at[t])
+        self.cuts = [links.copy(final.at[flip(t, m)], out.at[t], m) for m in range(1, team)]
+
+    def cut(self):
+        self.own.start()
+        for piece in self.cuts:
+            piece.start()
+
+    def finish(self):
+        self.own.wait()
+        self.far.wait_send()
+        self.side.wait_send()
+        for piece in self.cuts:
+            piece.wait()
 
 
 def entry_kernel(
@@ -255,17 +329,29 @@
     up_full,
     down_full,
     o_full,
-    *rest,
+    send,
+    recv,
+    local,
+    swapped,
+    dy_swapped,
+    slots,
+    chunk_ref,
+    dy_chunk,
+    acts,
+    wqkv,
+    mixed,
+    o_pieces,
+    taken,
+    row_in,
+    near_in,
+    near_sum,
 ):
-    relays, scratch = rest[:10], rest[10:]
-    (send, recv, local, swapped, dy_swapped, slots, chunk_ref, dy_chunk, acts, wqkv, mixed, o_pieces, taken, parts) = scratch
     links = Links(cp_size, send, recv, local)
     f, c = links.f, links.c
     team = cp_size // 2
     near, mirror = team // 2, team + team // 2
     side = c // team
     t = c % team + side * (flip(c, near) - c)
-    inner = t // near == 1
     row_count, width = tokens.shape[1], tokens.shape[2]
     block_len = row_count // 2
     unit = width // 8
@@ -287,14 +373,14 @@
     def columns_of(weight):
         return lambda m: weight.at[:, pl.ds(pl.multiple_of(flip(t, m) * cols, cols), cols)]
 
-    def spread(pieces, full, index):
-        return Spread(links, team, t, inner, pieces, full, relays[2 * index], relays[2 * index + 1])
-
-    qkv_spread = spread(lambda m: qkv_cut.at[flip(t, m)], qkv_full, 0)
-    o_spread = spread(lambda m: o_cut.at[flip(t, m)], o_full, 1)
-    gate_spread = spread(columns_of(gate_in), gate_full, 2)
-    up_spread = spread(columns_of(up_in), up_full, 3)
-    down_spread = spread(columns_of(down_in), down_full, 4)
+    def spread(pieces, full):
+        return Spread(links, team, t, pieces, full)
+
+    qkv_spread = spread(lambda m: qkv_cut.at[flip(t, m)], qkv_full)
+    o_spread = spread(lambda m: o_cut.at[flip(t, m)], o_full)
+    gate_spread = spread(columns_of(gate_in), gate_full)
+    up_spread = spread(columns_of(up_in), up_full)
+    down_spread = spread(columns_of(down_in), down_full)
 
     stages[0].start()
     qkv_spread.cut()
@@ -331,17 +417,15 @@
     dy_swap.start()
     qkv_spread.leave()
     o_spread.leave()
+    gather_one.pass_near()
+    gather_one.pass_row()
+    gate_spread.leave()
+    gather_one.pass_on()
     up_spread.cut()
     down_spread.cut()
-    for index in range(len(gather_one.sends) - 1):
-        gather_one.forward(index)
-    qkv_spread.relay()
-    o_spread.relay()
-    gather_one.forward(len(gather_one.sends) - 1)
-    gate_spread.leave()
     qkv_spread.arrive()
     o_spread.arrive()
-    gate_spread.relay()
+    up_spread.leave()
     qkv_spread.finish()
     load = links.inside(qkv_full, wqkv)
     load.start()
@@ -364,31 +448,29 @@
     o_own.start()
     for copy in o_sends:
         copy.start()
-    up_spread.leave()
 
     load.wait()
     weights = wqkv[...].reshape(width, wqkv.shape[-1])
 
     def project(m, carry):
         proj = dot(acts[spot_of(m, team)], weights)
-        qk = proj[:, : q_width + HEAD_DIM]
-        qk_swapped = swap_halves(qk)
+        keys = proj[:, q_width : q_width + HEAD_DIM]
+        qk = jnp.concatenate([proj[:, :q_width] * HEAD_DIM ** (-0.5), keys], axis=-1)
         blocks = chunk_blocks(differ(t, m, team), team)
         for slot in range(4):
             piece = slice(slot * block_len, (slot + 1) * block_len)
             rows = pl.ds(pl.multiple_of(blocks[slot] * block_len, block_len), block_len)
-            turned = qk[piece] * cos_ref[rows, :] + qk_swapped[piece] * sin_ref[rows, :]
+            turned = turn_by(qk[piece], cos_ref[rows, :], sin_ref[rows, :])
             rot_ref[rows, :] = jnp.concatenate([turned, proj[piece, q_width + HEAD_DIM :]], axis=-1).astype(BF16)
         return carry
 
     lax.fori_loop(0, team, project, 0)
-    gate_spread.arrive()
 
     dy_swap.wait_recv()
     fill(dy_chunk, cotangent, dy_swapped)
     gather_dy = TeamGather(links, team, dy_chunk, dy_ref)
     gather_dy.start()
-    up_spread.relay()
+    down_spread.leave()
 
     def attend(first, span, start, rows):
         keys = rot_ref[:span, q_width : q_width + HEAD_DIM]
@@ -403,8 +485,8 @@
             outs.append(dot(expo.astype(BF16), values) / total)
         mixed[pl.ds(start, rows), :] = jnp.concatenate(outs, axis=-1).astype(BF16)
 
-    over_row_blocks(token_count, attend)
-    gather_dy.forward(0)
+    over_row_blocks(token_count, 256, attend)
+    gather_dy.pass_near()
 
     def collect_mix(m, carry):
         blocks = chunk_blocks(differ(t, m, team), team)
@@ -425,40 +507,29 @@
             o_wide[:, start : start + span] = o_pieces[source].reshape(q_width, span)
 
     attn_out.wait()
-    half = team // 2
-    crossed = []
-    for spot in range(half, team):
-        acts[spot] = dot(mix_ref[spot], o_wide[...]).astype(BF16)
-        copy = links.copy(acts.at[spot], taken.at[spot - half], 1)
-        copy.start()
-        crossed.append(copy)
-    for index in range(1, len(gather_dy.sends)):
-        gather_dy.forward(index)
-    down_spread.leave()
-    given = []
-    for spot in list(range(1, half)) + [0]:
-        part = dot(mix_ref[spot], o_wide[...])
-        crossed[spot].wait_recv()
-        if spot:
-            acts[spot] = (part + taken[spot].astype(F32)).astype(BF16)
-            copy = links.copy(acts.at[spot], parts.at[spot - 1], 2 * spot)
-            copy.start()
-            given.append(copy)
-        else:
-            resid_ref[...] = x_ref[...] + part + taken[0].astype(F32)
-    up_spread.arrive()
-    down_spread.relay()
-    for index, copy in enumerate(given):
-        copy.wait_recv()
-        resid_ref[...] += parts[index].astype(F32)
+    summed = TeamSum(links, team, acts, taken, row_in, near_in)
+    row_pair = 2 * row_count
+    gather_dy.pass_row()
+
+    def mix_out(place, cols):
+        spots = pl.ds(place.start // row_pair, 2)
+        return dot(mix_ref[spots].reshape(2 * row_pair, q_width), o_wide[:, cols])
+
+    summed.start(mix_out, near_sum, resid_ref)
+    summed.pass_near(near_sum[...])
+    gather_dy.pass_on()
+    resid_ref[...] = x_ref[...] + summed.total(resid_ref[...])
     resid = resid_ref[...]
     inv_two = lax.rsqrt(jnp.mean(resid * resid, axis=-1, keepdims=True) + NORM_EPS)
     chunk_ref[...] = (resid * inv_two * gains_ref[1:2]).astype(BF16)
     gather_two = TeamGather(links, team, chunk_ref, ffn_in_ref)
     gather_two.start()
     gather_dy.finish()
-    for index in range(len(gather_two.sends)):
-        gather_two.forward(index)
+    gate_spread.arrive()
+    gather_two.pass_near()
+    gather_two.pass_row()
+    gather_two.pass_on()
+    up_spread.arrive()
     gate_spread.finish()
     down_spread.arrive()
     gather_two.finish()
@@ -466,26 +537,14 @@
     down_spread.finish()
     swap.wait_send()
     dy_swap.wait_send()
-    for copy in stages + o_sends + crossed + given:
+    summed.finish()
+    for copy in stages + o_sends:
         copy.wait_send()
 
 
-def attention_backward(
-    team, block_len, q_width, where_ref, rot_ref, grad_ref, cos_ref, sin_ref, out_ref, wide_ref, dq_ref, dkv_ref
-):
-    t = where_ref[0]
-    token_count = wide_ref.shape[0]
+def backward_heads(token_count, q_width, rot_ref, wide_ref, cos_ref, sin_ref, dq_ref, dkv_ref):
     heads = q_width // HEAD_DIM
     dkv_ref[...] = jnp.zeros_like(dkv_ref)
-
-    def place_grad(m, carry):
-        blocks = chunk_blocks(differ(t, m, team), team)
-        for slot in range(4):
-            where = pl.ds(pl.multiple_of(blocks[slot] * block_len, block_len), block_len)
-            wide_ref[where, :] = grad_ref[spot_of(m, team), slot * block_len : (slot + 1) * block_len, :]
-        return carry
-
-    lax.fori_loop(0, team, place_grad, 0)
 
     def attend(first, span, start, count):
         rows = pl.ds(start, count)
@@ -507,24 +566,471 @@
             dv = contract_rows(probs.astype(BF16), grad)
             dkv_ref[:span, :] += jnp.concatenate([dk, dv], axis=-1)
 
-    over_row_blocks(token_count, attend)
+    over_row_blocks(token_count, 128, attend)
 
     for start in range(0, token_count, token_count // 4):
         rows = slice(start, start + token_count // 4)
         qk = jnp.concatenate([dq_ref[rows, :], dkv_ref[rows, :HEAD_DIM]], axis=-1)
-        turned = qk * cos_ref[rows, :] - swap_halves(qk) * sin_ref[rows, :]
-        dq_ref[rows, :] = turned[:, :q_width]
+        turned = turn_by(qk, cos_ref[rows, :], -sin_ref[rows, :])
+        dq_ref[rows, :] = turned[:, :q_width] * HEAD_DIM ** (-0.5)
         dkv_ref[rows, :] = jnp.concatenate([turned[:, q_width:], dkv_ref[rows, HEAD_DIM:]], axis=-1)
 
+
+def scatter_chunk(t, m, team, block_len, wide_ref, value):
+    blocks = chunk_blocks(differ(t, m, team), team)
+    for slot in range(4):
+        where = pl.ds(pl.multiple_of(blocks[slot] * block_len, block_len), block_len)
+        wide_ref[where, :] = value[slot * block_len : (slot + 1) * block_len, :]
+
+
+def gather_chunk(t, m, team, block_len, out_ref, *sources):
+    blocks = chunk_blocks(differ(t, m, team), team)
+    for slot in range(4):
+        rows = pl.ds(pl.multiple_of(blocks[slot] * block_len, block_len), block_len)
+        place = pl.ds(pl.multiple_of((spot_of(m, team) * 4 + slot) * block_len, block_len), block_len)
+        piece = jnp.concatenate([source[rows, :] for source in sources], axis=-1)
+        out_ref[place, :] = piece.astype(BF16)
+
+
+def attention_backward(
+    team, block_len, q_width, where_ref, rot_ref, grad_ref, cos_ref, sin_ref, out_ref, wide_ref, dq_ref, dkv_ref
+):
+    t = where_ref[0]
+
+    def place_grad(m, carry):
+        scatter_chunk(t, m, team, block_len, wide_ref, grad_ref[spot_of(m, team)])
+        return carry
+
+    lax.fori_loop(0, team, place_grad, 0)
+    backward_heads(wide_ref.shape[0], q_width, rot_ref, wide_ref, cos_ref, sin_ref, dq_ref, dkv_ref)
+
     def give_chunk(m, carry):
-        blocks = chunk_blocks(differ(t, m, team), team)
-        for slot in range(4):
-            rows = pl.ds(pl.multiple_of(blocks[slot] * block_len, block_len), block_len)
-            piece = jnp.concatenate([dq_ref[rows, :], dkv_ref[rows, :]], axis=-1)
-            out_ref[spot_of(m, team), slot * block_len : (slot + 1) * block_len, :] = piece.astype(BF16)
+        gather_chunk(t, m, team, block_len, out_ref, dq_ref, dkv_ref)
         return carry
 
     lax.fori_loop(0, team, give_chunk, 0)
+
+
+def exit_kernel(
+    cp_size,
+    x_ref,
+    resid_ref,
+    gains_ref,
+    rot_ref,
+    mix_ref,
+    o_wide,
+    cos_ref,
+    sin_ref,
+    attn_in,
+    ffn_in,
+    dy,
+    gate_in,
+    up_in,
+    down_in,
+    qkv_in,
+    block_out,
+    input_grad,
+    gain_grads,
+    gate_out,
+    up_out,
+    down_out,
+    qkv_out,
+    o_out,
+    branch,
+    gate_grad,
+    gate_far,
+    gate_side,
+    gate_final,
+    up_grad,
+    up_far,
+    up_side,
+    up_final,
+    down_grad,
+    down_far,
+    down_side,
+    down_final,
+    qkv_grad,
+    qkv_far,
+    qkv_side,
+    qkv_final,
+    send,
+    recv,
+    local,
+    store_sem,
+    load_sem,
+    first,
+    second,
+    gate_w,
+    up_w,
+    down_w,
+    qkv_w,
+    parts,
+    hidden,
+    both,
+    stage_out,
+    stage_in,
+    taken_one,
+    row_one,
+    near_one,
+    taken_two,
+    row_two,
+    near_two,
+    resid_grad,
+    near_sum,
+    own_sum,
+    chunk_ref,
+    grad_rows,
+    wide,
+    dq_ref,
+    dkv_ref,
+    proj_grad,
+    o_far,
+    o_two,
+    o_side,
+    o_final,
+    gain_slots,
+    gain_in,
+):
+    links = Links(cp_size, send, recv, local)
+    f, c = links.f, links.c
+    team = cp_size // 2
+    near, mirror = team // 2, team + team // 2
+    side = c // team
+    t = c % team + side * (flip(c, near) - c)
+    mine = f * 2 + side
+    half = team // 2
+    token_count, width = first.shape
+    rows = token_count // team
+    row_count = rows // 2
+    block_len = row_count // 2
+    unit = width // 8
+    cols = hidden.shape[1]
+    q_width = wide.shape[1]
+    weight_rows = gate_grad.shape[2]
+
+    links.barrier(list(range(1, team)) + [mirror, cp_size])
+    loads = [
+        links.inside(source, target)
+        for source, target in (
+            (ffn_in, first),
+            (gate_in, gate_w),
+            (up_in, up_w),
+            (dy, second),
+            (down_in, down_w),
+            (qkv_in, qkv_w),
+        )
+    ]
+    for load in loads:
+        load.start()
+    for load in loads[:3]:
+        load.wait()
+
+    steps = token_count // 256
+
+    def forward(index, carry):
+        place = pl.ds(pl.multiple_of(index * 256, 256), 256)
+        spots = pl.ds(index * (256 // rows), 256 // rows)
+        block = first[place, :]
+        for start in range(0, cols, 256):
+            cut = slice(start, start + 256)
+            later = slice(cols + start, cols + start + 256)
+            gate = dot(block, gate_w[:, cut])
+            up_val = dot(block, up_w[:, cut])
+            sigma = jax.nn.sigmoid(gate)
+            silu_val = gate * sigma
+            hidden[place, cut] = (silu_val * up_val).astype(BF16)
+            factor = up_val * (sigma + silu_val * (1.0 - sigma))
+            parts[spots, :, cut] = silu_val.astype(BF16).reshape(256 // rows, rows, 256)
+            parts[spots, :, later] = factor.astype(BF16).reshape(256 // rows, rows, 256)
+        return carry
+
+    lax.fori_loop(0, steps, forward, 0)
+
+    def produce(left, right, widths, start, count, targets, adds):
+        def one(index, carry):
+            place = start + index
+            slot = index % 2
+            block, part = place // 2, pl.ds((place % 2) * half, half)
+            waits = []
+            for a, sources in enumerate(adds):
+                for k, source in enumerate(sources):
+                    load = pltpu.make_async_copy(
+                        source(block, part), stage_in.at[a, k, :, :, : widths[k]], load_sem.at[a, k]
+                    )
+                    load.start()
+                    waits.append(load)
+            stores = [
+                pltpu.make_async_copy(
+                    stage_out.at[slot, k, :, :, : widths[k]], target(block, part), store_sem.at[slot, k]
+                )
+                for k, target in enumerate(targets)
+            ]
+
+            @pl.when(index >= 2)
+            def _():
+                for store in stores:
+                    store.wait()
+
+            turned = left[:, pl.ds(pl.multiple_of(place * unit, unit), unit)].T
+            offset = 0
+            for k, span in enumerate(widths):
+                value = dot(turned, right[:, offset : offset + span]).reshape(half, weight_rows, span)
+                for a in range(len(adds)):
+                    waits[a * len(widths) + k].wait()
+                    value = value + stage_in[a, k, :, :, :span].astype(F32)
+                stage_out[slot, k, :, :, :span] = value.astype(BF16)
+                stores[k].start()
+                offset += span
+            return carry
+
+        lax.fori_loop(0, count, one, 0)
+        for index in range(max(0, count - 2), count):
+            for k, target in enumerate(targets):
+                pltpu.make_async_copy(
+                    stage_out.at[index % 2, k, :, :, : widths[k]], target(0, pl.ds(0, half)), store_sem.at[index % 2, k]
+                ).wait()
+
+    def in_block(ref):
+        return lambda block, part: ref.at[block, part]
+
+    def in_side(ref):
+        return lambda block, part: ref.at[part]
+
+    def give_far(left, right, widths, collects):
+        produce(left, right, widths, 4, 4, [in_block(k.grad) for k in collects], [])
+        for collect in collects:
+            collect.far.start()
+
+    def give_side(left, right, widths, collects):
+        for collect in collects:
+            collect.far.wait_recv()
+        produce(
+            left, right, widths, 2, 2, [in_block(k.grad) for k in collects], [[in_block(k.far_in) for k in collects]]
+        )
+        for collect in collects:
+            collect.side.start()
+
+    def give_final(left, right, widths, collects):
+        for collect in collects:
+            collect.side.wait_recv()
+        produce(
+            left,
+            right,
+            widths,
+            0,
+            2,
+            [in_side(k.final) for k in collects],
+            [[in_block(k.far_in) for k in collects], [in_side(k.side_in) for k in collects]],
+        )
+        for collect in collects:
+            collect.cut()
+
+    gate_sum = Collect(links, team, t, gate_grad, gate_far, gate_side, gate_final, gate_out)
+    up_sum = Collect(links, team, t, up_grad, up_far, up_side, up_final, up_out)
+    down_sum = Collect(links, team, t, down_grad, down_far, down_side, down_final, down_out)
+    qkv_sum = Collect(links, team, t, qkv_grad, qkv_far, qkv_side, qkv_final, qkv_out)
+
+    loads[3].wait()
+    give_far(second, hidden, [cols], [down_sum])
+    loads[4].wait()
+
+    def backward(index, carry):
+        place = pl.ds(pl.multiple_of(index * 256, 256), 256)
+        spots = pl.ds(index * (256 // rows), 256 // rows)
+        block = second[place, :]
+        for start in range(0, cols, 256):
+            cut = slice(start, start + 256)
+            later = slice(cols + start, cols + start + 256)
+            hidden_grad = dot(block, down_w[:, cut])
+            silu_val = parts[spots, :, cut].reshape(256, 256).astype(F32)
+            factor = parts[spots, :, later].reshape(256, 256).astype(F32)
+            both[place, cut] = (hidden_grad * factor).astype(BF16)
+            both[place, later] = (hidden_grad * silu_val).astype(BF16)
+        return carry
+
+    lax.fori_loop(0, steps, backward, 0)
+
+    def team_sum(taken, row_in, near_in, make):
+        summed = TeamSum(links, team, parts, taken, row_in, near_in)
+        summed.start(make, near_sum, own_sum)
+        return summed
+
+    def finish_sum(summed):
+        summed.pass_near(near_sum[...])
+        value = summed.total(own_sum[...])
+        summed.finish()
+        return value
+
+    ffn_sum = team_sum(
+        taken_one,
+        row_one,
+        near_one,
+        lambda place, cut: contract_cols(both[place, :cols], gate_w[cut, :]) + contract_cols(both[place, cols:], up_w[cut, :]),
+    )
+    ffn_sum.pass_near(near_sum[...])
+    give_far(first, both, [cols, cols], [gate_sum, up_sum])
+    ffn_in_grad = ffn_sum.total(own_sum[...])
+    ffn_sum.finish()
+
+    def place_gain(row, value):
+        share = width // (4 * team)
+        for b in range(4):
+            for member in range(team):
+                start = (b * team + member) * share
+                gain_slots[b * team + flip(t, member), row : row + 1, :share] = value[:, start : start + share]
+
+    gain_slots[...] = jnp.zeros_like(gain_slots)
+    resid = resid_ref[...]
+    inv_two = lax.rsqrt(jnp.mean(resid * resid, axis=-1, keepdims=True) + NORM_EPS)
+    normed = resid * inv_two
+    place_gain(1, jnp.sum(ffn_in_grad * normed, axis=0, keepdims=True))
+    scaled = ffn_in_grad * gains_ref[1:2]
+    value = second[:rows, :].astype(F32) + inv_two * (
+        scaled - normed * jnp.mean(scaled * normed, axis=-1, keepdims=True)
+    )
+    resid_grad[...] = value
+    chunk_ref[...] = value.astype(BF16)
+    gather = TeamGather(links, team, chunk_ref, branch)
+    gather.start()
+    give_side(second, hidden, [cols], [down_sum])
+    gather.pass_near()
+    gather.pass_row()
+    gather.pass_on()
+    gather.finish()
+    load = links.inside(branch, parts)
+    load.start()
+    load.wait()
+
+    for low in range(0, team, 2):
+        value = contract_cols(parts[low : low + 2].reshape(2 * rows, width), o_wide[...]).astype(BF16)
+        for spot in range(2):
+            m = 2 * (low + spot) if low + spot < half else 2 * (low + spot - half) + 1
+            scatter_chunk(t, m, team, block_len, wide, value[spot * rows : (spot + 1) * rows])
+
+    def head_rows(member):
+        return pl.ds(pl.multiple_of(member * q_width, q_width), q_width)
+
+    span = width // team
+    turned = mix_ref[...].reshape(token_count, q_width).T
+    for index in range(8):
+        value = dot(turned, parts[:, :, index * unit : (index + 1) * unit].reshape(token_count, unit)).astype(BF16)
+        for piece in range(team // 8):
+            target = natural_unit(mine, index) * (team // 8) + piece
+            gate_w[head_rows(target), span : 2 * span] = value[:, piece * span : (piece + 1) * span]
+    quarter = width // 4
+    o_place = gate_w.at[head_rows(t), pl.ds(0, span)]
+
+    def o_part(member):
+        return gate_w.at[head_rows(member), pl.ds(span, span)]
+
+    def o_land(block):
+        return gate_w[pl.ds(pl.multiple_of(block * quarter, quarter), quarter), :span].astype(F32)
+
+    o_own = links.inside(o_part(t), o_place)
+    o_sends = [links.copy(o_part(flip(t, m)), o_place, m) for m in range(1, team)]
+    o_own.start()
+    for copy in o_sends:
+        copy.start()
+
+    out_sum = team_sum(taken_two, row_two, near_two, lambda place, cut: contract_cols(hidden[place, :], down_w[cut, :]))
+    backward_heads(token_count, q_width, rot_ref, wide, cos_ref, sin_ref, dq_ref, dkv_ref)
+
+    def give_chunk(m, carry):
+        gather_chunk(t, m, team, block_len, proj_grad, dq_ref, dkv_ref)
+        return carry
+
+    lax.fori_loop(0, team, give_chunk, 0)
+
+    def give_rows(value, target, out):
+        for index in range(8):
+            natural = pl.ds(pl.multiple_of(natural_unit(mine, index) * unit, unit), unit)
+            target[:, natural] = value[:, index * unit : (index + 1) * unit].astype(BF16)
+        here = pl.ds(pl.multiple_of(side * row_count, row_count), row_count)
+        there = pl.ds(pl.multiple_of((1 - side) * row_count, row_count), row_count)
+        own = links.inside(target.at[here], out.at[side])
+        other = links.copy(target.at[there], out.at[side], mirror)
+        own.start()
+        other.start()
+        return own, other
+
+    out_copies = give_rows(resid_ref[...] + finish_sum(out_sum), chunk_ref, block_out)
+    qkv_width = q_width + 2 * HEAD_DIM
+    loads[5].wait()
+    attn_sum = team_sum(
+        taken_one,
+        row_one,
+        near_one,
+        lambda place, cut: contract_cols(proj_grad[place, :], qkv_w[cut, :]),
+    )
+    attn_load = links.inside(attn_in, second)
+    give_final(second, hidden, [cols], [down_sum])
+    attn_load.start()
+    for copy in o_sends:
+        copy.wait_recv()
+    o_own.wait()
+    other_half = pl.ds(pl.multiple_of((1 - f) * 2 * quarter, 2 * quarter), 2 * quarter)
+    o_across = links.copy(gate_w.at[other_half, pl.ds(0, span)], o_far, cp_size)
+    o_across.start()
+    give_side(first, both, [cols, cols], [gate_sum, up_sum])
+    attn_load.wait()
+    attn_in_grad = finish_sum(attn_sum)
+
+    x = x_ref[...]
+    inv_one = lax.rsqrt(jnp.mean(x * x, axis=-1, keepdims=True) + NORM_EPS)
+    normed = x * inv_one
+    place_gain(0, jnp.sum(attn_in_grad * normed, axis=0, keepdims=True))
+    size = 2 * team
+    gain_steps = []
+    for mask in [cp_size, mirror] + [1 << k for k in reversed(range(team.bit_length() - 1))]:
+        gain_steps.append(links.copy(gain_slots.at[pl.ds(size, size)], gain_in.at[pl.ds(size, size)], mask))
+        size //= 2
+    gain_steps[0].start()
+    scaled = attn_in_grad * gains_ref[0:1]
+    value = resid_grad[...] + inv_one * (scaled - normed * jnp.mean(scaled * normed, axis=-1, keepdims=True))
+    grad_copies = give_rows(value, grad_rows, input_grad)
+
+    give_far(second, proj_grad, [qkv_width], [qkv_sum])
+    o_across.wait_recv()
+
+    def o_came(block):
+        return o_far[pl.ds(pl.multiple_of(block * quarter, quarter), quarter), :].astype(F32)
+
+    o_two[...] = (o_land(f * 2 + 1 - side) + o_came(1 - side)).astype(BF16)
+    o_cross = links.copy(o_two, o_side, mirror)
+    o_cross.start()
+    size = 2 * team
+    for index, step in enumerate(gain_steps):
+        step.wait_recv()
+        gain_slots[:size] += gain_in[size : 2 * size]
+        size //= 2
+        if index + 1 < len(gain_steps):
+            gain_steps[index + 1].start()
+    gain_grads[...] = gain_slots[0]
+    give_side(second, proj_grad, [qkv_width], [qkv_sum])
+    o_cross.wait_recv()
+    o_final[...] = (o_land(f * 2 + side) + o_came(side) + o_side[...].astype(F32)).astype(BF16)
+
+    def o_rows(member):
+        place = member + side * (flip(member, near) - member)
+        return o_final.at[pl.ds(pl.multiple_of(place * weight_rows, weight_rows), weight_rows)]
+
+    o_last = links.inside(o_rows(t), o_out.at[t])
+    o_gives = [links.copy(o_rows(flip(t, m)), o_out.at[t], m) for m in range(1, team)]
+    o_last.start()
+    for copy in o_gives:
+        copy.start()
+    give_final(first, both, [cols, cols], [gate_sum, up_sum])
+    give_final(second, proj_grad, [qkv_width], [qkv_sum])
+    for own, other in (out_copies, grad_copies):
+        own.wait()
+        other.wait()
+    for copy in o_sends + [o_across, o_cross] + gain_steps:
+        copy.wait_send()
+    for copy in o_gives:
+        copy.wait()
+    o_last.wait()
+    for collect in (down_sum, gate_sum, up_sum, qkv_sum):
+        collect.finish()
 
 
 def vmem():
@@ -650,11 +1156,8 @@
     inverse = ROPE_BASE ** (-(2.0 * jnp.arange(HALF, dtype=F32)) / HEAD_DIM)
     angle = jnp.arange(token_count, dtype=jnp.int32).astype(F32)[:, None] * inverse[None, :]
     cosine, sine = jnp.cos(angle), jnp.sin(angle)
-    turn_heads = q_width // HEAD_DIM + 1
-    scale = HEAD_DIM ** (-0.5)
-    scales = jnp.concatenate([jnp.full((q_width,), scale, F32), jnp.ones((HEAD_DIM,), F32)])
-    cos_table = jnp.tile(jnp.concatenate([cosine, cosine], -1), (1, turn_heads)) * scales
-    sin_table = jnp.tile(jnp.concatenate([-sine, sine], -1), (1, turn_heads)) * scales
+    cos_table = jnp.concatenate([cosine] * 4, axis=-1)
+    sin_table = jnp.concatenate([-sine, sine] * 2, axis=-1)
 
     qkv_cut = jnp.concatenate([cut(q_weight), cut(repeat_heads(k_weight)), cut(repeat_heads(v_weight))], axis=-1)
     o_cut = cut(o_weight)
@@ -679,12 +1182,10 @@
         hbm(4, team, weight_rows, hidden_cols),
         hbm(4, team, weight_rows, width // team),
     )
-    relay_cols = (qkv_width, width // team, hidden_cols, hidden_cols, hidden_cols)
-    relays = tuple(hbm(team, weight_rows, cols) for cols in relay_cols for _ in range(2))
-    spaces = [vmem(), vmem(), anywhere(), anywhere(), vmem(), vmem(), vmem(), vmem()] + [anywhere()] * 16
+    spaces = [vmem(), vmem(), anywhere(), anywhere(), vmem(), vmem(), vmem(), vmem()] + [anywhere()] * 6
     outs = pl.pallas_call(
         functools.partial(entry_kernel, fsdp_size, cp_size),
-        out_shape=out_shape + relays,
+        out_shape=out_shape,
         in_specs=[vmem(), vmem(), vmem()] + [anywhere()] * 5 + [vmem()] * 2,
         out_specs=tuple(spaces),
         scratch_shapes=[
@@ -701,7 +1202,9 @@
             pltpu.VMEM((token_count, q_width), BF16),
             pltpu.VMEM((team, q_width // weight_rows, weight_rows, width // team), BF16),
             pltpu.VMEM((team // 2, chunk, width), BF16),
-            pltpu.VMEM((team // 2 - 1, chunk, width), BF16),
+            pltpu.VMEM((2, team // 4 - 1, chunk, width), BF16),
+            pltpu.VMEM((chunk, width), BF16),
+            pltpu.VMEM((chunk, width), F32),
         ],
         compiler_params=pltpu.CompilerParams(
             collective_id=0, has_side_effects=True, vmem_limit_bytes=VMEM_BYTES
@@ -718,6 +1221,110 @@
     gate_team, up_team, down_team = (w.reshape(width, hidden_cols) for w in (gate_team, up_team, down_team))
     mix = mix.reshape(token_count, q_width)
 
+    def f32(*shape):
+        return jax.ShapeDtypeStruct(shape, F32)
+
+    def buffers(cols):
+        part = (team, weight_rows, cols)
+        return hbm(4, *part), hbm(2, *part), hbm(*part), hbm(*part)
+
+    def scratch(*shape, dtype=BF16):
+        return pltpu.VMEM(shape, dtype)
+
+    if 2 * hidden_cols == width and KV_HEADS == team:
+        half = team // 2
+        span = width // team
+        sums = [scratch(half, chunk, width), scratch(2, team // 4 - 1, chunk, width), scratch(chunk, width)]
+        results = pl.pallas_call(
+            functools.partial(exit_kernel, cp_size),
+            out_shape=(
+                hbm(teams, row_count, width),
+                hbm(teams, row_count, width),
+                f32(8, 128),
+                hbm(team, weight_rows, hidden_cols),
+                hbm(team, weight_rows, hidden_cols),
+                hbm(team, weight_rows, hidden_cols),
+                hbm(team, weight_rows, qkv_width),
+                hbm(team, weight_rows, span),
+                hbm(team, chunk, width),
+                *buffers(hidden_cols),
+                *buffers(hidden_cols),
+                *buffers(hidden_cols),
+                *buffers(qkv_width),
+            ),
+            in_specs=[vmem()] * 8 + [anywhere()] * 7,
+            out_specs=tuple([anywhere()] * 2 + [vmem()] + [anywhere()] * 22),
+            scratch_shapes=[
+                pltpu.SemaphoreType.DMA((10 * team + 48,)),
+                pltpu.SemaphoreType.DMA((10 * team + 48,)),
+                pltpu.SemaphoreType.DMA((32,)),
+                pltpu.SemaphoreType.DMA((2, 2)),
+                pltpu.SemaphoreType.DMA((2, 2)),
+                scratch(token_count, width),
+                scratch(token_count, width),
+                scratch(width, hidden_cols),
+                scratch(width, hidden_cols),
+                scratch(width, hidden_cols),
+                scratch(width, qkv_width),
+                scratch(team, chunk, width),
+                scratch(token_count, hidden_cols),
+                scratch(token_count, 2 * hidden_cols),
+                scratch(2, 2, half, weight_rows, hidden_cols),
+                scratch(2, 2, half, weight_rows, hidden_cols),
+                *sums,
+                *sums,
+                scratch(chunk, width, dtype=F32),
+                scratch(chunk, width, dtype=F32),
+                scratch(chunk, width, dtype=F32),
+                scratch(chunk, width),
+                scratch(chunk, width),
+                scratch(token_count, q_width),
+                scratch(token_count, q_width, dtype=F32),
+                scratch(token_count, 2 * HEAD_DIM, dtype=F32),
+                scratch(token_count, qkv_width),
+                scratch(width // 2, span),
+                scratch(width // 4, span),
+                scratch(width // 4, span),
+                scratch(width // 4, span),
+                scratch(devices, 8, 128, dtype=F32),
+                scratch(devices, 8, 128, dtype=F32),
+            ],
+            compiler_params=pltpu.CompilerParams(
+                collective_id=1, has_side_effects=True, vmem_limit_bytes=63 << 20
+            ),
+            name="exit",
+        )(
+            x_float,
+            resid,
+            gains,
+            rot,
+            mix.reshape(team, chunk, q_width),
+            o_team,
+            cos_table,
+            sin_table,
+            attn_in,
+            ffn_in,
+            dy_team,
+            gate_team,
+            up_team,
+            down_team,
+            qkv_team,
+        )
+        block_out, input_grad, gain_grads, gate_parts, up_parts, down_parts, qkv_parts, o_parts = results[:8]
+        return (
+            block_out,
+            input_grad,
+            gain_grads[0, :weight_rows],
+            join(qkv_parts[:, :, :q_width]),
+            sum_heads(qkv_parts[:, :, q_width : q_width + HEAD_DIM]),
+            sum_heads(qkv_parts[:, :, q_width + HEAD_DIM :]),
+            join(o_parts),
+            gain_grads[1, :weight_rows],
+            join(gate_parts),
+            join(up_parts),
+            join(down_parts),
+        )
+
     inv_one = lax.rsqrt(jnp.mean(x_float * x_float, axis=-1, keepdims=True) + NORM_EPS)
     normed_one = x_float * inv_one
     inv_two = lax.rsqrt(jnp.mean(resid * resid, axis=-1, keepdims=True) + NORM_EPS)
@@ -759,7 +1366,7 @@
 
     proj_grad = pl.pallas_call(
         functools.partial(attention_backward, team, block_len, q_width),
-        out_shape=jax.ShapeDtypeStruct((team, chunk, qkv_width), BF16),
+        out_shape=jax.ShapeDtypeStruct((token_count, qkv_width), BF16),
         in_specs=[smem(), vmem(), vmem(), vmem(), vmem()],
         out_specs=vmem(),
         scratch_shapes=[
@@ -769,7 +1376,7 @@
         ],
         compiler_params=pltpu.CompilerParams(vmem_limit_bytes=VMEM_BYTES),
         name="attention_backward",
-    )(t.astype(jnp.int32).reshape(1), rot, mix_grad, cos_table, sin_table).reshape(token_count, qkv_width)
+    )(t.astype(jnp.int32).reshape(1), rot, mix_grad, cos_table, sin_table)
 
     attn_in_grad = team_reduce(lambda odd: contract_cols(half_of(proj_grad, odd), qkv_team).astype(BF16))
     attn_gain_grad = scatter_small(restore(jnp.sum(attn_in_grad * normed_one, axis=0)))

time: 869 us -> 632 us (0.73)
  Pallas kernels: 320 us -> 603 us
  waiting for transfers between devices: 202 us -> 0 us
  starting transfers between devices: 140 us -> 0 us
  matrix products: 76.9 us -> 0 us
  local copies, waits for them, and re-layouts: 68.6 us -> 14.8 us
  other arithmetic: 54.8 us -> 8.8 us
    pallas_call x1, Pallas kernels: 18.7 us -> 332 us  [body(): pl.pallas_call(functools.partial(exit_kernel, cp_size), out_shape=(hbm(te...]
    ppermute x38 -> x0, waiting for transfers between devices: 188 us -> none  [swap(): return lax.ppermute(value, BOTH, [(i, i ^ mask) for i in range(devices)])]
    ppermute x38 -> x0, starting transfers between devices: 112 us -> none  [swap(): return lax.ppermute(value, BOTH, [(i, i ^ mask) for i in range(devices)])]
    dot_general x17 -> x0, matrix products: 76.9 us -> none  [the longest x9 32.2 us: contract_cols(): lax.dot_general(left, right, (((1,), (1,)), ((), ())), preferred_element_...]
    pallas_call x1, Pallas kernels: 302 us -> 270 us  [body(): pl.pallas_call(functools.partial(entry_kernel, fsdp_size, cp_size), out_s...]
    all_to_all x6 -> x0, starting transfers between devices: 27.1 us -> none  [to_team(): lax.all_to_all(turn(value), 'cp', 0, 0, axis_index_groups=team_groups, ti...]
    convert_element_type x11 -> x0, other arithmetic: 19.1 us -> none  [the longest x5 10.5 us: collect(): blocks = (blocks[0].astype(F32) + theirs.astype(F32)).astype(BF16)]
    slice x28 -> x0, local copies, waits for them, and re-layouts: 15.6 us -> none  [the longest x5 8.79 us: collect(): theirs = swap(blocks[1], cp_size)]
  transfers between devices with their start and end apart: 44 -> 0, of which waited for: 23 -> 0; matrix products, arithmetic and copies ran while one was open for 16% -> 0% of each run, Pallas kernels for 0% -> 0%
where the time goes in v3:
time: 632 us; the launch traced here: 627 us
  Pallas kernels  603 us (95%)
  local copies, waits for them, and re-layouts  14.8 us (2%)
  other arithmetic  8.8 us (1%)
    pallas_call x1, Pallas kernels, body(): pl.pallas_call(functools.partial(exit_kernel, cp_size), out_shape=(hbm(te...  332 us
    pallas_call x1, Pallas kernels, body(): pl.pallas_call(functools.partial(entry_kernel, fsdp_size, cp_size), out_s...  270 us

profile of v3, /device:TPU:0, one launch (start us, length us, event | category | flops | bytes accessed | tf_op | source)
XLA Modules:
  0.0 627.3 jit_solution(14200581670040695772)
XLA Ops:
  0.7 1.3 fusion.6.gains_in
  2.0 1.0 reshape_reshape_reshape_broadcast_in_dim_reshape.6
  3.0 1.0 reshape_reshape_reshape_broadcast_in_dim_reshape.7
  4.0 1.0 copy.57
  5.0 0.9 pad_maximum_fusion.2.qkv_cut
  5.8 0.7 copy.56
  6.6 1.9 fusion
  8.5 1.8 pad_maximum_fusion
  10.3 270.4 %entry.1 = (f32[128,2048]{1,0:T(8,128)}, f32[8,2048]{1,0:T(8,128)}, bf16[8,128,2048]{2,1,0:T(8,128)(2,1)}, bf16[4,8,64,384]{3,2,1,0:T(8,128)(2,1)}, bf16[256,204...) custom-call(bf16[2,64,2048]{2,1,0:T(8,128)(2,1)} %tokens.1, ...), custom_call_target="tpu_custom_call" | custom-call | tf_op jit(solution)/shard_map/entry/pallas_call | solution.py:1186
  280.7 332.3 %exit.1 = (bf16[2,64,2048]{2,1,0:T(8,128)(2,1)}, bf16[2,64,2048]{2,1,0:T(8,128)(2,1)}, f32[8,128]{1,0:T(8,128)}, bf16[8,64,1024]{2,1,0:T(8,128)(2,1)}, bf16[8,64...) custom-call(f32[128,2048]{1,0:T(8,128)} %get-tuple-element.32.x_ref,, ...), custom_call_target="tpu_custom_call" | custom-call | tf_op jit(solution)/shard_map/exit/pallas_call | solution.py:1238
  613.0 1.3 slice_bitcast_fusion
  614.3 1.0 convert_bitcast_fusion.3
  615.3 0.8 copy.48
  616.1 1.1 convert_bitcast_fusion.4
  617.2 0.8 copy.47
  618.1 0.1 convert_bitcast_fusion.5
  618.2 0.2 copy.40
  618.3 0.8 reshape.110
  619.1 0.2 copy.39
  619.3 0.8 reshape.108
  620.0 0.2 convert_bitcast_fusion.2
  620.3 1.5 copy.49
  621.8 0.2 copy-done.1
  621.9 0.2 convert_bitcast_fusion.1
  622.2 1.5 copy.50
  623.6 0.2 copy-done
  623.8 0.2 convert_bitcast_fusion
  624.0 0.0 copy-start.5
  624.0 0.0 copy-start.4
  624.1 1.5 copy.51
  625.5 0.8 copy.60
  626.3 0.8 copy.61
  (13 shorter events, 0.1 us)
Async XLA Ops:
  0.6 5.2 copy-start.6
  613.0 5.0 copy-start.3
  616.1 3.9 copy-start.2
  620.3 1.6 copy-start.1
  622.2 1.6 copy-start
  624.0 1.5 copy-start.5
  624.0 2.3 copy-start.4

commit v4 on v3

--- a/solution.py
+++ b/solution.py
@@ -2,6 +2,7 @@
 
 import jax
 import jax.numpy as jnp
+import numpy as np
 from jax import lax
 from jax.experimental import pallas as pl
 from jax.experimental.pallas import tpu as pltpu
@@ -257,6 +258,7 @@
         self.cuts = [links.copy(pieces(m), full.at[0, t], m) for m in range(1, team)]
         self.far = [links.copy(full.at[b], full.at[b + 2], links.cp_size) for b in range(2)]
         self.side = links.copy(full.at[0], full.at[1], team + team // 2)
+        self.outer = t // (team // 2) == 0
 
     def cut(self):
         self.own.start()
@@ -268,7 +270,12 @@
         for piece in self.cuts:
             piece.wait_recv()
         self.far[0].start()
-        self.side.start()
+        self.cross(False)
+
+    def cross(self, outer):
+        @pl.when(self.outer == outer)
+        def _():
+            self.side.start()
 
     def arrive(self):
         self.side.wait_recv()
@@ -284,7 +291,8 @@
 class Collect:
     def __init__(self, links, team, t, grad, far_in, side_in, final, out):
         self.grad, self.far_in, self.side_in, self.final = grad, far_in, side_in, final
-        self.far = links.copy(grad.at[pl.ds(2, 2)], far_in, links.cp_size)
+        self.outer = t // (team // 2) == 0
+        self.far = [links.copy(grad.at[b + 2], far_in.at[b], links.cp_size) for b in range(2)]
         self.side = links.copy(grad.at[1], side_in, team + team // 2)
         self.own = links.inside(final.at[t], out.at[t])
         self.cuts = [links.copy(final.at[flip(t, m)], out.at[t], m) for m in range(1, team)]
@@ -294,9 +302,15 @@
         for piece in self.cuts:
             piece.start()
 
+    def cross(self, outer):
+        @pl.when(self.outer == outer)
+        def _():
+            self.side.start()
+
     def finish(self):
         self.own.wait()
-        self.far.wait_send()
+        for copy in self.far:
+            copy.wait_send()
         self.side.wait_send()
         for piece in self.cuts:
             piece.wait()
@@ -308,7 +322,8 @@
     tokens,
     cotangent,
     gains_in,
-    qkv_cut,
+    q_cut,
+    kv_cut,
     o_cut,
     gate_in,
     up_in,
@@ -318,7 +333,8 @@
     x_ref,
     gains_ref,
     attn_in_ref,
-    qkv_full,
+    q_full,
+    kv_full,
     o_wide,
     rot_ref,
     mix_ref,
@@ -338,7 +354,8 @@
     chunk_ref,
     dy_chunk,
     acts,
-    wqkv,
+    q_w,
+    kv_w,
     mixed,
     o_pieces,
     taken,
@@ -371,19 +388,24 @@
         size *= 2
 
     def columns_of(weight):
-        return lambda m: weight.at[:, pl.ds(pl.multiple_of(flip(t, m) * cols, cols), cols)]
+        if len(weight.shape) == 3:
+            return lambda m: weight.at[flip(t, m)]
+        count = weight.shape[1] // team
+        return lambda m: weight.at[:, pl.ds(pl.multiple_of(flip(t, m) * count, count), count)]
 
     def spread(pieces, full):
         return Spread(links, team, t, pieces, full)
 
-    qkv_spread = spread(lambda m: qkv_cut.at[flip(t, m)], qkv_full)
-    o_spread = spread(lambda m: o_cut.at[flip(t, m)], o_full)
+    q_spread = spread(columns_of(q_cut), q_full)
+    kv_spread = spread(columns_of(kv_cut), kv_full)
+    o_spread = spread(columns_of(o_cut), o_full)
     gate_spread = spread(columns_of(gate_in), gate_full)
     up_spread = spread(columns_of(up_in), up_full)
     down_spread = spread(columns_of(down_in), down_full)
 
     stages[0].start()
-    qkv_spread.cut()
+    q_spread.cut()
+    kv_spread.cut()
     o_spread.cut()
     for step in range(1, len(stages)):
         stages[step - 1].wait_recv()
@@ -415,20 +437,28 @@
     gather_one.start()
     dy_swap = links.copy(cotangent.at[1 - side], dy_swapped, mirror)
     dy_swap.start()
-    qkv_spread.leave()
+    q_spread.leave()
+    kv_spread.leave()
+    q_spread.cross(True)
+    kv_spread.cross(True)
     o_spread.leave()
+    o_spread.cross(True)
     gather_one.pass_near()
     gather_one.pass_row()
     gate_spread.leave()
+    gate_spread.cross(True)
     gather_one.pass_on()
     up_spread.cut()
     down_spread.cut()
-    qkv_spread.arrive()
+    q_spread.arrive()
+    kv_spread.arrive()
     o_spread.arrive()
     up_spread.leave()
-    qkv_spread.finish()
-    load = links.inside(qkv_full, wqkv)
-    load.start()
+    q_spread.finish()
+    kv_spread.finish()
+    weight_loads = [links.inside(q_full, q_w), links.inside(kv_full, kv_w)]
+    for load in weight_loads:
+        load.start()
     gather_one.finish()
     attn_out = links.inside(acts, attn_in_ref)
     attn_out.start()
@@ -449,19 +479,21 @@
     for copy in o_sends:
         copy.start()
 
-    load.wait()
-    weights = wqkv[...].reshape(width, wqkv.shape[-1])
+    for load in weight_loads:
+        load.wait()
+    q_weights = q_w[...].reshape(width, q_width)
+    kv_weights = kv_w[...].reshape(width, 2 * HEAD_DIM)
 
     def project(m, carry):
-        proj = dot(acts[spot_of(m, team)], weights)
-        keys = proj[:, q_width : q_width + HEAD_DIM]
-        qk = jnp.concatenate([proj[:, :q_width] * HEAD_DIM ** (-0.5), keys], axis=-1)
+        rows_in = acts[spot_of(m, team)]
+        key_value = dot(rows_in, kv_weights)
+        qk = jnp.concatenate([dot(rows_in, q_weights) * HEAD_DIM ** (-0.5), key_value[:, :HEAD_DIM]], axis=-1)
         blocks = chunk_blocks(differ(t, m, team), team)
         for slot in range(4):
             piece = slice(slot * block_len, (slot + 1) * block_len)
             rows = pl.ds(pl.multiple_of(blocks[slot] * block_len, block_len), block_len)
             turned = turn_by(qk[piece], cos_ref[rows, :], sin_ref[rows, :])
-            rot_ref[rows, :] = jnp.concatenate([turned, proj[piece, q_width + HEAD_DIM :]], axis=-1).astype(BF16)
+            rot_ref[rows, :] = jnp.concatenate([turned, key_value[piece, HEAD_DIM:]], axis=-1).astype(BF16)
         return carry
 
     lax.fori_loop(0, team, project, 0)
@@ -517,6 +549,7 @@
 
     summed.start(mix_out, near_sum, resid_ref)
     summed.pass_near(near_sum[...])
+    up_spread.cross(True)
     gather_dy.pass_on()
     resid_ref[...] = x_ref[...] + summed.total(resid_ref[...])
     resid = resid_ref[...]
@@ -524,6 +557,7 @@
     chunk_ref[...] = (resid * inv_two * gains_ref[1:2]).astype(BF16)
     gather_two = TeamGather(links, team, chunk_ref, ffn_in_ref)
     gather_two.start()
+    down_spread.cross(True)
     gather_dy.finish()
     gate_spread.arrive()
     gather_two.pass_near()
@@ -627,7 +661,8 @@
     gate_in,
     up_in,
     down_in,
-    qkv_in,
+    q_in,
+    kv_in,
     block_out,
     input_grad,
     gain_grads,
@@ -717,7 +752,8 @@
             (up_in, up_w),
             (dy, second),
             (down_in, down_w),
-            (qkv_in, qkv_w),
+            (q_in, qkv_w.at[:, pl.ds(0, q_in.shape[1])]),
+            (kv_in, qkv_w.at[:, pl.ds(q_in.shape[1], kv_in.shape[1])]),
         )
     ]
     for load in loads:
@@ -746,7 +782,7 @@
 
     lax.fori_loop(0, steps, forward, 0)
 
-    def produce(left, right, widths, start, count, targets, adds):
+    def produce(left, right, offset, widths, start, count, targets, adds):
         def one(index, carry):
             place = start + index
             slot = index % 2
@@ -772,15 +808,15 @@
                     store.wait()
 
             turned = left[:, pl.ds(pl.multiple_of(place * unit, unit), unit)].T
-            offset = 0
+            first_col = offset
             for k, span in enumerate(widths):
-                value = dot(turned, right[:, offset : offset + span]).reshape(half, weight_rows, span)
+                value = dot(turned, right[:, first_col : first_col + span]).reshape(half, weight_rows, span)
                 for a in range(len(adds)):
                     waits[a * len(widths) + k].wait()
                     value = value + stage_in[a, k, :, :, :span].astype(F32)
                 stage_out[slot, k, :, :, :span] = value.astype(BF16)
                 stores[k].start()
-                offset += span
+                first_col += span
             return carry
 
         lax.fori_loop(0, count, one, 0)
@@ -796,32 +832,25 @@
     def in_side(ref):
         return lambda block, part: ref.at[part]
 
-    def give_far(left, right, widths, collects):
-        produce(left, right, widths, 4, 4, [in_block(k.grad) for k in collects], [])
+    def give_far(block, left, right, offset, widths, collects):
+        produce(left, right, offset, widths, 4 + 2 * block, 2, [in_block(k.grad) for k in collects], [])
         for collect in collects:
-            collect.far.start()
-
-    def give_side(left, right, widths, collects):
+            collect.far[block].start()
+
+    def give_side(left, right, offset, widths, collects):
         for collect in collects:
-            collect.far.wait_recv()
-        produce(
-            left, right, widths, 2, 2, [in_block(k.grad) for k in collects], [[in_block(k.far_in) for k in collects]]
-        )
+            collect.far[1].wait_recv()
+        sources = [in_block(k.far_in) for k in collects]
+        produce(left, right, offset, widths, 2, 2, [in_block(k.grad) for k in collects], [sources])
         for collect in collects:
-            collect.side.start()
-
-    def give_final(left, right, widths, collects):
+            collect.cross(False)
+
+    def give_final(left, right, offset, widths, collects):
         for collect in collects:
+            collect.far[0].wait_recv()
             collect.side.wait_recv()
-        produce(
-            left,
-            right,
-            widths,
-            0,
-            2,
-            [in_side(k.final) for k in collects],
-            [[in_block(k.far_in) for k in collects], [in_side(k.side_in) for k in collects]],
-        )
+        sources = [[in_block(k.far_in) for k in collects], [in_side(k.side_in) for k in collects]]
+        produce(left, right, offset, widths, 0, 2, [in_side(k.final) for k in collects], sources)
         for collect in collects:
             collect.cut()
 
@@ -831,7 +860,7 @@
     qkv_sum = Collect(links, team, t, qkv_grad, qkv_far, qkv_side, qkv_final, qkv_out)
 
     loads[3].wait()
-    give_far(second, hidden, [cols], [down_sum])
+    give_far(1, second, hidden, 0, [cols], [down_sum])
     loads[4].wait()
 
     def backward(index, carry):
@@ -868,7 +897,10 @@
         lambda place, cut: contract_cols(both[place, :cols], gate_w[cut, :]) + contract_cols(both[place, cols:], up_w[cut, :]),
     )
     ffn_sum.pass_near(near_sum[...])
-    give_far(first, both, [cols, cols], [gate_sum, up_sum])
+    give_far(1, first, both, 0, [cols, cols], [gate_sum, up_sum])
+    give_far(0, second, hidden, 0, [cols], [down_sum])
+    give_side(second, hidden, 0, [cols], [down_sum])
+    give_far(0, first, both, 0, [cols, cols], [gate_sum, up_sum])
     ffn_in_grad = ffn_sum.total(own_sum[...])
     ffn_sum.finish()
 
@@ -892,10 +924,12 @@
     chunk_ref[...] = value.astype(BF16)
     gather = TeamGather(links, team, chunk_ref, branch)
     gather.start()
-    give_side(second, hidden, [cols], [down_sum])
+    down_sum.cross(True)
+    give_side(first, both, 0, [cols], [gate_sum])
     gather.pass_near()
     gather.pass_row()
     gather.pass_on()
+    give_side(first, both, cols, [cols], [up_sum])
     gather.finish()
     load = links.inside(branch, parts)
     load.start()
@@ -933,6 +967,8 @@
         copy.start()
 
     out_sum = team_sum(taken_two, row_two, near_two, lambda place, cut: contract_cols(hidden[place, :], down_w[cut, :]))
+    gate_sum.cross(True)
+    up_sum.cross(True)
     backward_heads(token_count, q_width, rot_ref, wide, cos_ref, sin_ref, dq_ref, dkv_ref)
 
     def give_chunk(m, carry):
@@ -956,6 +992,7 @@
     out_copies = give_rows(resid_ref[...] + finish_sum(out_sum), chunk_ref, block_out)
     qkv_width = q_width + 2 * HEAD_DIM
     loads[5].wait()
+    loads[6].wait()
     attn_sum = team_sum(
         taken_one,
         row_one,
@@ -963,7 +1000,7 @@
         lambda place, cut: contract_cols(proj_grad[place, :], qkv_w[cut, :]),
     )
     attn_load = links.inside(attn_in, second)
-    give_final(second, hidden, [cols], [down_sum])
+    give_final(second, hidden, 0, [cols], [down_sum])
     attn_load.start()
     for copy in o_sends:
         copy.wait_recv()
@@ -971,7 +1008,6 @@
     other_half = pl.ds(pl.multiple_of((1 - f) * 2 * quarter, 2 * quarter), 2 * quarter)
     o_across = links.copy(gate_w.at[other_half, pl.ds(0, span)], o_far, cp_size)
     o_across.start()
-    give_side(first, both, [cols, cols], [gate_sum, up_sum])
     attn_load.wait()
     attn_in_grad = finish_sum(attn_sum)
 
@@ -989,7 +1025,9 @@
     value = resid_grad[...] + inv_one * (scaled - normed * jnp.mean(scaled * normed, axis=-1, keepdims=True))
     grad_copies = give_rows(value, grad_rows, input_grad)
 
-    give_far(second, proj_grad, [qkv_width], [qkv_sum])
+    give_far(1, second, proj_grad, 0, [qkv_width], [qkv_sum])
+    give_far(0, second, proj_grad, 0, [qkv_width], [qkv_sum])
+    give_final(first, both, 0, [cols], [gate_sum])
     o_across.wait_recv()
 
     def o_came(block):
@@ -1006,7 +1044,8 @@
         if index + 1 < len(gain_steps):
             gain_steps[index + 1].start()
     gain_grads[...] = gain_slots[0]
-    give_side(second, proj_grad, [qkv_width], [qkv_sum])
+    give_side(second, proj_grad, 0, [qkv_width], [qkv_sum])
+    qkv_sum.cross(True)
     o_cross.wait_recv()
     o_final[...] = (o_land(f * 2 + side) + o_came(side) + o_side[...].astype(F32)).astype(BF16)
 
@@ -1019,8 +1058,8 @@
     o_last.start()
     for copy in o_gives:
         copy.start()
-    give_final(first, both, [cols, cols], [gate_sum, up_sum])
-    give_final(second, proj_grad, [qkv_width], [qkv_sum])
+    give_final(first, both, cols, [cols], [up_sum])
+    give_final(second, proj_grad, 0, [qkv_width], [qkv_sum])
     for own, other in (out_copies, grad_copies):
         own.wait()
         other.wait()
@@ -1031,6 +1070,19 @@
     o_last.wait()
     for collect in (down_sum, gate_sum, up_sum, qkv_sum):
         collect.finish()
+
+
+def join_kernel(team, q_width, qkv, o_part, gate_part, up_part, down_part, q_out, o_out, gate_out, up_out, down_out, k_out, v_out):
+    member = pl.program_id(0)
+    q_out[...] = qkv[member, :, :q_width].astype(F32)
+    for part, out in ((o_part, o_out), (gate_part, gate_out), (up_part, up_out), (down_part, down_out)):
+        out[...] = part[0].astype(F32)
+
+    @pl.when(member == 0)
+    def _():
+        keys, values = slice(q_width, q_width + HEAD_DIM), slice(q_width + HEAD_DIM, q_width + 2 * HEAD_DIM)
+        k_out[...] = jnp.concatenate([qkv[k, :, keys] for k in range(team)], axis=-1).astype(F32)
+        v_out[...] = jnp.concatenate([qkv[k, :, values] for k in range(team)], axis=-1).astype(F32)
 
 
 def vmem():
@@ -1145,22 +1197,21 @@
     def join(pieces):
         return pieces.transpose(1, 0, 2).reshape(pieces.shape[1], -1).astype(F32)
 
-    def repeat_heads(weight):
-        heads = weight.reshape(weight_rows, KV_HEADS, HEAD_DIM)
-        return jnp.repeat(heads, copies, axis=1).reshape(weight_rows, -1)
-
     def sum_heads(pieces):
         grouped = pieces.astype(F32).reshape(KV_HEADS, copies, -1, HEAD_DIM).sum(axis=1)
         return grouped.transpose(1, 0, 2).reshape(grouped.shape[1], -1)
 
-    inverse = ROPE_BASE ** (-(2.0 * jnp.arange(HALF, dtype=F32)) / HEAD_DIM)
-    angle = jnp.arange(token_count, dtype=jnp.int32).astype(F32)[:, None] * inverse[None, :]
-    cosine, sine = jnp.cos(angle), jnp.sin(angle)
-    cos_table = jnp.concatenate([cosine] * 4, axis=-1)
-    sin_table = jnp.concatenate([-sine, sine] * 2, axis=-1)
-
-    qkv_cut = jnp.concatenate([cut(q_weight), cut(repeat_heads(k_weight)), cut(repeat_heads(v_weight))], axis=-1)
-    o_cut = cut(o_weight)
+    inverse = np.float32(ROPE_BASE) ** (-(2.0 * np.arange(HALF, dtype=np.float32)) / HEAD_DIM)
+    angle = np.arange(token_count).astype(np.float32)[:, None] * inverse.astype(np.float32)[None, :]
+    cosine, sine = np.cos(angle), np.sin(angle)
+    cos_table = jnp.asarray(np.concatenate([cosine] * 4, axis=-1), F32)
+    sin_table = jnp.asarray(np.concatenate([-sine, sine] * 2, axis=-1), F32)
+
+    q_cut, o_cut = (
+        weight if weight.shape[1] // team % 128 == 0 else cut(weight) for weight in (q_weight, o_weight)
+    )
+    heads_of = [weight.reshape(weight_rows, KV_HEADS, HEAD_DIM) for weight in (k_weight, v_weight)]
+    kv_cut = jnp.repeat(jnp.concatenate(heads_of, axis=-1).transpose(1, 0, 2), copies, axis=0)
     gains_in = jnp.pad(jnp.stack([attn_gain, ffn_gain]), ((0, 14), (0, 128 - weight_rows)))
 
     def hbm(*shape):
@@ -1170,7 +1221,8 @@
         jax.ShapeDtypeStruct((chunk, width), F32),
         jax.ShapeDtypeStruct((8, width), F32),
         hbm(team, chunk, width),
-        hbm(4, team, weight_rows, qkv_width),
+        hbm(4, team, weight_rows, q_width),
+        hbm(4, team, weight_rows, 2 * HEAD_DIM),
         hbm(q_width, width),
         hbm(token_count, qkv_width),
         hbm(team, chunk, q_width),
@@ -1182,23 +1234,24 @@
         hbm(4, team, weight_rows, hidden_cols),
         hbm(4, team, weight_rows, width // team),
     )
-    spaces = [vmem(), vmem(), anywhere(), anywhere(), vmem(), vmem(), vmem(), vmem()] + [anywhere()] * 6
+    spaces = [vmem(), vmem()] + [anywhere()] * 3 + [vmem()] * 4 + [anywhere()] * 6
     outs = pl.pallas_call(
         functools.partial(entry_kernel, fsdp_size, cp_size),
         out_shape=out_shape,
-        in_specs=[vmem(), vmem(), vmem()] + [anywhere()] * 5 + [vmem()] * 2,
+        in_specs=[vmem(), vmem(), vmem()] + [anywhere()] * 6 + [vmem()] * 2,
         out_specs=tuple(spaces),
         scratch_shapes=[
-            pltpu.SemaphoreType.DMA((10 * team + 48,)),
-            pltpu.SemaphoreType.DMA((10 * team + 48,)),
-            pltpu.SemaphoreType.DMA((16,)),
+            pltpu.SemaphoreType.DMA((11 * team + 48,)),
+            pltpu.SemaphoreType.DMA((11 * team + 48,)),
+            pltpu.SemaphoreType.DMA((24,)),
             pltpu.VMEM((row_count, width), BF16),
             pltpu.VMEM((row_count, width), BF16),
             pltpu.VMEM((devices, 16, 128), BF16),
             pltpu.VMEM((chunk, width), BF16),
             pltpu.VMEM((chunk, width), BF16),
             pltpu.VMEM((team, chunk, width), BF16),
-            pltpu.VMEM((4, team, weight_rows, qkv_width), BF16),
+            pltpu.VMEM((4, team, weight_rows, q_width), BF16),
+            pltpu.VMEM((4, team, weight_rows, 2 * HEAD_DIM), BF16),
             pltpu.VMEM((token_count, q_width), BF16),
             pltpu.VMEM((team, q_width // weight_rows, weight_rows, width // team), BF16),
             pltpu.VMEM((team // 2, chunk, width), BF16),
@@ -1210,14 +1263,15 @@
             collective_id=0, has_side_effects=True, vmem_limit_bytes=VMEM_BYTES
         ),
         name="entry",
-    )(tokens, cotangent, gains_in, qkv_cut, o_cut, gate_weight, up_weight, down_weight, cos_table, sin_table)
-    x_float, gains, attn_in, qkv_team, o_team, rot, mix, resid, ffn_in, dy_team, gate_team, up_team, down_team = outs[:13]
+    )(tokens, cotangent, gains_in, q_cut, kv_cut, o_cut, gate_weight, up_weight, down_weight, cos_table, sin_table)
+    x_float, gains, attn_in, q_team, kv_team, o_team, rot, mix, resid = outs[:9]
+    ffn_in, dy_team, gate_team, up_team, down_team = outs[9:14]
     gain_one, gain_two = gains[0:1], gains[1:2]
     attn_in = attn_in.reshape(token_count, width)
     ffn_in = ffn_in.reshape(token_count, width)
     dy_low = dy_team[0]
     dy_team = dy_team.reshape(token_count, width)
-    qkv_team = qkv_team.reshape(width, qkv_width)
+    q_team, kv_team = q_team.reshape(width, q_width), kv_team.reshape(width, 2 * HEAD_DIM)
     gate_team, up_team, down_team = (w.reshape(width, hidden_cols) for w in (gate_team, up_team, down_team))
     mix = mix.reshape(token_count, q_width)
 
@@ -1252,7 +1306,7 @@
                 *buffers(hidden_cols),
                 *buffers(qkv_width),
             ),
-            in_specs=[vmem()] * 8 + [anywhere()] * 7,
+            in_specs=[vmem()] * 8 + [anywhere()] * 8,
             out_specs=tuple([anywhere()] * 2 + [vmem()] + [anywhere()] * 22),
             scratch_shapes=[
                 pltpu.SemaphoreType.DMA((10 * team + 48,)),
@@ -1308,21 +1362,45 @@
             gate_team,
             up_team,
             down_team,
-            qkv_team,
+            q_team,
+            kv_team,
         )
         block_out, input_grad, gain_grads, gate_parts, up_parts, down_parts, qkv_parts, o_parts = results[:8]
+        def part_spec(cols):
+            return pl.BlockSpec((1, weight_rows, cols), lambda member: (member, 0, 0))
+
+        def row_spec(cols):
+            return pl.BlockSpec((weight_rows, cols), lambda member: (0, member))
+
+        def fixed_spec(*shape):
+            return pl.BlockSpec(shape, lambda member: (0,) * len(shape))
+
+        kv_width = team * HEAD_DIM
+        wide_cols = [q_width, span, hidden_cols, hidden_cols, hidden_cols]
+        joined = pl.pallas_call(
+            functools.partial(join_kernel, team, q_width),
+            grid=(team,),
+            out_shape=tuple(f32(weight_rows, team * cols) for cols in wide_cols)
+            + (f32(weight_rows, kv_width), f32(weight_rows, kv_width)),
+            in_specs=[fixed_spec(team, weight_rows, qkv_width)] + [part_spec(cols) for cols in wide_cols[1:]],
+            out_specs=tuple(row_spec(cols) for cols in wide_cols)
+            + (fixed_spec(weight_rows, kv_width), fixed_spec(weight_rows, kv_width)),
+            compiler_params=pltpu.CompilerParams(vmem_limit_bytes=VMEM_BYTES),
+            name="join",
+        )(qkv_parts, o_parts, gate_parts, up_parts, down_parts)
+        q_out, o_out, gate_out, up_out, down_out, k_out, v_out = joined
         return (
             block_out,
             input_grad,
             gain_grads[0, :weight_rows],
-            join(qkv_parts[:, :, :q_width]),
-            sum_heads(qkv_parts[:, :, q_width : q_width + HEAD_DIM]),
-            sum_heads(qkv_parts[:, :, q_width + HEAD_DIM :]),
-            join(o_parts),
+            q_out,
+            k_out,
+            v_out,
+            o_out,
             gain_grads[1, :weight_rows],
-            join(gate_parts),
-            join(up_parts),
-            join(down_parts),
+            gate_out,
+            up_out,
+            down_out,
         )
 
     inv_one = lax.rsqrt(jnp.mean(x_float * x_float, axis=-1, keepdims=True) + NORM_EPS)
@@ -1378,6 +1456,7 @@
         name="attention_backward",
     )(t.astype(jnp.int32).reshape(1), rot, mix_grad, cos_table, sin_table)
 
+    qkv_team = jnp.concatenate([q_team, kv_team], axis=-1)
     attn_in_grad = team_reduce(lambda odd: contract_cols(half_of(proj_grad, odd), qkv_team).astype(BF16))
     attn_gain_grad = scatter_small(restore(jnp.sum(attn_in_grad * normed_one, axis=0)))
     scaled_one = attn_in_grad * gain_one

time: 632 us -> 573 us (0.907)
  Pallas kernels: 603 us -> 556 us
  local copies, waits for them, and re-layouts: 14.8 us -> 4.88 us
  other arithmetic: 8.8 us -> 2.04 us
    pallas_call x1, Pallas kernels: 332 us -> 280 us  [body(): pl.pallas_call(functools.partial(exit_kernel, cp_size), out_shape=(hbm(te...]
    pallas_call x0 -> x1, Pallas kernels: none -> 7.7 us  [body(): pl.pallas_call(functools.partial(join_kernel, team, q_width), grid=(team,...]
where the time goes in v4:
time: 573 us; the launch traced here: 564 us
  Pallas kernels  556 us (97%)
    pallas_call x1, Pallas kernels, body(): pl.pallas_call(functools.partial(exit_kernel, cp_size), out_shape=(hbm(te...  280 us
    pallas_call x1, Pallas kernels, body(): pl.pallas_call(functools.partial(entry_kernel, fsdp_size, cp_size), out_s...  268 us

profile of v4, /device:TPU:0, one launch (start us, length us, event | category | flops | bytes accessed | tf_op | source)
XLA Modules:
  0.0 564.3 jit_solution(1567937718562629198)
XLA Ops:
  0.6 1.3 fusion.5.gains_in
  1.9 1.0 reshape.52
  2.9 1.0 reshape.53
  3.9 0.8 maximum_bitcast_fusion.kv_cut
  4.7 268.3 %entry.1 = (f32[128,2048]{1,0:T(8,128)}, f32[8,2048]{1,0:T(8,128)}, bf16[8,128,2048]{2,1,0:T(8,128)(2,1)}, bf16[4,8,64,256]{3,2,1,0:T(8,128)(2,1)}, bf16[4,8,64,...) custom-call(bf16[2,64,2048]{2,1,0:T(8,128)(2,1)} %tokens.1, ...), custom_call_target="tpu_custom_call" | custom-call | tf_op jit(solution)/shard_map/entry/pallas_call | solution.py:1238
  273.0 280.2 %exit.1 = (bf16[2,64,2048]{2,1,0:T(8,128)(2,1)}, bf16[2,64,2048]{2,1,0:T(8,128)(2,1)}, f32[8,128]{1,0:T(8,128)}, bf16[8,64,1024]{2,1,0:T(8,128)(2,1)}, bf16[8,64...) custom-call(f32[128,2048]{1,0:T(8,128)} %get-tuple-element.40.x_ref,, ...), custom_call_target="tpu_custom_call" | custom-call | tf_op jit(solution)/shard_map/exit/pallas_call | solution.py:1292
  553.2 0.0 copy-start.1
  553.2 0.0 copy-start
  553.3 1.3 slice_bitcast_fusion
  554.5 7.7 %join.1 = (f32[64,2048]{1,0:T(8,128)}, f32[64,2048]{1,0:T(8,128)}, f32[64,8192]{1,0:T(8,128)}, f32[64,8192]{1,0:T(8,128)}, f32[64,8192]{1,0:T(8,128)}, /*index=5*/f32[64,512]{1,0:T(8,128)}, f32[64,512]{1,0:T(8,128)}) custom-call(bf16[8,64,384]{2,1,0:T(8,128)(2,1)} %get-tuple-element.57.qkv, bf16[8,64,256]{2,1,0:T(8,128)(2,1)} %get-tuple-element.58.o_part, ...), custom_call_target="tpu_custom_call" | custom-call | tf_op jit(solution)/shard_map/join/pallas_call | solution.py:1380
  562.3 0.0 copy-done.1
  562.3 0.8 copy.28
  563.1 0.0 copy-done
  563.1 0.8 copy.29
  (2 shorter events, 0.0 us)
Async XLA Ops:
  553.2 9.0 %copy-start.1 = (bf16[2,64,2048]{2,1,0:T(8,128)(2,1)S(1)}, bf16[2,64,2048]{2,1,0:T(8,128)(2,1)}, u32[]{:S(2)}) copy-start(bf16[2,64,2048]{2,1,0:T(8,128)(2,1)} %get-tuple-element.82) | copy-start | bytes 1572868
  553.2 9.8 %copy-start = (bf16[2,64,2048]{2,1,0:T(8,128)(2,1)S(1)}, bf16[2,64,2048]{2,1,0:T(8,128)(2,1)}, u32[]{:S(2)}) copy-start(bf16[2,64,2048]{2,1,0:T(8,128)(2,1)} %get-tuple-element.83) | copy-start | bytes 1572868

commit v5 on v4

--- a/solution.py
+++ b/solution.py
@@ -256,8 +256,10 @@
     def __init__(self, links, team, t, pieces, full):
         self.own = links.inside(pieces(0), full.at[0, t])
         self.cuts = [links.copy(pieces(m), full.at[0, t], m) for m in range(1, team)]
-        self.far = [links.copy(full.at[b], full.at[b + 2], links.cp_size) for b in range(2)]
-        self.side = links.copy(full.at[0], full.at[1], team + team // 2)
+        parts = [pl.ds(start, team // 2) for start in (0, team // 2)]
+        self.far = [links.copy(full.at[0], full.at[2], links.cp_size)]
+        self.far += [links.copy(full.at[1, part], full.at[3, part], links.cp_size) for part in parts]
+        self.side = [links.copy(full.at[0, part], full.at[1, part], team + team // 2) for part in parts]
         self.outer = t // (team // 2) == 0
 
     def cut(self):
@@ -275,16 +277,18 @@
     def cross(self, outer):
         @pl.when(self.outer == outer)
         def _():
-            self.side.start()
+            for copy in self.side:
+                copy.start()
 
     def arrive(self):
-        self.side.wait_recv()
-        self.far[1].start()
+        for copy, far in zip(self.side, self.far[1:]):
+            copy.wait_recv()
+            far.start()
 
     def finish(self):
         for copy in self.far:
             copy.wait_recv()
-        for copy in self.cuts + self.far + [self.side]:
+        for copy in self.cuts + self.far + self.side:
             copy.wait_send()
 
 
@@ -292,8 +296,9 @@
     def __init__(self, links, team, t, grad, far_in, side_in, final, out):
         self.grad, self.far_in, self.side_in, self.final = grad, far_in, side_in, final
         self.outer = t // (team // 2) == 0
-        self.far = [links.copy(grad.at[b + 2], far_in.at[b], links.cp_size) for b in range(2)]
-        self.side = links.copy(grad.at[1], side_in, team + team // 2)
+        parts = [pl.ds(start, team // 2) for start in (0, team // 2)]
+        self.far = [[links.copy(grad.at[b + 2, part], far_in.at[b, part], links.cp_size) for part in parts] for b in range(2)]
+        self.side = [links.copy(grad.at[1, part], side_in.at[part], team + team // 2) for part in parts]
         self.own = links.inside(final.at[t], out.at[t])
         self.cuts = [links.copy(final.at[flip(t, m)], out.at[t], m) for m in range(1, team)]
 
@@ -302,16 +307,10 @@
         for piece in self.cuts:
             piece.start()
 
-    def cross(self, outer):
-        @pl.when(self.outer == outer)
-        def _():
-            self.side.start()
-
     def finish(self):
         self.own.wait()
-        for copy in self.far:
+        for copy in self.far[0] + self.far[1] + self.side:
             copy.wait_send()
-        self.side.wait_send()
         for piece in self.cuts:
             piece.wait()
 
@@ -501,7 +500,6 @@
     dy_swap.wait_recv()
     fill(dy_chunk, cotangent, dy_swapped)
     gather_dy = TeamGather(links, team, dy_chunk, dy_ref)
-    gather_dy.start()
     down_spread.leave()
 
     def attend(first, span, start, rows):
@@ -518,7 +516,6 @@
         mixed[pl.ds(start, rows), :] = jnp.concatenate(outs, axis=-1).astype(BF16)
 
     over_row_blocks(token_count, 256, attend)
-    gather_dy.pass_near()
 
     def collect_mix(m, carry):
         blocks = chunk_blocks(differ(t, m, team), team)
@@ -541,7 +538,6 @@
     attn_out.wait()
     summed = TeamSum(links, team, acts, taken, row_in, near_in)
     row_pair = 2 * row_count
-    gather_dy.pass_row()
 
     def mix_out(place, cols):
         spots = pl.ds(place.start // row_pair, 2)
@@ -550,7 +546,6 @@
     summed.start(mix_out, near_sum, resid_ref)
     summed.pass_near(near_sum[...])
     up_spread.cross(True)
-    gather_dy.pass_on()
     resid_ref[...] = x_ref[...] + summed.total(resid_ref[...])
     resid = resid_ref[...]
     inv_two = lax.rsqrt(jnp.mean(resid * resid, axis=-1, keepdims=True) + NORM_EPS)
@@ -558,15 +553,19 @@
     gather_two = TeamGather(links, team, chunk_ref, ffn_in_ref)
     gather_two.start()
     down_spread.cross(True)
-    gather_dy.finish()
     gate_spread.arrive()
     gather_two.pass_near()
     gather_two.pass_row()
     gather_two.pass_on()
+    gather_dy.start()
     up_spread.arrive()
     gate_spread.finish()
     down_spread.arrive()
     gather_two.finish()
+    gather_dy.pass_near()
+    gather_dy.pass_row()
+    gather_dy.pass_on()
+    gather_dy.finish()
     up_spread.finish()
     down_spread.finish()
     swap.wait_send()
@@ -782,49 +781,28 @@
 
     lax.fori_loop(0, steps, forward, 0)
 
-    def produce(left, right, offset, widths, start, count, targets, adds):
-        def one(index, carry):
-            place = start + index
-            slot = index % 2
-            block, part = place // 2, pl.ds((place % 2) * half, half)
-            waits = []
-            for a, sources in enumerate(adds):
-                for k, source in enumerate(sources):
-                    load = pltpu.make_async_copy(
-                        source(block, part), stage_in.at[a, k, :, :, : widths[k]], load_sem.at[a, k]
-                    )
-                    load.start()
-                    waits.append(load)
-            stores = [
-                pltpu.make_async_copy(
-                    stage_out.at[slot, k, :, :, : widths[k]], target(block, part), store_sem.at[slot, k]
-                )
-                for k, target in enumerate(targets)
-            ]
-
-            @pl.when(index >= 2)
-            def _():
-                for store in stores:
-                    store.wait()
-
-            turned = left[:, pl.ds(pl.multiple_of(place * unit, unit), unit)].T
-            first_col = offset
-            for k, span in enumerate(widths):
-                value = dot(turned, right[:, first_col : first_col + span]).reshape(half, weight_rows, span)
-                for a in range(len(adds)):
-                    waits[a * len(widths) + k].wait()
-                    value = value + stage_in[a, k, :, :, :span].astype(F32)
-                stage_out[slot, k, :, :, :span] = value.astype(BF16)
-                stores[k].start()
-                first_col += span
-            return carry
-
-        lax.fori_loop(0, count, one, 0)
-        for index in range(max(0, count - 2), count):
-            for k, target in enumerate(targets):
-                pltpu.make_async_copy(
-                    stage_out.at[index % 2, k, :, :, : widths[k]], target(0, pl.ds(0, half)), store_sem.at[index % 2, k]
-                ).wait()
+    def produce(left, right, offset, widths, place, targets, adds):
+        block, part = place // 2, pl.ds((place % 2) * half, half)
+        waits = []
+        for a, sources in enumerate(adds):
+            for k, source in enumerate(sources):
+                load = pltpu.make_async_copy(source(block, part), stage_in.at[a, k, :, :, : widths[k]], load_sem.at[a, k])
+                load.start()
+                waits.append(load)
+        turned = left[:, place * unit : (place + 1) * unit].T
+        stores = []
+        for k, span in enumerate(widths):
+            value = dot(turned, right[:, offset : offset + span]).reshape(half, weight_rows, span)
+            for a in range(len(adds)):
+                waits[a * len(widths) + k].wait()
+                value = value + stage_in[a, k, :, :, :span].astype(F32)
+            stage_out[k, :, :, :span] = value.astype(BF16)
+            store = pltpu.make_async_copy(stage_out.at[k, :, :, :span], targets[k](block, part), store_sem.at[k])
+            store.start()
+            stores.append(store)
+            offset += span
+        for store in stores:
+            store.wait()
 
     def in_block(ref):
         return lambda block, part: ref.at[block, part]
@@ -833,24 +811,27 @@
         return lambda block, part: ref.at[part]
 
     def give_far(block, left, right, offset, widths, collects):
-        produce(left, right, offset, widths, 4 + 2 * block, 2, [in_block(k.grad) for k in collects], [])
-        for collect in collects:
-            collect.far[block].start()
+        for h in range(2):
+            produce(left, right, offset, widths, 4 + 2 * block + h, [in_block(k.grad) for k in collects], [])
+            for collect in collects:
+                collect.far[block][h].start()
 
     def give_side(left, right, offset, widths, collects):
-        for collect in collects:
-            collect.far[1].wait_recv()
         sources = [in_block(k.far_in) for k in collects]
-        produce(left, right, offset, widths, 2, 2, [in_block(k.grad) for k in collects], [sources])
-        for collect in collects:
-            collect.cross(False)
+        for h in range(2):
+            for collect in collects:
+                collect.far[1][h].wait_recv()
+            produce(left, right, offset, widths, 2 + h, [in_block(k.grad) for k in collects], [sources])
+            for collect in collects:
+                collect.side[h].start()
 
     def give_final(left, right, offset, widths, collects):
-        for collect in collects:
-            collect.far[0].wait_recv()
-            collect.side.wait_recv()
         sources = [[in_block(k.far_in) for k in collects], [in_side(k.side_in) for k in collects]]
-        produce(left, right, offset, widths, 0, 2, [in_side(k.final) for k in collects], sources)
+        for h in range(2):
+            for collect in collects:
+                collect.far[0][h].wait_recv()
+                collect.side[h].wait_recv()
+            produce(left, right, offset, widths, h, [in_side(k.final) for k in collects], sources)
         for collect in collects:
             collect.cut()
 
@@ -885,7 +866,6 @@
         return summed
 
     def finish_sum(summed):
-        summed.pass_near(near_sum[...])
         value = summed.total(own_sum[...])
         summed.finish()
         return value
@@ -924,19 +904,28 @@
     chunk_ref[...] = value.astype(BF16)
     gather = TeamGather(links, team, chunk_ref, branch)
     gather.start()
-    down_sum.cross(True)
     give_side(first, both, 0, [cols], [gate_sum])
     gather.pass_near()
     gather.pass_row()
+    out_sum = team_sum(taken_two, row_two, near_two, lambda place, cut: contract_cols(hidden[place, :], down_w[cut, :]))
     gather.pass_on()
     give_side(first, both, cols, [cols], [up_sum])
     gather.finish()
-    load = links.inside(branch, parts)
-    load.start()
-    load.wait()
+
+    branch_loads = []
+    for h in range(2):
+        for spot in range(team):
+            target = gate_w.at[pl.ds(h * token_count + spot * rows, rows)]
+            branch_loads.append(links.inside(branch.at[spot, :, pl.ds(h * cols, cols)], target))
+    for load in branch_loads:
+        load.start()
+    for load in branch_loads:
+        load.wait()
 
     for low in range(0, team, 2):
-        value = contract_cols(parts[low : low + 2].reshape(2 * rows, width), o_wide[...]).astype(BF16)
+        left, right = (pl.ds(h * token_count + low * rows, 2 * rows) for h in range(2))
+        value = contract_cols(gate_w[left, :], o_wide[:, :cols]) + contract_cols(gate_w[right, :], o_wide[:, cols:])
+        value = value.astype(BF16)
         for spot in range(2):
             m = 2 * (low + spot) if low + spot < half else 2 * (low + spot - half) + 1
             scatter_chunk(t, m, team, block_len, wide, value[spot * rows : (spot + 1) * rows])
@@ -947,18 +936,20 @@
     span = width // team
     turned = mix_ref[...].reshape(token_count, q_width).T
     for index in range(8):
-        value = dot(turned, parts[:, :, index * unit : (index + 1) * unit].reshape(token_count, unit)).astype(BF16)
+        above = index * unit // cols * token_count
+        start = index * unit % cols
+        value = dot(turned, gate_w[above : above + token_count, start : start + unit]).astype(BF16)
         for piece in range(team // 8):
             target = natural_unit(mine, index) * (team // 8) + piece
-            gate_w[head_rows(target), span : 2 * span] = value[:, piece * span : (piece + 1) * span]
+            up_w[head_rows(target), span : 2 * span] = value[:, piece * span : (piece + 1) * span]
     quarter = width // 4
-    o_place = gate_w.at[head_rows(t), pl.ds(0, span)]
+    o_place = up_w.at[head_rows(t), pl.ds(0, span)]
 
     def o_part(member):
-        return gate_w.at[head_rows(member), pl.ds(span, span)]
+        return up_w.at[head_rows(member), pl.ds(span, span)]
 
     def o_land(block):
-        return gate_w[pl.ds(pl.multiple_of(block * quarter, quarter), quarter), :span].astype(F32)
+        return up_w[pl.ds(pl.multiple_of(block * quarter, quarter), quarter), :span].astype(F32)
 
     o_own = links.inside(o_part(t), o_place)
     o_sends = [links.copy(o_part(flip(t, m)), o_place, m) for m in range(1, team)]
@@ -966,9 +957,7 @@
     for copy in o_sends:
         copy.start()
 
-    out_sum = team_sum(taken_two, row_two, near_two, lambda place, cut: contract_cols(hidden[place, :], down_w[cut, :]))
-    gate_sum.cross(True)
-    up_sum.cross(True)
+    out_sum.pass_near(near_sum[...])
     backward_heads(token_count, q_width, rot_ref, wide, cos_ref, sin_ref, dq_ref, dkv_ref)
 
     def give_chunk(m, carry):
@@ -976,6 +965,16 @@
         return carry
 
     lax.fori_loop(0, team, give_chunk, 0)
+    for copy in o_sends:
+        copy.wait_recv()
+    o_own.wait()
+    other_half = pl.ds(pl.multiple_of((1 - f) * 2 * quarter, 2 * quarter), 2 * quarter)
+    o_across = links.copy(up_w.at[other_half, pl.ds(0, span)], o_far, cp_size)
+    o_across.start()
+    o_cross = links.copy(o_two, o_side, mirror)
+
+    def o_came(block):
+        return o_far[pl.ds(pl.multiple_of(block * quarter, quarter), quarter), :].astype(F32)
 
     def give_rows(value, target, out):
         for index in range(8):
@@ -999,16 +998,16 @@
         near_one,
         lambda place, cut: contract_cols(proj_grad[place, :], qkv_w[cut, :]),
     )
+    attn_sum.pass_near(near_sum[...])
     attn_load = links.inside(attn_in, second)
     give_final(second, hidden, 0, [cols], [down_sum])
     attn_load.start()
-    for copy in o_sends:
-        copy.wait_recv()
-    o_own.wait()
-    other_half = pl.ds(pl.multiple_of((1 - f) * 2 * quarter, 2 * quarter), 2 * quarter)
-    o_across = links.copy(gate_w.at[other_half, pl.ds(0, span)], o_far, cp_size)
-    o_across.start()
     attn_load.wait()
+    give_far(1, second, proj_grad, 0, [qkv_width], [qkv_sum])
+    give_far(0, second, proj_grad, 0, [qkv_width], [qkv_sum])
+    o_across.wait_recv()
+    o_two[...] = (o_land(f * 2 + 1 - side) + o_came(1 - side)).astype(BF16)
+    o_cross.start()
     attn_in_grad = finish_sum(attn_sum)
 
     x = x_ref[...]
@@ -1025,17 +1024,8 @@
     value = resid_grad[...] + inv_one * (scaled - normed * jnp.mean(scaled * normed, axis=-1, keepdims=True))
     grad_copies = give_rows(value, grad_rows, input_grad)
 
-    give_far(1, second, proj_grad, 0, [qkv_width], [qkv_sum])
-    give_far(0, second, proj_grad, 0, [qkv_width], [qkv_sum])
+    give_side(second, proj_grad, 0, [qkv_width], [qkv_sum])
     give_final(first, both, 0, [cols], [gate_sum])
-    o_across.wait_recv()
-
-    def o_came(block):
-        return o_far[pl.ds(pl.multiple_of(block * quarter, quarter), quarter), :].astype(F32)
-
-    o_two[...] = (o_land(f * 2 + 1 - side) + o_came(1 - side)).astype(BF16)
-    o_cross = links.copy(o_two, o_side, mirror)
-    o_cross.start()
     size = 2 * team
     for index, step in enumerate(gain_steps):
         step.wait_recv()
@@ -1044,8 +1034,6 @@
         if index + 1 < len(gain_steps):
             gain_steps[index + 1].start()
     gain_grads[...] = gain_slots[0]
-    give_side(second, proj_grad, 0, [qkv_width], [qkv_sum])
-    qkv_sum.cross(True)
     o_cross.wait_recv()
     o_final[...] = (o_land(f * 2 + side) + o_came(side) + o_side[...].astype(F32)).astype(BF16)
 
@@ -1072,17 +1060,40 @@
         collect.finish()
 
 
-def join_kernel(team, q_width, qkv, o_part, gate_part, up_part, down_part, q_out, o_out, gate_out, up_out, down_out, k_out, v_out):
-    member = pl.program_id(0)
-    q_out[...] = qkv[member, :, :q_width].astype(F32)
-    for part, out in ((o_part, o_out), (gate_part, gate_out), (up_part, up_out), (down_part, down_out)):
-        out[...] = part[0].astype(F32)
-
-    @pl.when(member == 0)
+def join_kernel(
+    team,
+    q_width,
+    qkv,
+    block_in,
+    grad_in,
+    o_part,
+    gate_part,
+    up_part,
+    down_part,
+    q_out,
+    o_out,
+    gate_out,
+    up_out,
+    down_out,
+    k_out,
+    v_out,
+    block_out,
+    grad_out,
+):
+    step = pl.program_id(0)
+    for k in range(2):
+        q_out[:, k * q_width : (k + 1) * q_width] = qkv[2 * step + k, :, :q_width].astype(F32)
+        for part, out in ((o_part, o_out), (gate_part, gate_out), (up_part, up_out), (down_part, down_out)):
+            cols = part.shape[2]
+            out[:, k * cols : (k + 1) * cols] = part[k].astype(F32)
+
+    @pl.when(step == 0)
     def _():
         keys, values = slice(q_width, q_width + HEAD_DIM), slice(q_width + HEAD_DIM, q_width + 2 * HEAD_DIM)
         k_out[...] = jnp.concatenate([qkv[k, :, keys] for k in range(team)], axis=-1).astype(F32)
         v_out[...] = jnp.concatenate([qkv[k, :, values] for k in range(team)], axis=-1).astype(F32)
+        block_out[...] = block_in[...]
+        grad_out[...] = grad_in[...]
 
 
 def vmem():
@@ -1241,8 +1252,8 @@
         in_specs=[vmem(), vmem(), vmem()] + [anywhere()] * 6 + [vmem()] * 2,
         out_specs=tuple(spaces),
         scratch_shapes=[
-            pltpu.SemaphoreType.DMA((11 * team + 48,)),
-            pltpu.SemaphoreType.DMA((11 * team + 48,)),
+            pltpu.SemaphoreType.DMA((11 * team + 64,)),
+            pltpu.SemaphoreType.DMA((11 * team + 64,)),
             pltpu.SemaphoreType.DMA((24,)),
             pltpu.VMEM((row_count, width), BF16),
             pltpu.VMEM((row_count, width), BF16),
@@ -1311,8 +1322,8 @@
             scratch_shapes=[
                 pltpu.SemaphoreType.DMA((10 * team + 48,)),
                 pltpu.SemaphoreType.DMA((10 * team + 48,)),
-                pltpu.SemaphoreType.DMA((32,)),
-                pltpu.SemaphoreType.DMA((2, 2)),
+                pltpu.SemaphoreType.DMA((2 * team + 32,)),
+                pltpu.SemaphoreType.DMA((2,)),
                 pltpu.SemaphoreType.DMA((2, 2)),
                 scratch(token_count, width),
                 scratch(token_count, width),
@@ -1323,7 +1334,7 @@
                 scratch(team, chunk, width),
                 scratch(token_count, hidden_cols),
                 scratch(token_count, 2 * hidden_cols),
-                scratch(2, 2, half, weight_rows, hidden_cols),
+                scratch(2, half, weight_rows, hidden_cols),
                 scratch(2, 2, half, weight_rows, hidden_cols),
                 *sums,
                 *sums,
@@ -1367,28 +1378,33 @@
         )
         block_out, input_grad, gain_grads, gate_parts, up_parts, down_parts, qkv_parts, o_parts = results[:8]
         def part_spec(cols):
-            return pl.BlockSpec((1, weight_rows, cols), lambda member: (member, 0, 0))
+            return pl.BlockSpec((2, weight_rows, cols), lambda step: (step, 0, 0))
 
         def row_spec(cols):
-            return pl.BlockSpec((weight_rows, cols), lambda member: (0, member))
+            return pl.BlockSpec((weight_rows, 2 * cols), lambda step: (0, step))
 
         def fixed_spec(*shape):
-            return pl.BlockSpec(shape, lambda member: (0,) * len(shape))
+            return pl.BlockSpec(shape, lambda step: (0,) * len(shape))
 
         kv_width = team * HEAD_DIM
         wide_cols = [q_width, span, hidden_cols, hidden_cols, hidden_cols]
+        row_specs = [fixed_spec(teams, row_count, width)] * 2
         joined = pl.pallas_call(
             functools.partial(join_kernel, team, q_width),
-            grid=(team,),
+            grid=(team // 2,),
             out_shape=tuple(f32(weight_rows, team * cols) for cols in wide_cols)
-            + (f32(weight_rows, kv_width), f32(weight_rows, kv_width)),
-            in_specs=[fixed_spec(team, weight_rows, qkv_width)] + [part_spec(cols) for cols in wide_cols[1:]],
+            + (f32(weight_rows, kv_width), f32(weight_rows, kv_width))
+            + (hbm(teams, row_count, width), hbm(teams, row_count, width)),
+            in_specs=[fixed_spec(team, weight_rows, qkv_width)]
+            + row_specs
+            + [part_spec(cols) for cols in wide_cols[1:]],
             out_specs=tuple(row_spec(cols) for cols in wide_cols)
-            + (fixed_spec(weight_rows, kv_width), fixed_spec(weight_rows, kv_width)),
+            + (fixed_spec(weight_rows, kv_width), fixed_spec(weight_rows, kv_width))
+            + tuple(row_specs),
             compiler_params=pltpu.CompilerParams(vmem_limit_bytes=VMEM_BYTES),
             name="join",
-        )(qkv_parts, o_parts, gate_parts, up_parts, down_parts)
-        q_out, o_out, gate_out, up_out, down_out, k_out, v_out = joined
+        )(qkv_parts, block_out, input_grad, o_parts, gate_parts, up_parts, down_parts)
+        q_out, o_out, gate_out, up_out, down_out, k_out, v_out, block_out, input_grad = joined
         return (
             block_out,
             input_grad,

time: 573 us -> 555 us (0.969)
  Pallas kernels: 556 us -> 539 us
    pallas_call x1, Pallas kernels: 268 us -> 252 us  [body(): pl.pallas_call(functools.partial(entry_kernel, fsdp_size, cp_size), out_s...]
where the time goes in v5:
time: 555 us; the launch traced here: 545 us
  Pallas kernels  539 us (97%)
    pallas_call x1, Pallas kernels, body(): pl.pallas_call(functools.partial(exit_kernel, cp_size), out_shape=(hbm(te...  280 us
    pallas_call x1, Pallas kernels, body(): pl.pallas_call(functools.partial(entry_kernel, fsdp_size, cp_size), out_s...  252 us

profile of v5, /device:TPU:0, one launch (start us, length us, event | category | flops | bytes accessed | tf_op | source)
XLA Modules:
  0.0 545.4 jit_solution(2898537963310596802)
XLA Ops:
  0.6 1.3 fusion.5.gains_in
  1.9 1.0 reshape.52
  2.9 1.0 reshape.53
  3.9 0.8 maximum_bitcast_fusion.kv_cut
  4.7 252.3 %entry.1 = (f32[128,2048]{1,0:T(8,128)}, f32[8,2048]{1,0:T(8,128)}, bf16[8,128,2048]{2,1,0:T(8,128)(2,1)}, bf16[4,8,64,256]{3,2,1,0:T(8,128)(2,1)}, bf16[4,8,64,...) custom-call(bf16[2,64,2048]{2,1,0:T(8,128)(2,1)} %tokens.1, ...), custom_call_target="tpu_custom_call" | custom-call | tf_op jit(solution)/shard_map/entry/pallas_call | solution.py:1249
  257.1 280.1 %exit.1 = (bf16[2,64,2048]{2,1,0:T(8,128)(2,1)}, bf16[2,64,2048]{2,1,0:T(8,128)(2,1)}, f32[8,128]{1,0:T(8,128)}, bf16[8,64,1024]{2,1,0:T(8,128)(2,1)}, bf16[8,64...) custom-call(f32[128,2048]{1,0:T(8,128)} %get-tuple-element.42.x_ref,, ...), custom_call_target="tpu_custom_call" | custom-call | tf_op jit(solution)/shard_map/exit/pallas_call | solution.py:1303
  537.2 1.3 slice_bitcast_fusion
  538.4 6.5 %join.1 = (f32[64,2048]{1,0:T(8,128)}, f32[64,2048]{1,0:T(8,128)}, f32[64,8192]{1,0:T(8,128)}, f32[64,8192]{1,0:T(8,128)}, f32[64,8192]{1,0:T(8,128)}, /*index=5...) custom-call(bf16[8,64,384]{2,1,0:T(8,128)(2,1)} %get-tuple-element.56.qkv, ...), custom_call_target="tpu_custom_call" | custom-call | tf_op jit(solution)/shard_map/join/pallas_call | solution.py:1392
  (2 shorter events, 0.0 us)
